TPU v7x, 32 devices: a whole 2x2x4 slice. The times are simulated.
32 devices in a mesh: rep: 2 (over x), grp: 4 (over z), tp: 4 (over y, core).
Axes of the slice: x: 2, y: 2, z: 4, core: 2. Of those that a mesh axis runs over, the one named last changes fastest.
Arguments:
- x_in: bfloat16 [4, 8, 128, 1280], P(None, ('rep', 'grp'), None, 'tp'), parts along dimension 1, may hold values from -6 to 6
- taps: bfloat16 [4, 8, 128, 6400], P(None, ('rep', 'grp'), None, 'tp'), parts along dimension 1, may hold values from -6 to 6
- ln_gain: float32 [1280], replicated, may hold values from 0.1 to 1.9
- ln_bias: float32 [1280], replicated, may hold values from -3 to 3
- w_up: bfloat16 [1280, 5120], P(None, 'tp'), may hold values from -0.15625 to 0.15625
- b_up: float32 [5120], P('tp'), may hold values from -3 to 3
- w_down: bfloat16 [5120, 1280], P('tp'), may hold values from -0.078125 to 0.078125
- b_down: float32 [1280], P('tp'), may hold values from -3 to 3
- kv_w_out: bfloat16 [1280, 2048], P('tp'), may hold values from -0.0625 to 0.0625
- kv_w_taps: bfloat16 [6400, 2048], P('tp'), may hold values from -0.09375 to 0.09375
- k_gain: float32 [128], replicated, may hold values from 1 to 2.5
- q_gain: float32 [128], replicated, may hold values from 1 to 2.5
- queries: bfloat16 [4096, 8192], P(('rep', 'grp'), 'tp'), parts along dimension 0, may hold values from -6 to 6
- tiles_per_request: int32 [16], P('rep'), parts along dimension 0, may hold values from 1 to 4, as said below
- owner: int32 [16], P('rep'), parts along dimension 0, may hold values from 0 to 3, as said below
- text_per_request: int32 [16], P('rep'), parts along dimension 0, may hold values from 64 to 256, as said below
Outputs:
- attended: bfloat16 [4096, 8192], P(('rep', 'grp'), 'tp'), parts along dimension 0
There are 2 independent parts, one for each index of `rep`. A program takes and returns all parts, laid end to end along the dimension named above; an argument that names none is the same for every part. Nothing has to cross between parts.
Inputs may be any that keep to these rules, and one draw needn't show every extreme that they name: `owner`: each group owns exactly 2 requests. `tiles_per_request`: the tiles of all requests sum to 16; the tiles of one group's requests sum to at most 8, and some group has exactly 8. `text_per_request`: the text tokens of one group's requests sum to at most 512, and some group has exactly 512.
All inputs are finite; a program needn't handle non-finite values.
Results may differ from a plain program's by a relative error of at most 0.04.
Values may be sent and summed in bfloat16 or wider, within the bound.
No kernel may reach another device: no remote copies, remote signals or barrier semaphores. Data moves between devices by JAX's collectives and lax.ppermute only.
A program may use at most 128 MiB of HBM per device.

v0:
```python
import functools
import math

import jax
import jax.numpy as jnp
from jax import lax
from jax.experimental import pallas as pl
from jax.experimental.pallas import tpu as pltpu
from jax.sharding import PartitionSpec as P

KVH = 8
HD = 128
MAXT = 4
REQ_G = 2
LANES = 128
ROW_BLOCK = 128
HIDDEN_BLOCK = 256
HEAD_GROUP = 8
HALVES = 1
TAPS_EARLY = 3
VALUE_SHIFT = 2.0**-24
epsilon = 1e-05

F32 = jnp.float32
BF16 = jnp.bfloat16
VMEM = pl.BlockSpec(memory_space=pltpu.VMEM)
HBM = pl.BlockSpec(memory_space=pltpu.HBM)
SMEM = pl.BlockSpec(memory_space=pltpu.SMEM)
MIB = 1024 * 1024
LIGHT = pl.CostEstimate(flops=1024, bytes_accessed=1024, transcendentals=0)


def bits_of(count):
    bits = count.bit_length() - 1
    assert 1 << bits == count
    return bits


def xor_order(blocks, index):
    blocks = list(blocks)
    for b in range(bits_of(len(blocks))):
        swap = ((index >> b) & 1) == 1
        for k in range(len(blocks)):
            if not (k >> b) & 1:
                low, high = blocks[k], blocks[k | (1 << b)]
                blocks[k] = lax.select(swap, high, low)
                blocks[k | (1 << b)] = lax.select(swap, low, high)
    return blocks


def xor_pairs(count, mask):
    return [(i, i ^ mask) for i in range(count)]


def lane_rows(vector):
    return jnp.pad(vector, (0, -vector.shape[0] % LANES)).reshape(-1, LANES)


def one_row(ref, width):
    rows = [ref[n : n + 1, :] for n in range(ref.shape[0])]
    return (rows[0] if len(rows) == 1 else jnp.concatenate(rows, axis=1))[:, :width]


def column_step(width):
    return HIDDEN_BLOCK if width % HIDDEN_BLOCK == 0 else width


def tail_plan(rows, width):
    whole = width // LANES * LANES
    tail = width - whole
    packed = tail > 0 and whole > 0 and whole % tail == 0 and rows * tail % whole == 0
    extra = rows * tail // whole if packed else 0
    packed = packed and extra % 16 == 0 and ROW_BLOCK % extra == 0
    return whole, tail, extra if packed else 0


def sent_shape(rows, width):
    whole, _, extra = tail_plan(rows, width)
    return (rows + extra, whole) if extra else (rows, width)


def layout_kernel(group_count, tiles_local, where_ref, meta_ref):
    group = where_ref[0]
    requests = (where_ref.shape[0] - 2) // 3
    tiles_of, owner_of, text_of = ([where_ref[2 + n * requests + r] for r in range(requests)] for n in range(3))
    zero = jnp.int32(0)
    firsts, counts, offsets, texts_first, texts_both = [], [], [], [], []
    offset = zero
    for p in range(group_count):
        first, count, text_first, text_both, seen = zero, zero, zero, zero, zero
        for r in range(requests):
            mine = owner_of[r] == p
            tiles = jnp.where(mine, tiles_of[r], 0)
            text = jnp.where(mine, text_of[r], 0)
            first = first + jnp.where(seen == 0, tiles, 0)
            text_first = text_first + jnp.where(seen == 0, text, 0)
            count = count + tiles
            text_both = text_both + text
            seen = seen + jnp.where(mine, 1, 0)
        firsts.append(first)
        counts.append(count)
        offsets.append(offset)
        texts_first.append(text_first)
        texts_both.append(text_both)
        offset = offset + count

    def pick(values, index):
        out = values[0]
        for p in range(1, group_count):
            out = jnp.where(index == p, values[p], out)
        return out

    slots = slot_count_of(group_count)
    star, most = zero, counts[0]
    for p in range(1, group_count):
        larger = counts[p] > most
        star = jnp.where(larger, p, star)
        most = jnp.where(larger, counts[p], most)

    def local_tile(offset, slot):
        lane = lax.rem(group - offset + group_count * REQ_G * MAXT * group_count, group_count)
        tile = lax.div(offset + slot * group_count + lane, group_count)
        return jnp.minimum(tile, tiles_local - 1)

    my_first, my_count = pick(firsts, group), pick(counts, group)
    my_offset = pick(offsets, group)
    place = meta_places(group_count)
    meta_ref[place["first"]] = my_first
    meta_ref[place["second"]] = my_count - my_first
    meta_ref[place["text_first"]] = pick(texts_first, group)
    meta_ref[place["text_both"]] = pick(texts_both, group)
    meta_ref[place["star"]] = local_tile(pick(offsets, star), 1)
    for slot in range(slots):
        for d in range(group_count):
            other = group ^ d
            meta_ref[place["send"] + slot * group_count + d] = local_tile(pick(offsets, other), slot)
            lane = lax.rem(other - my_offset + group_count * REQ_G * MAXT * group_count, group_count)
            position = slot * group_count + lane
            goes = jnp.where(
                position < my_first,
                position,
                jnp.where(position < my_count, MAXT + position - my_first, -1),
            )
            meta_ref[place["goes"] + slot * group_count + d] = goes


def slot_count_of(group_count):
    return (REQ_G * MAXT + group_count - 1) // group_count


def meta_places(group_count):
    table = slot_count_of(group_count) * group_count
    return {
        "first": 0,
        "second": 1,
        "text_first": 2,
        "text_both": 3,
        "star": 4,
        "send": 8,
        "goes": 8 + table,
        "size": 8 + 2 * table,
    }


def mlp_kernel(piece_count, bases, tiles, where_ref, *refs):
    pieces = refs[:piece_count]
    gain_ref, bias_ref, up_bias_ref, up_ref, down_ref = refs[piece_count : piece_count + 5]
    outs = refs[piece_count + 5 : 2 * piece_count + 5]
    cat_ref, normed_ref, hidden_ref, total_ref = refs[2 * piece_count + 5 :]
    index = where_ref[1]
    _, width, tile_rows = pieces[0].shape
    rows = tiles * tile_rows
    channels, hidden_width = up_ref.shape
    up_step = column_step(hidden_width)
    down_step = column_step(channels)

    gain, bias = one_row(gain_ref, channels), one_row(bias_ref, channels)
    up_bias = one_row(up_bias_ref, hidden_width)
    for tile in range(tiles):
        for k, piece in enumerate(pieces):
            start = pl.multiple_of((index ^ k) * width, math.gcd(width, LANES))
            cat_ref[pl.ds(start, width), :] = piece[bases[k] + tile]
        values = cat_ref[...].T.astype(F32)
        average = jnp.sum(values, axis=1, keepdims=True) * (1.0 / channels)
        centered = values - average
        variance = jnp.sum(centered * centered, axis=1, keepdims=True) * (1.0 / channels)
        normed = centered * lax.rsqrt(variance + epsilon)
        normed = normed * gain + bias
        normed_ref[tile * tile_rows : (tile + 1) * tile_rows, :] = normed.astype(BF16)
    for n in range(hidden_width // up_step):
        take = slice(n * up_step, (n + 1) * up_step)
        value = jnp.dot(normed_ref[...], up_ref[:, take], preferred_element_type=F32)
        value = value + up_bias[:, take]
        value = 0.5 * value * (1.0 + lax.erf(value * (1.0 / math.sqrt(2.0))))
        hidden_ref[:, take] = value.astype(BF16)
    for n in range(channels // down_step):
        take = slice(n * down_step, (n + 1) * down_step)
        total_ref[:, take] = jnp.dot(
            hidden_ref[...], down_ref[:, take], preferred_element_type=F32
        )
    whole, tail, extra = tail_plan(rows, width)
    step = extra or ROW_BLOCK
    for part in range(rows // step):
        take = pl.ds(part * step, step)
        blocks = [total_ref[take, j * width : (j + 1) * width] for j in range(piece_count)]
        for out, block in zip(outs, xor_order(blocks, index)):
            block = block.astype(BF16)
            if extra:
                out[take, :] = block[:, :whole]
                out[rows : rows + extra, part * tail : (part + 1) * tail] = block[:, whole:]
            else:
                out[take, :] = block


def encoder_mlp(where, pieces, bases, tiles, ln_gain, ln_bias, w_up, b_up, w_down):
    _, width, tile_rows = pieces[0].shape
    rows = tiles * tile_rows
    count = len(pieces)
    channels, hidden_width = w_up.shape
    shape = sent_shape(rows, width)
    return pl.pallas_call(
        functools.partial(mlp_kernel, count, bases, tiles),
        out_shape=[jax.ShapeDtypeStruct(shape, BF16)] * count,
        in_specs=[SMEM] + [VMEM] * (count + 5),
        out_specs=[VMEM] * count,
        scratch_shapes=[
            pltpu.VMEM((channels, tile_rows), BF16),
            pltpu.VMEM((rows, channels), BF16),
            pltpu.VMEM((rows, hidden_width), BF16),
            pltpu.VMEM((rows, channels), F32),
        ],
        compiler_params=pltpu.CompilerParams(vmem_limit_bytes=44 * MIB),
        cost_estimate=LIGHT,
        name="encoder_mlp",
    )(
        where,
        *pieces,
        lane_rows(ln_gain),
        lane_rows(ln_bias),
        lane_rows(b_up),
        w_up,
        w_down,
    )


def prepare_kernel(
    group_count,
    tiles_local,
    where_ref,
    gain_ref,
    query_ref,
    normed_ref,
    meta_ref,
):
    @pl.when(pl.program_id(0) == 0)
    def _():
        layout_kernel(group_count, tiles_local, where_ref, meta_ref)

    gain = gain_ref[...] * (math.log2(math.e) / math.sqrt(HD))
    for col in range(0, query_ref.shape[1], HD):
        values = query_ref[:, col : col + HD].astype(F32)
        square = jnp.sum(values * values, axis=1, keepdims=True) * (1.0 / HD)
        normed_ref[:, col : col + HD] = (values * lax.rsqrt(square + epsilon) * gain).astype(BF16)


def prepare(where, q_gain, queries, group_count, tiles_local):
    text_rows, width = queries.shape
    step = ROW_BLOCK
    return pl.pallas_call(
        functools.partial(prepare_kernel, group_count, tiles_local),
        out_shape=[
            jax.ShapeDtypeStruct((text_rows, width), BF16),
            jax.ShapeDtypeStruct((meta_places(group_count)["size"],), jnp.int32),
        ],
        grid=(text_rows // step,),
        in_specs=[
            SMEM,
            pl.BlockSpec((1, HD), lambda n: (0, 0)),
            pl.BlockSpec((step, width), lambda n: (n, 0)),
        ],
        out_specs=[pl.BlockSpec((step, width), lambda n: (n, 0)), SMEM],
        compiler_params=pltpu.CompilerParams(vmem_limit_bytes=16 * MIB),
        cost_estimate=LIGHT,
        name="prepare",
    )(where, lane_rows(q_gain), queries)


def tap_kernel(blocks, head_count, dup, staged, where_ref, tap_hbm, weight_hbm, *refs):
    sources, out_ref = refs[:staged], refs[staged]
    targets = refs[staged + 1 : 2 * staged + 1]
    if staged:
        tap_ref, weight_ref, tap_sem, weight_sem, staged_sem = refs[2 * staged + 1 :]
    else:
        tap_ref, (weight_ref, weight_sem) = tap_hbm, refs[1:]
    tiles, _, tile_rows = tap_ref.shape
    block = weight_ref.shape[2]
    mine = lax.div(where_ref[1], jnp.int32(dup))
    taps = [
        pltpu.make_async_copy(tap_hbm.at[n], tap_ref.at[n], tap_sem.at[n])
        for n in range(tiles if staged else 0)
    ]
    weights = []
    for n, (head, k) in enumerate(blocks):
        column = pl.multiple_of(((mine ^ k) * head_count + head) * block, block)
        weights.append(
            pltpu.make_async_copy(
                weight_hbm.at[:, pl.ds(column, block)], weight_ref.at[n], weight_sem.at[n]
            )
        )
    others = [
        pltpu.make_async_copy(source, target, staged_sem.at[n])
        for n, (source, target) in enumerate(zip(sources, targets))
    ]
    for copy in weights[:1] + taps + weights[1:] + others:
        copy.start()
    for n in range(len(blocks)):
        weights[n].wait()
        for tile in range(tiles):
            if n == 0 and staged:
                taps[tile].wait()
            value = lax.dot_general(
                tap_ref[tile],
                weight_ref[n],
                (((0,), (0,)), ((), ())),
                preferred_element_type=F32,
            )
            out_ref[n, tile * tile_rows : (tile + 1) * tile_rows, :] = value.astype(BF16)
    for copy in others:
        copy.wait()


def tap_projection(where, tap_tiles, weights, blocks, head_count, dup, staged):
    tiles, depth, tile_rows = tap_tiles.shape
    block = 2 * HD
    return pl.pallas_call(
        functools.partial(tap_kernel, blocks, head_count, dup, len(staged)),
        out_shape=[jax.ShapeDtypeStruct((len(blocks), tiles * tile_rows, block), BF16)]
        + [jax.ShapeDtypeStruct(w.shape, w.dtype) for w in staged]
        + ([jax.ShapeDtypeStruct(tap_tiles.shape, BF16)] if staged else []),
        in_specs=[SMEM, HBM if staged else VMEM, HBM] + [HBM] * len(staged),
        out_specs=[VMEM] * (1 + len(staged) + bool(staged)),
        scratch_shapes=[pltpu.VMEM((len(blocks), depth, block), BF16)]
        + ([pltpu.SemaphoreType.DMA((tiles,))] if staged else [])
        + [pltpu.SemaphoreType.DMA((len(blocks),))]
        + ([pltpu.SemaphoreType.DMA((len(staged),))] if staged else []),
        compiler_params=pltpu.CompilerParams(vmem_limit_bytes=(42 if staged else 50) * MIB),
        cost_estimate=LIGHT,
        name="tap_projection",
    )(where, tap_tiles, weights, *staged)


def kv_kernel(head_count, dest_count, dup, part_count, term_counts, where_ref, *refs):
    x_ref, bias_ref, weight_ref = refs[:3]
    tap_blocks = [ref.at[n] for ref in refs[3 : 3 + part_count] for n in range(ref.shape[0])]
    terms = refs[3 + part_count : 3 + part_count + sum(term_counts)]
    outs = refs[3 + part_count + sum(term_counts) : -1]
    encoded_ref = refs[-1]
    tiles, width, tile_rows = x_ref.shape
    half_tiles = tiles // len(term_counts)
    whole, tail, extra = tail_plan(half_tiles * tile_rows, width)
    bias = one_row(bias_ref, width)
    for tile in range(tiles):
        half, row = tile // half_tiles, tile % half_tiles * tile_rows
        mine = terms[sum(term_counts[:half]) : sum(term_counts[: half + 1])]

        def summed(part, lanes):
            out = mine[0][part, lanes].astype(F32)
            for term in mine[1:]:
                out = out + term[part, lanes].astype(F32)
            return out

        total = summed(pl.ds(row, tile_rows), slice(None))
        if extra:
            chunks = range(row // extra, (row + tile_rows) // extra)
            rest = [
                summed(pl.ds(half_tiles * tile_rows, extra), slice(c * tail, (c + 1) * tail))
                for c in chunks
            ]
            rest = rest[0] if len(rest) == 1 else jnp.concatenate(rest, axis=0)
            total = jnp.concatenate([total, rest], axis=1)
        total = total + x_ref[tile].T.astype(F32) + bias
        encoded_ref[tile * tile_rows : (tile + 1) * tile_rows, :] = total.astype(BF16)
    block = 2 * HD
    mine = lax.div(where_ref[1], jnp.int32(dup))
    for head in range(head_count):
        for k in range(dest_count):
            column = ((mine ^ k) * head_count + head) * block
            weights = weight_ref[:, pl.ds(pl.multiple_of(column, block), block)]
            value = jnp.dot(encoded_ref[...], weights, preferred_element_type=F32)
            value = value + tap_blocks[head * dest_count + k][...].astype(F32)
            outs[head * dest_count + k][...] = value.astype(BF16)


def kv_projection(
    where, x_tiles, b_down, weights, tap_parts, halves, head_count, dest_count, dup
):
    terms = [term for half in halves for term in half]
    tiles, width, tile_rows = x_tiles.shape
    rows = tiles * tile_rows
    block = 2 * HD
    outs = pl.pallas_call(
        functools.partial(
            kv_kernel,
            head_count,
            dest_count,
            dup,
            len(tap_parts),
            tuple(len(half) for half in halves),
        ),
        out_shape=[jax.ShapeDtypeStruct((rows, block), BF16)] * (head_count * dest_count),
        in_specs=[SMEM] + [VMEM] * (3 + len(tap_parts) + len(terms)),
        out_specs=[VMEM] * (head_count * dest_count),
        scratch_shapes=[pltpu.VMEM((rows, width), BF16)],
        compiler_params=pltpu.CompilerParams(vmem_limit_bytes=24 * MIB),
        cost_estimate=LIGHT,
        name="kv_projection",
    )(where, x_tiles, lane_rows(b_down), weights, *tap_parts, *terms)
    return [outs[h * dest_count : (h + 1) * dest_count] for h in range(head_count)]


def finish_kernel(term_count, picks, meta_ref, gain_ref, *refs):
    terms = refs[:term_count]
    outs = refs[term_count : term_count + len(picks)]
    done_ref = refs[-1]
    rows = terms[0].shape[0]
    for row in range(0, rows, ROW_BLOCK):
        take = pl.ds(row, ROW_BLOCK)
        total = terms[0][take, :].astype(F32)
        for term in terms[1:]:
            total = total + term[take, :].astype(F32)
        keys = total[:, :HD]
        square = jnp.sum(keys * keys, axis=1, keepdims=True) * (1.0 / HD)
        keys = keys * lax.rsqrt(square + epsilon) * gain_ref[...]
        done_ref[take, :HD] = keys.astype(BF16).T
        done_ref[take, HD:] = (total[:, HD:] * VALUE_SHIFT).astype(BF16)
    for out, places in zip(outs, picks):
        for n, place in enumerate(places):
            start = pl.multiple_of(meta_ref[place] * ROW_BLOCK, ROW_BLOCK)
            out[n] = done_ref[pl.ds(start, ROW_BLOCK), :]


def finish_tiles(meta, k_gain, terms, picks):
    rows, block = terms[0].shape
    return pl.pallas_call(
        functools.partial(finish_kernel, len(terms), picks),
        out_shape=[jax.ShapeDtypeStruct((len(p), ROW_BLOCK, block), BF16) for p in picks],
        in_specs=[SMEM] + [VMEM] * (1 + len(terms)),
        out_specs=[VMEM] * len(picks),
        scratch_shapes=[pltpu.VMEM((rows, block), BF16)],
        compiler_params=pltpu.CompilerParams(vmem_limit_bytes=8 * MIB),
        cost_estimate=LIGHT,
        name="finish_tiles",
    )(meta, lane_rows(k_gain), *terms)


def attend_kernel(group_count, sources, head, has_base, meta_ref, query_ref, *refs):
    tile_refs = refs[: len(sources)]
    out_hbm, out_ref, key_ref, value_ref, out_sem = refs[len(sources) + has_base :]
    place = meta_places(group_count)
    counts = (meta_ref[place["first"]], meta_ref[place["second"]])
    text_first, text_both = meta_ref[place["text_first"]], meta_ref[place["text_both"]]
    span = MAXT * ROW_BLOCK
    text_rows, width = out_ref.shape
    heads = width // HD
    for label in range(REQ_G):
        for tile in range(1, MAXT):

            @pl.when(counts[label] <= tile)
            def _(tile=label * MAXT + tile):
                take = slice(tile * ROW_BLOCK, (tile + 1) * ROW_BLOCK)
                key_ref[:, take] = jnp.zeros((HD, ROW_BLOCK), BF16)
                value_ref[take, :] = jnp.zeros((ROW_BLOCK, 2 * HD), BF16)

    for tile_ref, places in zip(tile_refs, sources):
        for n, slot in enumerate(places):
            if slot is None:
                continue
            goes = meta_ref[place["goes"] + slot]

            @pl.when(goes >= 0)
            def _(tile_ref=tile_ref, n=n, goes=goes):
                take = pl.ds(pl.multiple_of(goes * ROW_BLOCK, ROW_BLOCK), ROW_BLOCK)
                key_ref[:, take] = tile_ref[n, :, :HD]
                value_ref[take, :HD] = tile_ref[n, :, HD:]
                value_ref[take, HD:] = jnp.ones((ROW_BLOCK, HD), BF16)

    copies = []
    for block in range(text_rows // ROW_BLOCK):
        start = block * ROW_BLOCK
        take = pl.ds(start, ROW_BLOCK)
        for label, (low, high) in enumerate(((0, text_first), (text_first, text_both))):
            meets = jnp.maximum(low, start) < jnp.minimum(high, start + ROW_BLOCK)

            def attend(key_rows, label=label, start=start, take=take, low=low, high=high):
                part = pl.ds(label * span, key_rows)
                slots = start + lax.broadcasted_iota(jnp.int32, (ROW_BLOCK, HD), 0)
                owned = (slots >= low) & (slots < high)
                for first in range(0, heads, HEAD_GROUP):
                    group = range(first, min(first + HEAD_GROUP, heads))
                    column = head * width
                    stacked = jnp.concatenate(
                        [
                            query_ref[take, column + h * HD : column + (h + 1) * HD]
                            for h in group
                        ],
                        axis=0,
                    )
                    scores = jnp.dot(stacked, key_ref[:, part], preferred_element_type=F32)
                    weights = jnp.exp2(scores).astype(BF16)
                    sums = jnp.dot(weights, value_ref[part, :], preferred_element_type=F32)
                    result = sums[:, :HD] / sums[:, HD:] * (1.0 / VALUE_SHIFT)
                    for n, h in enumerate(group):
                        lanes = slice(h * HD, (h + 1) * HD)
                        own = result[n * ROW_BLOCK : (n + 1) * ROW_BLOCK]
                        kept = 0.0 if label == 0 else out_ref[take, lanes].astype(F32)
                        out_ref[take, lanes] = jnp.where(owned, own, kept).astype(BF16)

            half = span // 2
            few = counts[label] * ROW_BLOCK <= half

            @pl.when(meets & few)
            def _(attend=attend):
                attend(half)

            @pl.when(meets & jnp.logical_not(few))
            def _(attend=attend):
                attend(span)

            if label == 0:

                @pl.when(jnp.logical_not(meets))
                def _(take=take):
                    out_ref[take, :] = jnp.zeros((ROW_BLOCK, width), BF16)

        copies.append(
            pltpu.make_async_copy(
                out_ref.at[take, :],
                out_hbm.at[take, pl.ds(head * width, width)],
                out_sem.at[block],
            )
        )
        copies[-1].start()
    for copy in copies:
        copy.wait()


def attend_head(group_count, meta, queries, tiles, sources, base, head, head_count):
    rows, width = queries.shape
    head_width = width // head_count
    group_rows = REQ_G * MAXT * ROW_BLOCK
    extra = [] if base is None else [base]
    return pl.pallas_call(
        functools.partial(attend_kernel, group_count, sources, head, len(extra)),
        out_shape=jax.ShapeDtypeStruct((rows, width), BF16),
        in_specs=[SMEM] + [VMEM] * (1 + len(tiles)) + [HBM] * len(extra),
        out_specs=HBM,
        scratch_shapes=[
            pltpu.VMEM((rows, head_width), BF16),
            pltpu.VMEM((HD, group_rows), BF16),
            pltpu.VMEM((group_rows, 2 * HD), BF16),
            pltpu.SemaphoreType.DMA((rows // ROW_BLOCK,)),
        ],
        input_output_aliases={2 + len(tiles): 0} if extra else {},
        compiler_params=pltpu.CompilerParams(vmem_limit_bytes=24 * MIB),
        cost_estimate=LIGHT,
        name="attend_head",
    )(meta, queries, *tiles, *extra)


def add_rounded(a, b):
    return (a.astype(F32) + b.astype(F32)).astype(BF16)


def after(value, *others):
    others = [v for v in others if v is not None]
    return lax.optimization_barrier((value, others))[0]


def scatter_sum(blocks, count, first_bit, earlier=None):
    blocks = dict(enumerate(blocks))
    bits = bits_of(len(blocks))
    for b in range(bits):
        pairs = xor_pairs(count, 1 << (b + first_bit))
        got, sent = {}, None
        for k in sorted((k for k in blocks if (k >> b) & 1), reverse=True):
            sent = blocks[k]
            if b == bits - 1 and earlier is not None:
                sent = after(sent, earlier)
            got[k ^ (1 << b)] = lax.ppermute(sent, "tp", pairs)
        if b == bits - 1:
            return [blocks[0], got[0]], sent
        blocks = {k: add_rounded(blocks[k], got[k]) for k in got}
    return [blocks[0]], blocks[0]


def gather_half(whole, own, first, count, ready):
    bits = bits_of(count)
    pieces = {0: own}
    for b in reversed(range(1, bits)):
        pairs = xor_pairs(count, 1 << b)
        for k in sorted(pieces):
            pieces[k | (1 << b)] = lax.ppermute(pieces[k], "tp", pairs)
    pairs = xor_pairs(count, 1)
    for k in sorted(pieces):
        if k:
            pieces[k | 1] = lax.ppermute(after(pieces[k], ready), "tp", pairs)
    pieces[0], pieces[1] = whole
    bases = tuple(first if k < 2 else 0 for k in range(count))
    return [pieces[k] for k in range(count)], bases


def local(
    x_in,
    taps,
    ln_gain,
    ln_bias,
    w_up,
    b_up,
    w_down,
    b_down,
    kv_w_out,
    kv_w_taps,
    k_gain,
    q_gain,
    queries,
    tiles_per_request,
    owner,
    text_per_request,
):
    group_count = lax.axis_size("grp")
    tp_count = lax.axis_size("tp")
    position = jnp.stack([lax.axis_index("grp"), lax.axis_index("tp")]).astype(jnp.int32)
    where = jnp.concatenate([position, tiles_per_request, owner, text_per_request])
    tiles_local = x_in.shape[0]
    x_tiles = jnp.swapaxes(x_in, 2, 3)[:, 0]
    tap_tiles = jnp.swapaxes(taps, 2, 3)[:, 0]
    head_count = max(1, KVH // tp_count)
    dup = max(1, tp_count // KVH)
    dest_count = tp_count // dup
    place = meta_places(group_count)

    halves = HALVES if tiles_local % HALVES == 0 else 1
    tiles = tiles_local // halves
    own_halves = [x_tiles[:tiles]] + [
        after(x_tiles, where)[h * tiles : (h + 1) * tiles] for h in range(1, halves)
    ]
    whole = [x_tiles, lax.ppermute(x_tiles, "tp", xor_pairs(tp_count, 1))]

    tap_blocks = [(h, k) for h in range(head_count) for k in range(dest_count)]
    early = len(tap_blocks) * TAPS_EARLY // 8
    first_taps, w_up, w_down, tap_tiles = tap_projection(
        where, tap_tiles, kv_w_taps, tap_blocks[:early], head_count, dup, (w_up, w_down)
    )
    mlp_terms = []
    ready, begun = first_taps, where
    for half in range(halves):
        pieces, bases = gather_half(whole, own_halves[half], half * tiles, tp_count, ready)
        mlp_blocks = encoder_mlp(
            begun, pieces, bases, tiles, ln_gain, ln_bias, w_up, b_up, w_down
        )
        terms, sent = scatter_sum(mlp_blocks, tp_count, 0)
        mlp_terms.append(terms)
        ready, begun = mlp_blocks[0], after(where, sent)
    (last_taps,) = tap_projection(
        begun, tap_tiles, kv_w_taps, tap_blocks[early:], head_count, dup, ()
    )
    kv_blocks = kv_projection(
        where,
        x_tiles,
        b_down,
        kv_w_out,
        (first_taps, last_taps),
        mlp_terms,
        head_count,
        dest_count,
        dup,
    )
    kv_terms, arrived = [], None
    for head in range(head_count):
        blocks = kv_blocks[head]
        for b in range(bits_of(dup)):
            pairs = xor_pairs(tp_count, 1 << b)
            blocks = [add_rounded(v, lax.ppermute(v, "tp", pairs)) for v in blocks]
        terms, sent = scatter_sum(blocks, tp_count, bits_of(dup), arrived)
        kv_terms.append(terms)
        if head == 0:
            query_rows, meta = prepare(
                after(where, sent), q_gain, queries, group_count, tiles_local
            )
        arrived = (terms[-1], meta)

    slots = slot_count_of(group_count)
    total_tiles = group_count * tiles_local
    most_other = total_tiles - REQ_G * MAXT - REQ_G * (group_count - 2)
    one_large = group_count == 4 and slots == 2 and most_other <= group_count
    send = place["send"]
    out = None

    def move(value, mask):
        return lax.ppermute(value, "grp", xor_pairs(group_count, mask))

    for head in range(head_count):
        terms = kv_terms[head]
        if one_large:
            star = place["star"]
            picks = ((send, star), (send + 1, star), (send + 2, star), (send + 3,))
            own, near, middle, far = finish_tiles(meta, k_gain, terms, picks)
            middle_got, far_got, near_got = move(middle, 2), move(far, 3), move(near, 1)
            passed = move(middle_got[1:], 1)
            tiles = (own, near_got, middle_got, far_got, passed)
            sources = ((0, 4), (1, 5), (2, 6), (3,), (7,))
        else:
            picks = tuple(
                tuple(send + s * group_count + d for s in range(slots)) for d in range(group_count)
            )
            made = finish_tiles(meta, k_gain, terms, picks)
            tiles = tuple(made[:1]) + tuple(move(made[d], d) for d in range(1, group_count))
            sources = tuple(
                tuple(s * group_count + d for s in range(slots)) for d in range(group_count)
            )
        out = attend_head(
            group_count, meta, query_rows, tiles, sources, out, head, head_count
        )
    return out


def solution(mesh):
    in_specs = (
        P(None, ("rep", "grp"), None, "tp"),
        P(None, ("rep", "grp"), None, "tp"),
        P(),
        P(),
        P(None, "tp"),
        P("tp"),
        P("tp", None),
        P("tp"),
        P("tp", None),
        P("tp", None),
        P(),
        P(),
        P(("rep", "grp"), "tp"),
        P("rep"),
        P("rep"),
        P("rep"),
    )
    out_specs = P(("rep", "grp"), "tp")
    return jax.shard_map(local, mesh=mesh, in_specs=in_specs, out_specs=out_specs, check_vma=False)
```

profile of v0, /device:TPU:0, one launch (start us, length us, event | category | flops | bytes accessed | tf_op | source)
XLA Modules:
  0.0 73.6 jit_solution(12263423213823770774)
XLA Ops:
  0.0 3.0 %collective-permute-start.1 = (bf16[4,320,128]{2,1,0:T(8,128)(2,1)}, bf16[4,320,128]{2,1,0:T(8,128)(2,1)S(1)}, u32[]{:S(2)}, u32[]{:S(2)}) collective-permute-start(bf16[4,320,128]{2,1,0:T(8,128)(2,1)} %bitcast.20), channel_id=1, source_target_pairs={{0,2},{1,3},{2,0},{3,1},{4,6},{5,7},{6,4},{7,5},{8,10},{9,11},{10,... | collective-permute-start | bytes 983048 | tf_op jit(solution)/shard_map/ppermute | solution.py:602
  3.7 1.4 %copy-done.1 = bf16[4,1,128,1600]{2,3,1,0:T(8,128)(2,1)S(1)} copy-done((bf16[4,1,128,1600]{2,3,1,0:T(8,128)(2,1)S(1)}, bf16[4,1,128,1600]{2,3,1,0:T(8,128)(2,1)}, u32[]{:S(2)}) %copy-start.1) | copy-done | bytes 1638424
  5.2 4.9 %tap_projection.2 = (bf16[3,512,256]{2,1,0:T(8,128)(2,1)S(1)}, bf16[1280,1280]{1,0:T(8,128)(2,1)S(1)}, bf16[1280,1280]{1,0:T(8,128)(2,1)S(1)}, bf16[4,1600,128]{2,1,0:T(8,128)(2,1)S(1)}) custom-call(s32[26]{0:T(128)S(1)} %concatenate.3.where_ref, bf16[4,1600,128]{2,1,0:T(8,128)(2,1)S(1)} %bitcast.19, bf16[1600,2048]{1,0:T(8,128)(2,1)} %weight_hbm.3, ...), custom_call_target="tpu_custom_call" | custom-call | flops 1024 | bytes 1024 | tf_op jit(solution)/shard_map/tap_projection/pallas_call | solution.py:335
  10.9 1.6 %collective-permute-done.2.refs_3_ = bf16[4,320,128]{2,1,0:T(8,128)(2,1)S(1)} collective-permute-done((bf16[4,320,128]{2,1,0:T(8,128)(2,1)S(1)}, bf16[4,320,128]{2,1,0:T(8,128)(2,1)S(1)}, u32[]{:S(2)}, u32[]{:S(2)}) %collective-permute-start.2) | collective-permute-done | bytes 327712 | tf_op jit(solution)/shard_map/ppermute | solution.py:606
  12.5 5.7 %encoder_mlp.1 = (bf16[640,256]{1,0:T(8,128)(2,1)S(1)}, bf16[640,256]{1,0:T(8,128)(2,1)S(1)}, bf16[640,256]{1,0:T(8,128)(2,1)S(1)}, bf16[640,256]{1,0:T(8,128)(2,1)S(1)}) custom-call(s32[26]{0:T(128)S(1)} %concatenate.3.where_ref, bf16[4,320,128]{2,1,0:T(8,128)(2,1)S(1)} %bitcast.22, bf16[4,320,128]{2,1,0:T(8,128)(2,1)S(1)} %collective-permute-done.refs_1_, ...), custom_call_target="tpu_custom_call" | custom-call | flops 1024 | bytes 1024 | tf_op jit(solution)/shard_map/encoder_mlp/pallas_call | solution.py:221
  18.8 1.1 %collective-permute-done.3 = bf16[640,256]{1,0:T(8,128)(2,1)S(1)} collective-permute-done((bf16[640,256]{1,0:T(8,128)(2,1)S(1)}, bf16[640,256]{1,0:T(8,128)(2,1)S(1)}, u32[]{:S(2)}, u32[]{:S(2)}) %collective-permute-start.3) | collective-permute-done | bytes 327712 | tf_op jit(solution)/shard_map/ppermute | solution.py:589
  20.0 1.8 %collective-permute-start.5 = (bf16[640,256]{1,0:T(8,128)(2,1)S(1)}, bf16[640,256]{1,0:T(8,128)(2,1)S(1)}, u32[]{:S(2)}, u32[]{:S(2)}) collective-permute-start(bf16[640,256]{1,0:T(8,128)(2,1)S(1)} %add_convert_fusion.1), channel_id=1, source_target_pairs={{0,2},{1,3},{2,0},{3,1},{4,6},{5,7},{6,4},{7,5},{8,10},{9,11},{10,... | collective-permute-start | bytes 983048 | tf_op jit(solution)/shard_map/ppermute | solution.py:589
  21.8 5.3 %tap_projection.3.refs_4_ = bf16[5,512,256]{2,1,0:T(8,128)(2,1)S(1)} custom-call(s32[26]{0:T(128)S(1)} %concatenate.3.where_ref, bf16[4,1600,128]{2,1,0:T(8,128)(2,1)S(1)} %get-tuple-element.42.tap_hbm, bf16[1600,2048]{1,0:T(8,128)(2,1)} %weight_hbm.3), custom_call_target="tpu_custom_call" | custom-call | flops 1024 | bytes 1024 | tf_op jit(solution)/shard_map/tap_projection/pallas_call | solution.py:335
  27.2 2.6 %collective-permute-done.5.refs_6_ = bf16[640,256]{1,0:T(8,128)(2,1)S(1)} collective-permute-done((bf16[640,256]{1,0:T(8,128)(2,1)S(1)}, bf16[640,256]{1,0:T(8,128)(2,1)S(1)}, u32[]{:S(2)}, u32[]{:S(2)}) %collective-permute-start.5) | collective-permute-done | bytes 327712 | tf_op jit(solution)/shard_map/ppermute | solution.py:589
  29.8 1.9 %kv_projection.1 = (bf16[512,256]{1,0:T(8,128)(2,1)S(1)}, bf16[512,256]{1,0:T(8,128)(2,1)S(1)}, bf16[512,256]{1,0:T(8,128)(2,1)S(1)}, bf16[512,256]{1,0:T(8,128)...) custom-call(s32[26]{0:T(128)S(1)} %concatenate.3.where_ref, ...), custom_call_target="tpu_custom_call" | custom-call | flops 1024 | bytes 1024 | tf_op jit(solution)/shard_map/kv_projection/pallas_call | solution.py:401
  33.3 1.8 %collective-permute-start.9 = (bf16[512,256]{1,0:T(8,128)(2,1)S(1)}, bf16[512,256]{1,0:T(8,128)(2,1)S(1)}, u32[]{:S(2)}, u32[]{:S(2)}) collective-permute-start(bf16[512,256]{1,0:T(8,128)(2,1)S(1)} %add_convert_fusion.5), channel_id=1, source_target_pairs={{0,2},{1,3},{2,0},{3,1},{4,6},{5,7},{6,4},{7,5},{8,10},{9,11},{10,... | collective-permute-start | bytes 786440 | tf_op jit(solution)/shard_map/ppermute | solution.py:589
  35.8 2.8 %prepare.1 = (bf16[512,2048]{1,0:T(8,128)(2,1)S(1)}, s32[24]{0:T(128)S(1)}) custom-call(s32[26]{0:T(128)S(1)} %concatenate.3.where_ref, f32[1,128]{1,0:T(1,128)S(1)} %bitcast.29, bf16[512,2048]{1,0:T(8,128)(2,1)S(1)} %copy-done), custom_call_target="tpu_custom_call" | custom-call | flops 1024 | bytes 1024 | tf_op jit(solution)/shard_map/prepare/pallas_call | solution.py:269
  38.6 3.2 %collective-permute-done.9.refs_1_ = bf16[512,256]{1,0:T(8,128)(2,1)S(1)} collective-permute-done((bf16[512,256]{1,0:T(8,128)(2,1)S(1)}, bf16[512,256]{1,0:T(8,128)(2,1)S(1)}, u32[]{:S(2)}, u32[]{:S(2)}) %collective-permute-start.9) | collective-permute-done | bytes 262176 | tf_op jit(solution)/shard_map/ppermute | solution.py:589
  41.8 1.7 %collective-permute-start.10 = (bf16[512,256]{1,0:T(8,128)(2,1)S(1)}, bf16[512,256]{1,0:T(8,128)(2,1)S(1)}, u32[]{:S(2)}, u32[]{:S(2)}) collective-permute-start(bf16[512,256]{1,0:T(8,128)(2,1)S(1)} %add_convert_fusion.3), channel_id=1, source_target_pairs={{0,2},{1,3},{2,0},{3,1},{4,6},{5,7},{6,4},{7,5},{8,10},{9,11},{10,... | collective-permute-start | bytes 786440 | tf_op jit(solution)/shard_map/ppermute | solution.py:589
  44.5 2.7 %collective-permute-start.17 = (bf16[2,128,256]{2,1,0:T(8,128)(2,1)S(1)}, bf16[2,128,256]{2,1,0:T(8,128)(2,1)S(1)}, u32[]{:S(2)}, u32[]{:S(2)}) collective-permute-start(bf16[2,128,256]{2,1,0:T(8,128)(2,1)S(1)} %get-tuple-element.63), channel_id=1, source_target_pairs={{0,8},{4,12},{8,0},{12,4},{1,9},{5,13},{9,1},{13,5},{2,10},{6,14},... | collective-permute-start | bytes 393224 | tf_op jit(solution)/shard_map/ppermute | solution.py:700
  47.1 2.1 %collective-permute-done.10.refs_1_ = bf16[512,256]{1,0:T(8,128)(2,1)S(1)} collective-permute-done((bf16[512,256]{1,0:T(8,128)(2,1)S(1)}, bf16[512,256]{1,0:T(8,128)(2,1)S(1)}, u32[]{:S(2)}, u32[]{:S(2)}) %collective-permute-start.10) | collective-permute-done | bytes 262176 | tf_op jit(solution)/shard_map/ppermute | solution.py:589
  50.1 2.9 %collective-permute-start.12 = (bf16[2,128,256]{2,1,0:T(8,128)(2,1)S(1)}, bf16[2,128,256]{2,1,0:T(8,128)(2,1)S(1)}, u32[]{:S(2)}, u32[]{:S(2)}) collective-permute-start(bf16[2,128,256]{2,1,0:T(8,128)(2,1)S(1)} %get-tuple-element.57), channel_id=1, source_target_pairs={{0,8},{4,12},{8,0},{12,4},{1,9},{5,13},{9,1},{13,5},{2,10},{6,14},... | collective-permute-start | bytes 393224 | tf_op jit(solution)/shard_map/ppermute | solution.py:700
  53.0 1.6 %collective-permute-start.16 = (bf16[2,128,256]{2,1,0:T(8,128)(2,1)S(1)}, bf16[2,128,256]{2,1,0:T(8,128)(2,1)S(1)}, u32[]{:S(2)}, u32[]{:S(2)}) collective-permute-start(bf16[2,128,256]{2,1,0:T(8,128)(2,1)S(1)} %get-tuple-element.62), channel_id=1, source_target_pairs={{0,4},{4,0},{8,12},{12,8},{1,5},{5,1},{9,13},{13,9},{2,6},{6,2},{1... | collective-permute-start | bytes 393224 | tf_op jit(solution)/shard_map/ppermute | solution.py:700
  55.4 1.2 %collective-permute-start.19 = (bf16[1,128,256]{2,1,0:T(8,128)(2,1)S(1)}, bf16[1,128,256]{2,1,0:T(8,128)(2,1)S(1)}, u32[]{:S(2)}, u32[]{:S(2)}) collective-permute-start(bf16[1,128,256]{2,1,0:T(8,128)(2,1)S(1)} %slice.9), channel_id=1, source_target_pairs={{0,4},{4,0},{8,12},{12,8},{1,5},{5,1},{9,13},{13,9},{2,6},{6,2},{1... | collective-permute-start | bytes 196616 | tf_op jit(solution)/shard_map/ppermute | solution.py:700
  56.6 3.1 %collective-permute-done.12.refs_2_ = bf16[2,128,256]{2,1,0:T(8,128)(2,1)S(1)} collective-permute-done((bf16[2,128,256]{2,1,0:T(8,128)(2,1)S(1)}, bf16[2,128,256]{2,1,0:T(8,128)(2,1)S(1)}, u32[]{:S(2)}, u32[]{:S(2)}) %collective-permute-start.12) | collective-permute-done | bytes 131104 | tf_op jit(solution)/shard_map/ppermute | solution.py:700
  59.7 3.6 %collective-permute-start.13 = (bf16[1,128,256]{2,1,0:T(8,128)(2,1)S(1)}, bf16[1,128,256]{2,1,0:T(8,128)(2,1)S(1)}, u32[]{:S(2)}, u32[]{:S(2)}) collective-permute-start(bf16[1,128,256]{2,1,0:T(8,128)(2,1)S(1)} %get-tuple-element.58), channel_id=1, source_target_pairs={{0,12},{4,8},{8,4},{12,0},{1,13},{5,9},{9,5},{13,1},{2,14},{6,10},... | collective-permute-start | bytes 196616 | tf_op jit(solution)/shard_map/ppermute | solution.py:700
  63.5 2.1 %collective-permute-done.19.refs_4_ = bf16[1,128,256]{2,1,0:T(8,128)(2,1)S(1)} collective-permute-done((bf16[1,128,256]{2,1,0:T(8,128)(2,1)S(1)}, bf16[1,128,256]{2,1,0:T(8,128)(2,1)S(1)}, u32[]{:S(2)}, u32[]{:S(2)}) %collective-permute-start.19) | collective-permute-done | bytes 65568 | tf_op jit(solution)/shard_map/ppermute | solution.py:700
  65.6 3.8 %attend_head.2.refs_5_ = bf16[512,2048]{1,0:T(8,128)(2,1)} custom-call(s32[24]{0:T(128)S(1)} %get-tuple-element.48.meta_ref, bf16[512,2048]{1,0:T(8,128)(2,1)S(1)} %get-tuple-element.49.query_ref, bf16[2,128,256]{2,1,0:T(8,128)(2,1)S(1)} %get-tuple-element.61.refs_0_, bf16[2,128,256]{2,1,0:T(8,128)(2,1)S(1)} %collective-permute-done.16.refs_1_, ...), custom_call_target="tpu_custom_call" | custom-call | flops 1024 | bytes 1024 | tf_op jit(solution)/shard_map/attend_head/pallas_call | solution.py:552
  69.4 4.0 %attend_head.3 = bf16[512,2048]{1,0:T(8,128)(2,1)} custom-call(s32[24]{0:T(128)S(1)} %get-tuple-element.48.meta_ref, bf16[512,2048]{1,0:T(8,128)(2,1)S(1)} %get-tuple-element.49.query_ref, bf16[2,128,256]{2,1,0:T(8,128)(2,1)S(1)} %get-tuple-element.55.refs_0_, ...), custom_call_target="tpu_custom_call", output_to_operand_aliasing={{}: (7, {})} | custom-call | flops 1024 | bytes 1024 | tf_op jit(solution)/shard_map/attend_head/pallas_call | solution.py:552
  (55 shorter events, 7.3 us)
Async XLA Ops:
  0.0 10.9 %collective-permute-start.1 = (bf16[4,320,128]{2,1,0:T(8,128)(2,1)}, bf16[4,320,128]{2,1,0:T(8,128)(2,1)S(1)}, u32[]{:S(2)}, u32[]{:S(2)}) collective-permute-start(bf16[4,320,128]{2,1,0:T(8,128)(2,1)} %bitcast.20), channel_id=1, source_target_pairs={{0,2},{1,3},{2,0},{3,1},{4,6},{5,7},{6,4},{7,5},{8,10},{9,11},{10,... | collective-permute-start | bytes 983048 | tf_op jit(solution)/shard_map/ppermute | solution.py:602
  3.0 7.9 %collective-permute-start = (bf16[4,320,128]{2,1,0:T(8,128)(2,1)}, bf16[4,320,128]{2,1,0:T(8,128)(2,1)S(1)}, u32[]{:S(2)}, u32[]{:S(2)}) collective-permute-start(bf16[4,320,128]{2,1,0:T(8,128)(2,1)} %bitcast.21), channel_id=1, source_target_pairs={{0,1},{1,0},{2,3},{3,2},{4,5},{5,4},{6,7},{7,6},{8,9},{9,8},{10,11... | collective-permute-start | bytes 983048 | tf_op jit(solution)/shard_map/ppermute | solution.py:647
  10.9 1.6 %collective-permute-start.2 = (bf16[4,320,128]{2,1,0:T(8,128)(2,1)S(1)}, bf16[4,320,128]{2,1,0:T(8,128)(2,1)S(1)}, u32[]{:S(2)}, u32[]{:S(2)}) collective-permute-start(bf16[4,320,128]{2,1,0:T(8,128)(2,1)S(1)} %collective-permute-done.1.refs_2_), channel_id=1, source_target_pairs={{0,1},{1,0},{2,3},{3,2},{4,5},{5,4},{6,7},{7,6},{8,9},{9,8},{10,11... | collective-permute-start | bytes 983048 | tf_op jit(solution)/shard_map/ppermute | solution.py:606
  12.5 9.3 %copy-start.9 = (f32[320]{0:T(512)S(1)}, f32[320]{0:T(512)}, u32[]{:S(2)}) copy-start(f32[320]{0:T(512)} %param.23) | copy-start | bytes 3844
  18.2 1.7 %collective-permute-start.3 = (bf16[640,256]{1,0:T(8,128)(2,1)S(1)}, bf16[640,256]{1,0:T(8,128)(2,1)S(1)}, u32[]{:S(2)}, u32[]{:S(2)}) collective-permute-start(bf16[640,256]{1,0:T(8,128)(2,1)S(1)} %get-tuple-element.40), channel_id=1, source_target_pairs={{0,1},{1,0},{2,3},{3,2},{4,5},{5,4},{6,7},{7,6},{8,9},{9,8},{10,11... | collective-permute-start | bytes 983048 | tf_op jit(solution)/shard_map/ppermute | solution.py:589
  18.4 8.7 %collective-permute-start.4 = (bf16[640,256]{1,0:T(8,128)(2,1)S(1)}, bf16[640,256]{1,0:T(8,128)(2,1)S(1)}, u32[]{:S(2)}, u32[]{:S(2)}) collective-permute-start(bf16[640,256]{1,0:T(8,128)(2,1)S(1)} %get-tuple-element.44), channel_id=1, source_target_pairs={{0,1},{1,0},{2,3},{3,2},{4,5},{5,4},{6,7},{7,6},{8,9},{9,8},{10,11... | collective-permute-start | bytes 983048 | tf_op jit(solution)/shard_map/ppermute | solution.py:589
  20.0 9.8 %collective-permute-start.5 = (bf16[640,256]{1,0:T(8,128)(2,1)S(1)}, bf16[640,256]{1,0:T(8,128)(2,1)S(1)}, u32[]{:S(2)}, u32[]{:S(2)}) collective-permute-start(bf16[640,256]{1,0:T(8,128)(2,1)S(1)} %add_convert_fusion.1), channel_id=1, source_target_pairs={{0,2},{1,3},{2,0},{3,1},{4,6},{5,7},{6,4},{7,5},{8,10},{9,11},{10,... | collective-permute-start | bytes 983048 | tf_op jit(solution)/shard_map/ppermute | solution.py:589
  21.8 8.0 %copy-start.3 = (bf16[320,2048]{1,0:T(8,128)(2,1)S(1)}, bf16[320,2048]{1,0:T(8,128)(2,1)}, u32[]{:S(2)}) copy-start(bf16[320,2048]{1,0:T(8,128)(2,1)} %refs_2_.1) | copy-start | bytes 3932164
  27.2 8.6 %copy-start = (bf16[512,2048]{1,0:T(8,128)(2,1)S(1)}, bf16[512,2048]{1,0:T(8,128)(2,1)}, u32[]{:S(2)}) copy-start(bf16[512,2048]{1,0:T(8,128)(2,1)} %query_ref.1) | copy-start | bytes 6291460
  27.2 8.6 %copy-start.8 = (f32[128]{0:T(128)S(1)}, f32[128]{0:T(128)}, u32[]{:S(2)}) copy-start(f32[128]{0:T(128)} %param.27) | copy-start | bytes 1540
  31.7 1.6 %collective-permute-start.6 = (bf16[512,256]{1,0:T(8,128)(2,1)S(1)}, bf16[512,256]{1,0:T(8,128)(2,1)S(1)}, u32[]{:S(2)}, u32[]{:S(2)}) collective-permute-start(bf16[512,256]{1,0:T(8,128)(2,1)S(1)} %get-tuple-element.46), channel_id=1, source_target_pairs={{0,1},{1,0},{2,3},{3,2},{4,5},{5,4},{6,7},{7,6},{8,9},{9,8},{10,11... | collective-permute-start | bytes 786440 | tf_op jit(solution)/shard_map/ppermute | solution.py:589
  31.7 3.9 %collective-permute-start.8 = (bf16[512,256]{1,0:T(8,128)(2,1)S(1)}, bf16[512,256]{1,0:T(8,128)(2,1)S(1)}, u32[]{:S(2)}, u32[]{:S(2)}) collective-permute-start(bf16[512,256]{1,0:T(8,128)(2,1)S(1)} %get-tuple-element.53), channel_id=1, source_target_pairs={{0,1},{1,0},{2,3},{3,2},{4,5},{5,4},{6,7},{7,6},{8,9},{9,8},{10,11... | collective-permute-start | bytes 786440 | tf_op jit(solution)/shard_map/ppermute | solution.py:589
  33.3 8.4 %collective-permute-start.9 = (bf16[512,256]{1,0:T(8,128)(2,1)S(1)}, bf16[512,256]{1,0:T(8,128)(2,1)S(1)}, u32[]{:S(2)}, u32[]{:S(2)}) collective-permute-start(bf16[512,256]{1,0:T(8,128)(2,1)S(1)} %add_convert_fusion.5), channel_id=1, source_target_pairs={{0,2},{1,3},{2,0},{3,1},{4,6},{5,7},{6,4},{7,5},{8,10},{9,11},{10,... | collective-permute-start | bytes 786440 | tf_op jit(solution)/shard_map/ppermute | solution.py:589
  35.2 8.4 %collective-permute-start.15 = (bf16[512,256]{1,0:T(8,128)(2,1)S(1)}, bf16[512,256]{1,0:T(8,128)(2,1)S(1)}, u32[]{:S(2)}, u32[]{:S(2)}) collective-permute-start(bf16[512,256]{1,0:T(8,128)(2,1)S(1)} %get-tuple-element.60), channel_id=1, source_target_pairs={{0,1},{1,0},{2,3},{3,2},{4,5},{5,4},{6,7},{7,6},{8,9},{9,8},{10,11... | collective-permute-start | bytes 786440 | tf_op jit(solution)/shard_map/ppermute | solution.py:589
  35.2 8.4 %collective-permute-start.7 = (bf16[512,256]{1,0:T(8,128)(2,1)S(1)}, bf16[512,256]{1,0:T(8,128)(2,1)S(1)}, u32[]{:S(2)}, u32[]{:S(2)}) collective-permute-start(bf16[512,256]{1,0:T(8,128)(2,1)S(1)} %get-tuple-element.51), channel_id=1, source_target_pairs={{0,1},{1,0},{2,3},{3,2},{4,5},{5,4},{6,7},{7,6},{8,9},{9,8},{10,11... | collective-permute-start | bytes 786440 | tf_op jit(solution)/shard_map/ppermute | solution.py:589
  41.8 7.5 %collective-permute-start.10 = (bf16[512,256]{1,0:T(8,128)(2,1)S(1)}, bf16[512,256]{1,0:T(8,128)(2,1)S(1)}, u32[]{:S(2)}, u32[]{:S(2)}) collective-permute-start(bf16[512,256]{1,0:T(8,128)(2,1)S(1)} %add_convert_fusion.3), channel_id=1, source_target_pairs={{0,2},{1,3},{2,0},{3,1},{4,6},{5,7},{6,4},{7,5},{8,10},{9,11},{10,... | collective-permute-start | bytes 786440 | tf_op jit(solution)/shard_map/ppermute | solution.py:589
  44.5 11.0 %collective-permute-start.17 = (bf16[2,128,256]{2,1,0:T(8,128)(2,1)S(1)}, bf16[2,128,256]{2,1,0:T(8,128)(2,1)S(1)}, u32[]{:S(2)}, u32[]{:S(2)}) collective-permute-start(bf16[2,128,256]{2,1,0:T(8,128)(2,1)S(1)} %get-tuple-element.63), channel_id=1, source_target_pairs={{0,8},{4,12},{8,0},{12,4},{1,9},{5,13},{9,1},{13,5},{2,10},{6,14},... | collective-permute-start | bytes 393224 | tf_op jit(solution)/shard_map/ppermute | solution.py:700
  50.1 9.7 %collective-permute-start.12 = (bf16[2,128,256]{2,1,0:T(8,128)(2,1)S(1)}, bf16[2,128,256]{2,1,0:T(8,128)(2,1)S(1)}, u32[]{:S(2)}, u32[]{:S(2)}) collective-permute-start(bf16[2,128,256]{2,1,0:T(8,128)(2,1)S(1)} %get-tuple-element.57), channel_id=1, source_target_pairs={{0,8},{4,12},{8,0},{12,4},{1,9},{5,13},{9,1},{13,5},{2,10},{6,14},... | collective-permute-start | bytes 393224 | tf_op jit(solution)/shard_map/ppermute | solution.py:700
  53.0 10.5 %collective-permute-start.16 = (bf16[2,128,256]{2,1,0:T(8,128)(2,1)S(1)}, bf16[2,128,256]{2,1,0:T(8,128)(2,1)S(1)}, u32[]{:S(2)}, u32[]{:S(2)}) collective-permute-start(bf16[2,128,256]{2,1,0:T(8,128)(2,1)S(1)} %get-tuple-element.62), channel_id=1, source_target_pairs={{0,4},{4,0},{8,12},{12,8},{1,5},{5,1},{9,13},{13,9},{2,6},{6,2},{1... | collective-permute-start | bytes 393224 | tf_op jit(solution)/shard_map/ppermute | solution.py:700
  54.5 8.9 %collective-permute-start.18 = (bf16[1,128,256]{2,1,0:T(8,128)(2,1)S(1)}, bf16[1,128,256]{2,1,0:T(8,128)(2,1)S(1)}, u32[]{:S(2)}, u32[]{:S(2)}) collective-permute-start(bf16[1,128,256]{2,1,0:T(8,128)(2,1)S(1)} %get-tuple-element.64), channel_id=1, source_target_pairs={{0,12},{4,8},{8,4},{12,0},{1,13},{5,9},{9,5},{13,1},{2,14},{6,10},... | collective-permute-start | bytes 196616 | tf_op jit(solution)/shard_map/ppermute | solution.py:700
  54.5 14.9 %collective-permute-start.11 = (bf16[2,128,256]{2,1,0:T(8,128)(2,1)S(1)}, bf16[2,128,256]{2,1,0:T(8,128)(2,1)S(1)}, u32[]{:S(2)}, u32[]{:S(2)}) collective-permute-start(bf16[2,128,256]{2,1,0:T(8,128)(2,1)S(1)} %get-tuple-element.56), channel_id=1, source_target_pairs={{0,4},{4,0},{8,12},{12,8},{1,5},{5,1},{9,13},{13,9},{2,6},{6,2},{1... | collective-permute-start | bytes 393224 | tf_op jit(solution)/shard_map/ppermute | solution.py:700
  55.4 10.2 %collective-permute-start.19 = (bf16[1,128,256]{2,1,0:T(8,128)(2,1)S(1)}, bf16[1,128,256]{2,1,0:T(8,128)(2,1)S(1)}, u32[]{:S(2)}, u32[]{:S(2)}) collective-permute-start(bf16[1,128,256]{2,1,0:T(8,128)(2,1)S(1)} %slice.9), channel_id=1, source_target_pairs={{0,4},{4,0},{8,12},{12,8},{1,5},{5,1},{9,13},{13,9},{2,6},{6,2},{1... | collective-permute-start | bytes 196616 | tf_op jit(solution)/shard_map/ppermute | solution.py:700
  59.7 9.6 %collective-permute-start.13 = (bf16[1,128,256]{2,1,0:T(8,128)(2,1)S(1)}, bf16[1,128,256]{2,1,0:T(8,128)(2,1)S(1)}, u32[]{:S(2)}, u32[]{:S(2)}) collective-permute-start(bf16[1,128,256]{2,1,0:T(8,128)(2,1)S(1)} %get-tuple-element.58), channel_id=1, source_target_pairs={{0,12},{4,8},{8,4},{12,0},{1,13},{5,9},{9,5},{13,1},{2,14},{6,10},... | collective-permute-start | bytes 196616 | tf_op jit(solution)/shard_map/ppermute | solution.py:700
  63.4 6.0 %collective-permute-start.14 = (bf16[1,128,256]{2,1,0:T(8,128)(2,1)S(1)}, bf16[1,128,256]{2,1,0:T(8,128)(2,1)S(1)}, u32[]{:S(2)}, u32[]{:S(2)}) collective-permute-start(bf16[1,128,256]{2,1,0:T(8,128)(2,1)S(1)} %slice.8), channel_id=1, source_target_pairs={{0,4},{4,0},{8,12},{12,8},{1,5},{5,1},{9,13},{13,9},{2,6},{6,2},{1... | collective-permute-start | bytes 196616 | tf_op jit(solution)/shard_map/ppermute | solution.py:700
  (6 other events, 38.8 us)
where the time goes:
time: 73.4 us; the launch traced here: 73.6 us
  Pallas kernels  29.9 us (41%)
  starting transfers between devices  22.9 us (31%)
  waiting for transfers between devices  17.7 us (24%)
  local copies, waits for them, and re-layouts  2.25 us (3%)
    ppermute x8, starting transfers between devices, move(): return lax.ppermute(value, 'grp', xor_pairs(group_count, mask))  12.9 us
    pallas_call x2, Pallas kernels, tap_projection(): pl.pallas_call(functools.partial(tap_kernel, blocks, head_count, dup, len...  10.2 us
    ppermute x9, waiting for transfers between devices, scatter_sum(): got[k ^ 1 << b] = lax.ppermute(sent, 'tp', pairs)  10.1 us
    pallas_call x2, Pallas kernels, attend_head(): pl.pallas_call(functools.partial(attend_kernel, group_count, sources, hea...  7.74 us
    ppermute x9, starting transfers between devices, scatter_sum(): got[k ^ 1 << b] = lax.ppermute(sent, 'tp', pairs)  6.99 us
    pallas_call x1, Pallas kernels, encoder_mlp(): pl.pallas_call(functools.partial(mlp_kernel, count, bases, tiles), out_sh...  5.66 us
    ppermute x8, waiting for transfers between devices, move(): return lax.ppermute(value, 'grp', xor_pairs(group_count, mask))  5.25 us
    ppermute x1, starting transfers between devices, gather_half(): pieces[k | 1 << b] = lax.ppermute(pieces[k], 'tp', pairs)  2.97 us
  transfers between devices with their start and end apart: 20, of which 9 were waited for; matrix products, arithmetic and copies ran while one was open for 2% of the time, Pallas kernels for 25%

commit v1 on v0

--- a/solution.py
+++ b/solution.py
@@ -706,7 +706,7 @@
             picks = ((send, star), (send + 1, star), (send + 2, star), (send + 3,))
             own, near, middle, far = finish_tiles(meta, k_gain, terms, picks)
             middle_got, far_got, near_got = move(middle, 2), move(far, 3), move(near, 1)
-            passed = move(middle_got[1:], 1)
+            passed = move(after(middle_got[1:], far_got, out), 1)
             tiles = (own, near_got, middle_got, far_got, passed)
             sources = ((0, 4), (1, 5), (2, 6), (3,), (7,))
         else:

time: 73.4 us -> 75.7 us (1.031)
  starting transfers between devices: 22.9 us -> 24.9 us
    ppermute x8, starting transfers between devices: 12.9 us -> 15 us  [move(): return lax.ppermute(value, 'grp', xor_pairs(group_count, mask))]
    ppermute x9, waiting for transfers between devices: 10.1 us -> 8.51 us  [scatter_sum(): got[k ^ 1 << b] = lax.ppermute(sent, 'tp', pairs)]
    ppermute x8, waiting for transfers between devices: 5.25 us -> 6.5 us  [move(): return lax.ppermute(value, 'grp', xor_pairs(group_count, mask))]
  transfers between devices with their start and end apart: 20 -> 20, of which waited for: 9 -> 11; matrix products, arithmetic and copies ran while one was open for 2% -> 2% of each run, Pallas kernels for 25% -> 24%
where the time goes in v1:
time: 75.7 us; the launch traced here: 75.2 us
  Pallas kernels  29.7 us (39%)
  starting transfers between devices  24.9 us (33%)
  waiting for transfers between devices  17.4 us (23%)
  local copies, waits for them, and re-layouts  2.25 us (3%)
    ppermute x8, starting transfers between devices, move(): return lax.ppermute(value, 'grp', xor_pairs(group_count, mask))  15 us
    pallas_call x2, Pallas kernels, tap_projection(): pl.pallas_call(functools.partial(tap_kernel, blocks, head_count, dup, len...  10.2 us
    ppermute x9, waiting for transfers between devices, scatter_sum(): got[k ^ 1 << b] = lax.ppermute(sent, 'tp', pairs)  8.51 us
    pallas_call x2, Pallas kernels, attend_head(): pl.pallas_call(functools.partial(attend_kernel, group_count, sources, hea...  7.62 us
    ppermute x9, starting transfers between devices, scatter_sum(): got[k ^ 1 << b] = lax.ppermute(sent, 'tp', pairs)  6.99 us
    ppermute x8, waiting for transfers between devices, move(): return lax.ppermute(value, 'grp', xor_pairs(group_count, mask))  6.5 us
    pallas_call x1, Pallas kernels, encoder_mlp(): pl.pallas_call(functools.partial(mlp_kernel, count, bases, tiles), out_sh...  5.66 us
    ppermute x1, starting transfers between devices, gather_half(): pieces[k | 1 << b] = lax.ppermute(pieces[k], 'tp', pairs)  2.97 us
  transfers between devices with their start and end apart: 20, of which 11 were waited for; matrix products, arithmetic and copies ran while one was open for 2% of the time, Pallas kernels for 24%

profile of v1, /device:TPU:0, one launch (start us, length us, event | category | flops | bytes accessed | tf_op | source)
XLA Modules:
  0.0 75.2 jit_solution(10785733786088542107)
XLA Ops:
  0.0 3.0 %collective-permute-start.1 = (bf16[4,320,128]{2,1,0:T(8,128)(2,1)}, bf16[4,320,128]{2,1,0:T(8,128)(2,1)S(1)}, u32[]{:S(2)}, u32[]{:S(2)}) collective-permute-start(bf16[4,320,128]{2,1,0:T(8,128)(2,1)} %bitcast.20), channel_id=1, source_target_pairs={{0,2},{1,3},{2,0},{3,1},{4,6},{5,7},{6,4},{7,5},{8,10},{9,11},{10,... | collective-permute-start | bytes 983048 | tf_op jit(solution)/shard_map/ppermute | solution.py:602
  3.7 1.4 %copy-done.1 = bf16[4,1,128,1600]{2,3,1,0:T(8,128)(2,1)S(1)} copy-done((bf16[4,1,128,1600]{2,3,1,0:T(8,128)(2,1)S(1)}, bf16[4,1,128,1600]{2,3,1,0:T(8,128)(2,1)}, u32[]{:S(2)}) %copy-start.1) | copy-done | bytes 1638424
  5.2 4.9 %tap_projection.2 = (bf16[3,512,256]{2,1,0:T(8,128)(2,1)S(1)}, bf16[1280,1280]{1,0:T(8,128)(2,1)S(1)}, bf16[1280,1280]{1,0:T(8,128)(2,1)S(1)}, bf16[4,1600,128]{2,1,0:T(8,128)(2,1)S(1)}) custom-call(s32[26]{0:T(128)S(1)} %concatenate.3.where_ref, bf16[4,1600,128]{2,1,0:T(8,128)(2,1)S(1)} %bitcast.19, bf16[1600,2048]{1,0:T(8,128)(2,1)} %weight_hbm.3, ...), custom_call_target="tpu_custom_call" | custom-call | flops 1024 | bytes 1024 | tf_op jit(solution)/shard_map/tap_projection/pallas_call | solution.py:335
  10.9 1.6 %collective-permute-done.2.refs_3_ = bf16[4,320,128]{2,1,0:T(8,128)(2,1)S(1)} collective-permute-done((bf16[4,320,128]{2,1,0:T(8,128)(2,1)S(1)}, bf16[4,320,128]{2,1,0:T(8,128)(2,1)S(1)}, u32[]{:S(2)}, u32[]{:S(2)}) %collective-permute-start.2) | collective-permute-done | bytes 327712 | tf_op jit(solution)/shard_map/ppermute | solution.py:606
  12.5 5.7 %encoder_mlp.1 = (bf16[640,256]{1,0:T(8,128)(2,1)S(1)}, bf16[640,256]{1,0:T(8,128)(2,1)S(1)}, bf16[640,256]{1,0:T(8,128)(2,1)S(1)}, bf16[640,256]{1,0:T(8,128)(2,1)S(1)}) custom-call(s32[26]{0:T(128)S(1)} %concatenate.3.where_ref, bf16[4,320,128]{2,1,0:T(8,128)(2,1)S(1)} %bitcast.22, bf16[4,320,128]{2,1,0:T(8,128)(2,1)S(1)} %collective-permute-done.refs_1_, ...), custom_call_target="tpu_custom_call" | custom-call | flops 1024 | bytes 1024 | tf_op jit(solution)/shard_map/encoder_mlp/pallas_call | solution.py:221
  18.8 1.1 %collective-permute-done.3 = bf16[640,256]{1,0:T(8,128)(2,1)S(1)} collective-permute-done((bf16[640,256]{1,0:T(8,128)(2,1)S(1)}, bf16[640,256]{1,0:T(8,128)(2,1)S(1)}, u32[]{:S(2)}, u32[]{:S(2)}) %collective-permute-start.3) | collective-permute-done | bytes 327712 | tf_op jit(solution)/shard_map/ppermute | solution.py:589
  20.0 1.8 %collective-permute-start.5 = (bf16[640,256]{1,0:T(8,128)(2,1)S(1)}, bf16[640,256]{1,0:T(8,128)(2,1)S(1)}, u32[]{:S(2)}, u32[]{:S(2)}) collective-permute-start(bf16[640,256]{1,0:T(8,128)(2,1)S(1)} %add_convert_fusion.1), channel_id=1, source_target_pairs={{0,2},{1,3},{2,0},{3,1},{4,6},{5,7},{6,4},{7,5},{8,10},{9,11},{10,... | collective-permute-start | bytes 983048 | tf_op jit(solution)/shard_map/ppermute | solution.py:589
  21.8 5.3 %tap_projection.3.refs_4_ = bf16[5,512,256]{2,1,0:T(8,128)(2,1)S(1)} custom-call(s32[26]{0:T(128)S(1)} %concatenate.3.where_ref, bf16[4,1600,128]{2,1,0:T(8,128)(2,1)S(1)} %get-tuple-element.44.tap_hbm, bf16[1600,2048]{1,0:T(8,128)(2,1)} %weight_hbm.3), custom_call_target="tpu_custom_call" | custom-call | flops 1024 | bytes 1024 | tf_op jit(solution)/shard_map/tap_projection/pallas_call | solution.py:335
  27.2 2.6 %collective-permute-done.5.refs_6_ = bf16[640,256]{1,0:T(8,128)(2,1)S(1)} collective-permute-done((bf16[640,256]{1,0:T(8,128)(2,1)S(1)}, bf16[640,256]{1,0:T(8,128)(2,1)S(1)}, u32[]{:S(2)}, u32[]{:S(2)}) %collective-permute-start.5) | collective-permute-done | bytes 327712 | tf_op jit(solution)/shard_map/ppermute | solution.py:589
  29.8 1.9 %kv_projection.1 = (bf16[512,256]{1,0:T(8,128)(2,1)S(1)}, bf16[512,256]{1,0:T(8,128)(2,1)S(1)}, bf16[512,256]{1,0:T(8,128)(2,1)S(1)}, bf16[512,256]{1,0:T(8,128)...) custom-call(s32[26]{0:T(128)S(1)} %concatenate.3.where_ref, ...), custom_call_target="tpu_custom_call" | custom-call | flops 1024 | bytes 1024 | tf_op jit(solution)/shard_map/kv_projection/pallas_call | solution.py:401
  33.4 1.8 %collective-permute-start.9 = (bf16[512,256]{1,0:T(8,128)(2,1)S(1)}, bf16[512,256]{1,0:T(8,128)(2,1)S(1)}, u32[]{:S(2)}, u32[]{:S(2)}) collective-permute-start(bf16[512,256]{1,0:T(8,128)(2,1)S(1)} %add_convert_fusion.5), channel_id=1, source_target_pairs={{0,2},{1,3},{2,0},{3,1},{4,6},{5,7},{6,4},{7,5},{8,10},{9,11},{10,... | collective-permute-start | bytes 786440 | tf_op jit(solution)/shard_map/ppermute | solution.py:589
  35.8 2.8 %prepare.1 = (bf16[512,2048]{1,0:T(8,128)(2,1)S(1)}, s32[24]{0:T(128)S(1)}) custom-call(s32[26]{0:T(128)S(1)} %concatenate.3.where_ref, f32[1,128]{1,0:T(1,128)S(1)} %bitcast.29, bf16[512,2048]{1,0:T(8,128)(2,1)S(1)} %copy-done), custom_call_target="tpu_custom_call" | custom-call | flops 1024 | bytes 1024 | tf_op jit(solution)/shard_map/prepare/pallas_call | solution.py:269
  38.6 3.2 %collective-permute-done.9.refs_1_ = bf16[512,256]{1,0:T(8,128)(2,1)S(1)} collective-permute-done((bf16[512,256]{1,0:T(8,128)(2,1)S(1)}, bf16[512,256]{1,0:T(8,128)(2,1)S(1)}, u32[]{:S(2)}, u32[]{:S(2)}) %collective-permute-start.9) | collective-permute-done | bytes 262176 | tf_op jit(solution)/shard_map/ppermute | solution.py:589
  41.8 1.7 %collective-permute-start.10 = (bf16[512,256]{1,0:T(8,128)(2,1)S(1)}, bf16[512,256]{1,0:T(8,128)(2,1)S(1)}, u32[]{:S(2)}, u32[]{:S(2)}) collective-permute-start(bf16[512,256]{1,0:T(8,128)(2,1)S(1)} %add_convert_fusion.3), channel_id=1, source_target_pairs={{0,2},{1,3},{2,0},{3,1},{4,6},{5,7},{6,4},{7,5},{8,10},{9,11},{10,... | collective-permute-start | bytes 786440 | tf_op jit(solution)/shard_map/ppermute | solution.py:589
  44.4 2.7 %collective-permute-start.16 = (bf16[2,128,256]{2,1,0:T(8,128)(2,1)S(1)}, bf16[2,128,256]{2,1,0:T(8,128)(2,1)S(1)}, u32[]{:S(2)}, u32[]{:S(2)}) collective-permute-start(bf16[2,128,256]{2,1,0:T(8,128)(2,1)S(1)} %get-tuple-element.65), channel_id=1, source_target_pairs={{0,8},{4,12},{8,0},{12,4},{1,9},{5,13},{9,1},{13,5},{2,10},{6,14},... | collective-permute-start | bytes 393224 | tf_op jit(solution)/shard_map/ppermute | solution.py:700
  47.0 1.4 %collective-permute-start.17 = (bf16[1,128,256]{2,1,0:T(8,128)(2,1)S(1)}, bf16[1,128,256]{2,1,0:T(8,128)(2,1)S(1)}, u32[]{:S(2)}, u32[]{:S(2)}) collective-permute-start(bf16[1,128,256]{2,1,0:T(8,128)(2,1)S(1)} %get-tuple-element.66), channel_id=1, source_target_pairs={{0,12},{4,8},{8,4},{12,0},{1,13},{5,9},{9,5},{13,1},{2,14},{6,10},... | collective-permute-start | bytes 196616 | tf_op jit(solution)/shard_map/ppermute | solution.py:700
  50.1 2.9 %collective-permute-start.12 = (bf16[2,128,256]{2,1,0:T(8,128)(2,1)S(1)}, bf16[2,128,256]{2,1,0:T(8,128)(2,1)S(1)}, u32[]{:S(2)}, u32[]{:S(2)}) collective-permute-start(bf16[2,128,256]{2,1,0:T(8,128)(2,1)S(1)} %get-tuple-element.59), channel_id=1, source_target_pairs={{0,8},{4,12},{8,0},{12,4},{1,9},{5,13},{9,1},{13,5},{2,10},{6,14},... | collective-permute-start | bytes 393224 | tf_op jit(solution)/shard_map/ppermute | solution.py:700
  53.0 3.0 %collective-permute-done.16.refs_2_ = bf16[2,128,256]{2,1,0:T(8,128)(2,1)S(1)} collective-permute-done((bf16[2,128,256]{2,1,0:T(8,128)(2,1)S(1)}, bf16[2,128,256]{2,1,0:T(8,128)(2,1)S(1)}, u32[]{:S(2)}, u32[]{:S(2)}) %collective-permute-start.16) | collective-permute-done | bytes 131104 | tf_op jit(solution)/shard_map/ppermute | solution.py:700
  56.0 4.0 %collective-permute-start.18 = (bf16[1,128,256]{2,1,0:T(8,128)(2,1)S(1)}, bf16[1,128,256]{2,1,0:T(8,128)(2,1)S(1)}, u32[]{:S(2)}, u32[]{:S(2)}) collective-permute-start(bf16[1,128,256]{2,1,0:T(8,128)(2,1)S(1)} %slice.9), channel_id=1, source_target_pairs={{0,4},{4,0},{8,12},{12,8},{1,5},{5,1},{9,13},{13,9},{2,6},{6,2},{1... | collective-permute-start | bytes 196616 | tf_op jit(solution)/shard_map/ppermute | solution.py:700
  60.0 2.4 %collective-permute-start.13 = (bf16[1,128,256]{2,1,0:T(8,128)(2,1)S(1)}, bf16[1,128,256]{2,1,0:T(8,128)(2,1)S(1)}, u32[]{:S(2)}, u32[]{:S(2)}) collective-permute-start(bf16[1,128,256]{2,1,0:T(8,128)(2,1)S(1)} %get-tuple-element.60), channel_id=1, source_target_pairs={{0,12},{4,8},{8,4},{12,0},{1,13},{5,9},{9,5},{13,1},{2,14},{6,10},... | collective-permute-start | bytes 196616 | tf_op jit(solution)/shard_map/ppermute | solution.py:700
  62.4 3.7 %attend_head.2.refs_5_ = bf16[512,2048]{1,0:T(8,128)(2,1)} custom-call(s32[24]{0:T(128)S(1)} %get-tuple-element.50.meta_ref, bf16[512,2048]{1,0:T(8,128)(2,1)S(1)} %get-tuple-element.51.query_ref, bf16[2,128,256]{2,1,0:T(8,128)(2,1)S(1)} %get-tuple-element.63.refs_0_, bf16[2,128,256]{2,1,0:T(8,128)(2,1)S(1)} %collective-permute-done.15.refs_1_, ...), custom_call_target="tpu_custom_call" | custom-call | flops 1024 | bytes 1024 | tf_op jit(solution)/shard_map/attend_head/pallas_call | solution.py:552
  66.8 1.5 %collective-permute-start.19 = (bf16[1,128,256]{2,1,0:T(8,128)(2,1)S(1)}, bf16[1,128,256]{2,1,0:T(8,128)(2,1)S(1)}, u32[]{:S(2)}, u32[]{:S(2)}) collective-permute-start(bf16[1,128,256]{2,1,0:T(8,128)(2,1)S(1)} %slice.8), channel_id=1, source_target_pairs={{0,4},{4,0},{8,12},{12,8},{1,5},{5,1},{9,13},{13,9},{2,6},{6,2},{1... | collective-permute-start | bytes 196616 | tf_op jit(solution)/shard_map/ppermute | solution.py:700
  68.2 2.8 %collective-permute-done.19.refs_4_ = bf16[1,128,256]{2,1,0:T(8,128)(2,1)S(1)} collective-permute-done((bf16[1,128,256]{2,1,0:T(8,128)(2,1)S(1)}, bf16[1,128,256]{2,1,0:T(8,128)(2,1)S(1)}, u32[]{:S(2)}, u32[]{:S(2)}) %collective-permute-start.19) | collective-permute-done | bytes 65568 | tf_op jit(solution)/shard_map/ppermute | solution.py:700
  71.1 3.9 %attend_head.3 = bf16[512,2048]{1,0:T(8,128)(2,1)} custom-call(s32[24]{0:T(128)S(1)} %get-tuple-element.50.meta_ref, bf16[512,2048]{1,0:T(8,128)(2,1)S(1)} %get-tuple-element.51.query_ref, bf16[2,128,256]{2,1,0:T(8,128)(2,1)S(1)} %get-tuple-element.57.refs_0_, ...), custom_call_target="tpu_custom_call", output_to_operand_aliasing={{}: (7, {})} | custom-call | flops 1024 | bytes 1024 | tf_op jit(solution)/shard_map/attend_head/pallas_call | solution.py:552
  (55 shorter events, 7.8 us)
Async XLA Ops:
  0.0 10.9 %collective-permute-start.1 = (bf16[4,320,128]{2,1,0:T(8,128)(2,1)}, bf16[4,320,128]{2,1,0:T(8,128)(2,1)S(1)}, u32[]{:S(2)}, u32[]{:S(2)}) collective-permute-start(bf16[4,320,128]{2,1,0:T(8,128)(2,1)} %bitcast.20), channel_id=1, source_target_pairs={{0,2},{1,3},{2,0},{3,1},{4,6},{5,7},{6,4},{7,5},{8,10},{9,11},{10,... | collective-permute-start | bytes 983048 | tf_op jit(solution)/shard_map/ppermute | solution.py:602
  3.0 7.9 %collective-permute-start = (bf16[4,320,128]{2,1,0:T(8,128)(2,1)}, bf16[4,320,128]{2,1,0:T(8,128)(2,1)S(1)}, u32[]{:S(2)}, u32[]{:S(2)}) collective-permute-start(bf16[4,320,128]{2,1,0:T(8,128)(2,1)} %bitcast.21), channel_id=1, source_target_pairs={{0,1},{1,0},{2,3},{3,2},{4,5},{5,4},{6,7},{7,6},{8,9},{9,8},{10,11... | collective-permute-start | bytes 983048 | tf_op jit(solution)/shard_map/ppermute | solution.py:647
  10.9 1.6 %collective-permute-start.2 = (bf16[4,320,128]{2,1,0:T(8,128)(2,1)S(1)}, bf16[4,320,128]{2,1,0:T(8,128)(2,1)S(1)}, u32[]{:S(2)}, u32[]{:S(2)}) collective-permute-start(bf16[4,320,128]{2,1,0:T(8,128)(2,1)S(1)} %collective-permute-done.1.refs_2_), channel_id=1, source_target_pairs={{0,1},{1,0},{2,3},{3,2},{4,5},{5,4},{6,7},{7,6},{8,9},{9,8},{10,11... | collective-permute-start | bytes 983048 | tf_op jit(solution)/shard_map/ppermute | solution.py:606
  12.5 9.3 %copy-start.9 = (f32[320]{0:T(512)S(1)}, f32[320]{0:T(512)}, u32[]{:S(2)}) copy-start(f32[320]{0:T(512)} %param.23) | copy-start | bytes 3844
  18.2 1.7 %collective-permute-start.3 = (bf16[640,256]{1,0:T(8,128)(2,1)S(1)}, bf16[640,256]{1,0:T(8,128)(2,1)S(1)}, u32[]{:S(2)}, u32[]{:S(2)}) collective-permute-start(bf16[640,256]{1,0:T(8,128)(2,1)S(1)} %get-tuple-element.42), channel_id=1, source_target_pairs={{0,1},{1,0},{2,3},{3,2},{4,5},{5,4},{6,7},{7,6},{8,9},{9,8},{10,11... | collective-permute-start | bytes 983048 | tf_op jit(solution)/shard_map/ppermute | solution.py:589
  18.4 8.7 %collective-permute-start.4 = (bf16[640,256]{1,0:T(8,128)(2,1)S(1)}, bf16[640,256]{1,0:T(8,128)(2,1)S(1)}, u32[]{:S(2)}, u32[]{:S(2)}) collective-permute-start(bf16[640,256]{1,0:T(8,128)(2,1)S(1)} %get-tuple-element.46), channel_id=1, source_target_pairs={{0,1},{1,0},{2,3},{3,2},{4,5},{5,4},{6,7},{7,6},{8,9},{9,8},{10,11... | collective-permute-start | bytes 983048 | tf_op jit(solution)/shard_map/ppermute | solution.py:589
  20.0 9.8 %collective-permute-start.5 = (bf16[640,256]{1,0:T(8,128)(2,1)S(1)}, bf16[640,256]{1,0:T(8,128)(2,1)S(1)}, u32[]{:S(2)}, u32[]{:S(2)}) collective-permute-start(bf16[640,256]{1,0:T(8,128)(2,1)S(1)} %add_convert_fusion.1), channel_id=1, source_target_pairs={{0,2},{1,3},{2,0},{3,1},{4,6},{5,7},{6,4},{7,5},{8,10},{9,11},{10,... | collective-permute-start | bytes 983048 | tf_op jit(solution)/shard_map/ppermute | solution.py:589
  27.2 8.6 %copy-start = (bf16[512,2048]{1,0:T(8,128)(2,1)S(1)}, bf16[512,2048]{1,0:T(8,128)(2,1)}, u32[]{:S(2)}) copy-start(bf16[512,2048]{1,0:T(8,128)(2,1)} %query_ref.1) | copy-start | bytes 6291460
  27.2 8.6 %copy-start.8 = (f32[128]{0:T(128)S(1)}, f32[128]{0:T(128)}, u32[]{:S(2)}) copy-start(f32[128]{0:T(128)} %param.27) | copy-start | bytes 1540
  31.7 1.6 %collective-permute-start.6 = (bf16[512,256]{1,0:T(8,128)(2,1)S(1)}, bf16[512,256]{1,0:T(8,128)(2,1)S(1)}, u32[]{:S(2)}, u32[]{:S(2)}) collective-permute-start(bf16[512,256]{1,0:T(8,128)(2,1)S(1)} %get-tuple-element.48), channel_id=1, source_target_pairs={{0,1},{1,0},{2,3},{3,2},{4,5},{5,4},{6,7},{7,6},{8,9},{9,8},{10,11... | collective-permute-start | bytes 786440 | tf_op jit(solution)/shard_map/ppermute | solution.py:589
  31.7 3.9 %collective-permute-start.8 = (bf16[512,256]{1,0:T(8,128)(2,1)S(1)}, bf16[512,256]{1,0:T(8,128)(2,1)S(1)}, u32[]{:S(2)}, u32[]{:S(2)}) collective-permute-start(bf16[512,256]{1,0:T(8,128)(2,1)S(1)} %get-tuple-element.55), channel_id=1, source_target_pairs={{0,1},{1,0},{2,3},{3,2},{4,5},{5,4},{6,7},{7,6},{8,9},{9,8},{10,11... | collective-permute-start | bytes 786440 | tf_op jit(solution)/shard_map/ppermute | solution.py:589
  33.3 10.3 %copy-start.7 = (f32[128]{0:T(128)S(1)}, f32[128]{0:T(128)}, u32[]{:S(2)}) copy-start(f32[128]{0:T(128)} %param.26) | copy-start | bytes 1540
  33.4 8.4 %collective-permute-start.9 = (bf16[512,256]{1,0:T(8,128)(2,1)S(1)}, bf16[512,256]{1,0:T(8,128)(2,1)S(1)}, u32[]{:S(2)}, u32[]{:S(2)}) collective-permute-start(bf16[512,256]{1,0:T(8,128)(2,1)S(1)} %add_convert_fusion.5), channel_id=1, source_target_pairs={{0,2},{1,3},{2,0},{3,1},{4,6},{5,7},{6,4},{7,5},{8,10},{9,11},{10,... | collective-permute-start | bytes 786440 | tf_op jit(solution)/shard_map/ppermute | solution.py:589
  35.2 8.4 %collective-permute-start.14 = (bf16[512,256]{1,0:T(8,128)(2,1)S(1)}, bf16[512,256]{1,0:T(8,128)(2,1)S(1)}, u32[]{:S(2)}, u32[]{:S(2)}) collective-permute-start(bf16[512,256]{1,0:T(8,128)(2,1)S(1)} %get-tuple-element.62), channel_id=1, source_target_pairs={{0,1},{1,0},{2,3},{3,2},{4,5},{5,4},{6,7},{7,6},{8,9},{9,8},{10,11... | collective-permute-start | bytes 786440 | tf_op jit(solution)/shard_map/ppermute | solution.py:589
  35.2 13.5 %collective-permute-start.7 = (bf16[512,256]{1,0:T(8,128)(2,1)S(1)}, bf16[512,256]{1,0:T(8,128)(2,1)S(1)}, u32[]{:S(2)}, u32[]{:S(2)}) collective-permute-start(bf16[512,256]{1,0:T(8,128)(2,1)S(1)} %get-tuple-element.53), channel_id=1, source_target_pairs={{0,1},{1,0},{2,3},{3,2},{4,5},{5,4},{6,7},{7,6},{8,9},{9,8},{10,11... | collective-permute-start | bytes 786440 | tf_op jit(solution)/shard_map/ppermute | solution.py:589
  41.8 7.5 %collective-permute-start.10 = (bf16[512,256]{1,0:T(8,128)(2,1)S(1)}, bf16[512,256]{1,0:T(8,128)(2,1)S(1)}, u32[]{:S(2)}, u32[]{:S(2)}) collective-permute-start(bf16[512,256]{1,0:T(8,128)(2,1)S(1)} %add_convert_fusion.3), channel_id=1, source_target_pairs={{0,2},{1,3},{2,0},{3,1},{4,6},{5,7},{6,4},{7,5},{8,10},{9,11},{10,... | collective-permute-start | bytes 786440 | tf_op jit(solution)/shard_map/ppermute | solution.py:589
  44.4 11.6 %collective-permute-start.16 = (bf16[2,128,256]{2,1,0:T(8,128)(2,1)S(1)}, bf16[2,128,256]{2,1,0:T(8,128)(2,1)S(1)}, u32[]{:S(2)}, u32[]{:S(2)}) collective-permute-start(bf16[2,128,256]{2,1,0:T(8,128)(2,1)S(1)} %get-tuple-element.65), channel_id=1, source_target_pairs={{0,8},{4,12},{8,0},{12,4},{1,9},{5,13},{9,1},{13,5},{2,10},{6,14},... | collective-permute-start | bytes 393224 | tf_op jit(solution)/shard_map/ppermute | solution.py:700
  47.0 8.9 %collective-permute-start.17 = (bf16[1,128,256]{2,1,0:T(8,128)(2,1)S(1)}, bf16[1,128,256]{2,1,0:T(8,128)(2,1)S(1)}, u32[]{:S(2)}, u32[]{:S(2)}) collective-permute-start(bf16[1,128,256]{2,1,0:T(8,128)(2,1)S(1)} %get-tuple-element.66), channel_id=1, source_target_pairs={{0,12},{4,8},{8,4},{12,0},{1,13},{5,9},{9,5},{13,1},{2,14},{6,10},... | collective-permute-start | bytes 196616 | tf_op jit(solution)/shard_map/ppermute | solution.py:700
  48.4 14.0 %collective-permute-start.15 = (bf16[2,128,256]{2,1,0:T(8,128)(2,1)S(1)}, bf16[2,128,256]{2,1,0:T(8,128)(2,1)S(1)}, u32[]{:S(2)}, u32[]{:S(2)}) collective-permute-start(bf16[2,128,256]{2,1,0:T(8,128)(2,1)S(1)} %get-tuple-element.64), channel_id=1, source_target_pairs={{0,4},{4,0},{8,12},{12,8},{1,5},{5,1},{9,13},{13,9},{2,6},{6,2},{1... | collective-permute-start | bytes 393224 | tf_op jit(solution)/shard_map/ppermute | solution.py:700
  50.1 16.1 %collective-permute-start.12 = (bf16[2,128,256]{2,1,0:T(8,128)(2,1)S(1)}, bf16[2,128,256]{2,1,0:T(8,128)(2,1)S(1)}, u32[]{:S(2)}, u32[]{:S(2)}) collective-permute-start(bf16[2,128,256]{2,1,0:T(8,128)(2,1)S(1)} %get-tuple-element.59), channel_id=1, source_target_pairs={{0,8},{4,12},{8,0},{12,4},{1,9},{5,13},{9,1},{13,5},{2,10},{6,14},... | collective-permute-start | bytes 393224 | tf_op jit(solution)/shard_map/ppermute | solution.py:700
  56.0 6.5 %collective-permute-start.18 = (bf16[1,128,256]{2,1,0:T(8,128)(2,1)S(1)}, bf16[1,128,256]{2,1,0:T(8,128)(2,1)S(1)}, u32[]{:S(2)}, u32[]{:S(2)}) collective-permute-start(bf16[1,128,256]{2,1,0:T(8,128)(2,1)S(1)} %slice.9), channel_id=1, source_target_pairs={{0,4},{4,0},{8,12},{12,8},{1,5},{5,1},{9,13},{13,9},{2,6},{6,2},{1... | collective-permute-start | bytes 196616 | tf_op jit(solution)/shard_map/ppermute | solution.py:700
  60.0 6.8 %collective-permute-start.13 = (bf16[1,128,256]{2,1,0:T(8,128)(2,1)S(1)}, bf16[1,128,256]{2,1,0:T(8,128)(2,1)S(1)}, u32[]{:S(2)}, u32[]{:S(2)}) collective-permute-start(bf16[1,128,256]{2,1,0:T(8,128)(2,1)S(1)} %get-tuple-element.60), channel_id=1, source_target_pairs={{0,12},{4,8},{8,4},{12,0},{1,13},{5,9},{9,5},{13,1},{2,14},{6,10},... | collective-permute-start | bytes 196616 | tf_op jit(solution)/shard_map/ppermute | solution.py:700
  62.4 5.9 %collective-permute-start.11 = (bf16[2,128,256]{2,1,0:T(8,128)(2,1)S(1)}, bf16[2,128,256]{2,1,0:T(8,128)(2,1)S(1)}, u32[]{:S(2)}, u32[]{:S(2)}) collective-permute-start(bf16[2,128,256]{2,1,0:T(8,128)(2,1)S(1)} %get-tuple-element.58), channel_id=1, source_target_pairs={{0,4},{4,0},{8,12},{12,8},{1,5},{5,1},{9,13},{13,9},{2,6},{6,2},{1... | collective-permute-start | bytes 393224 | tf_op jit(solution)/shard_map/ppermute | solution.py:700
  66.8 4.3 %collective-permute-start.19 = (bf16[1,128,256]{2,1,0:T(8,128)(2,1)S(1)}, bf16[1,128,256]{2,1,0:T(8,128)(2,1)S(1)}, u32[]{:S(2)}, u32[]{:S(2)}) collective-permute-start(bf16[1,128,256]{2,1,0:T(8,128)(2,1)S(1)} %slice.8), channel_id=1, source_target_pairs={{0,4},{4,0},{8,12},{12,8},{1,5},{5,1},{9,13},{13,9},{2,6},{6,2},{1... | collective-permute-start | bytes 196616 | tf_op jit(solution)/shard_map/ppermute | solution.py:700
  (6 other events, 38.8 us)

commit v2 on v1

--- a/solution.py
+++ b/solution.py
@@ -703,12 +703,11 @@
         terms = kv_terms[head]
         if one_large:
             star = place["star"]
-            picks = ((send, star), (send + 1, star), (send + 2, star), (send + 3,))
-            own, near, middle, far = finish_tiles(meta, k_gain, terms, picks)
-            middle_got, far_got, near_got = move(middle, 2), move(far, 3), move(near, 1)
-            passed = move(after(middle_got[1:], far_got, out), 1)
-            tiles = (own, near_got, middle_got, far_got, passed)
-            sources = ((0, 4), (1, 5), (2, 6), (3,), (7,))
+            picks = tuple((send + d, star) for d in range(group_count))
+            made = finish_tiles(meta, k_gain, terms, picks)
+            moved = {d: move(made[d], d) for d in (2, 3, 1)}
+            tiles = (made[0],) + tuple(moved[d] for d in (1, 2, 3))
+            sources = tuple((d, group_count + d) for d in range(group_count))
         else:
             picks = tuple(
                 tuple(send + s * group_count + d for s in range(slots)) for d in range(group_count)

time: 75.7 us -> 74.5 us (0.984)
  starting transfers between devices: 24.9 us -> 18.9 us
  waiting for transfers between devices: 17.4 us -> 21.2 us
  Pallas kernels: 29.7 us -> 31.1 us
    ppermute x8 -> x6, starting transfers between devices: 15 us -> 8.98 us  [move(): return lax.ppermute(value, 'grp', xor_pairs(group_count, mask))]
    ppermute x8 -> x6, waiting for transfers between devices: 6.5 us -> 10.6 us  [move(): return lax.ppermute(value, 'grp', xor_pairs(group_count, mask))]
    pallas_call x2, Pallas kernels: 7.62 us -> 9 us  [attend_head(): pl.pallas_call(functools.partial(attend_kernel, group_count, sources, hea...]
  transfers between devices with their start and end apart: 20 -> 18, of which waited for: 11 -> 9; matrix products, arithmetic and copies ran while one was open for 2% -> 2% of each run, Pallas kernels for 24% -> 26%
where the time goes in v2:
time: 74.5 us; the launch traced here: 74.3 us
  Pallas kernels  31.1 us (42%)
  waiting for transfers between devices  21.2 us (28%)
  starting transfers between devices  18.9 us (25%)
  local copies, waits for them, and re-layouts  2.24 us (3%)
    ppermute x6, waiting for transfers between devices, move(): return lax.ppermute(value, 'grp', xor_pairs(group_count, mask))  10.6 us
    pallas_call x2, Pallas kernels, tap_projection(): pl.pallas_call(functools.partial(tap_kernel, blocks, head_count, dup, len...  10.2 us
    pallas_call x2, Pallas kernels, attend_head(): pl.pallas_call(functools.partial(attend_kernel, group_count, sources, hea...  9 us
    ppermute x6, starting transfers between devices, move(): return lax.ppermute(value, 'grp', xor_pairs(group_count, mask))  8.98 us
    ppermute x9, waiting for transfers between devices, scatter_sum(): got[k ^ 1 << b] = lax.ppermute(sent, 'tp', pairs)  8.23 us
    ppermute x9, starting transfers between devices, scatter_sum(): got[k ^ 1 << b] = lax.ppermute(sent, 'tp', pairs)  6.99 us
    pallas_call x1, Pallas kernels, encoder_mlp(): pl.pallas_call(functools.partial(mlp_kernel, count, bases, tiles), out_sh...  5.66 us
    ppermute x1, starting transfers between devices, gather_half(): pieces[k | 1 << b] = lax.ppermute(pieces[k], 'tp', pairs)  2.97 us
  transfers between devices with their start and end apart: 18, of which 9 were waited for; matrix products, arithmetic and copies ran while one was open for 2% of the time, Pallas kernels for 26%

profile of v2, /device:TPU:0, one launch (start us, length us, event | category | flops | bytes accessed | tf_op | source)
XLA Modules:
  0.0 74.3 jit_solution(1617237148114717229)
XLA Ops:
  0.0 3.0 %collective-permute-start.1 = (bf16[4,320,128]{2,1,0:T(8,128)(2,1)}, bf16[4,320,128]{2,1,0:T(8,128)(2,1)S(1)}, u32[]{:S(2)}, u32[]{:S(2)}) collective-permute-start(bf16[4,320,128]{2,1,0:T(8,128)(2,1)} %bitcast.20), channel_id=1, source_target_pairs={{0,2},{1,3},{2,0},{3,1},{4,6},{5,7},{6,4},{7,5},{8,10},{9,11},{10,... | collective-permute-start | bytes 983048 | tf_op jit(solution)/shard_map/ppermute | solution.py:602
  3.7 1.4 %copy-done.1 = bf16[4,1,128,1600]{2,3,1,0:T(8,128)(2,1)S(1)} copy-done((bf16[4,1,128,1600]{2,3,1,0:T(8,128)(2,1)S(1)}, bf16[4,1,128,1600]{2,3,1,0:T(8,128)(2,1)}, u32[]{:S(2)}) %copy-start.1) | copy-done | bytes 1638424
  5.2 4.9 %tap_projection.2 = (bf16[3,512,256]{2,1,0:T(8,128)(2,1)S(1)}, bf16[1280,1280]{1,0:T(8,128)(2,1)S(1)}, bf16[1280,1280]{1,0:T(8,128)(2,1)S(1)}, bf16[4,1600,128]{2,1,0:T(8,128)(2,1)S(1)}) custom-call(s32[26]{0:T(128)S(1)} %concatenate.3.where_ref, bf16[4,1600,128]{2,1,0:T(8,128)(2,1)S(1)} %bitcast.19, bf16[1600,2048]{1,0:T(8,128)(2,1)} %weight_hbm.3, ...), custom_call_target="tpu_custom_call" | custom-call | flops 1024 | bytes 1024 | tf_op jit(solution)/shard_map/tap_projection/pallas_call | solution.py:335
  10.9 1.6 %collective-permute-done.2.refs_3_ = bf16[4,320,128]{2,1,0:T(8,128)(2,1)S(1)} collective-permute-done((bf16[4,320,128]{2,1,0:T(8,128)(2,1)S(1)}, bf16[4,320,128]{2,1,0:T(8,128)(2,1)S(1)}, u32[]{:S(2)}, u32[]{:S(2)}) %collective-permute-start.2) | collective-permute-done | bytes 327712 | tf_op jit(solution)/shard_map/ppermute | solution.py:606
  12.5 5.7 %encoder_mlp.1 = (bf16[640,256]{1,0:T(8,128)(2,1)S(1)}, bf16[640,256]{1,0:T(8,128)(2,1)S(1)}, bf16[640,256]{1,0:T(8,128)(2,1)S(1)}, bf16[640,256]{1,0:T(8,128)(2,1)S(1)}) custom-call(s32[26]{0:T(128)S(1)} %concatenate.3.where_ref, bf16[4,320,128]{2,1,0:T(8,128)(2,1)S(1)} %bitcast.22, bf16[4,320,128]{2,1,0:T(8,128)(2,1)S(1)} %collective-permute-done.refs_1_, ...), custom_call_target="tpu_custom_call" | custom-call | flops 1024 | bytes 1024 | tf_op jit(solution)/shard_map/encoder_mlp/pallas_call | solution.py:221
  18.8 1.1 %collective-permute-done.3 = bf16[640,256]{1,0:T(8,128)(2,1)S(1)} collective-permute-done((bf16[640,256]{1,0:T(8,128)(2,1)S(1)}, bf16[640,256]{1,0:T(8,128)(2,1)S(1)}, u32[]{:S(2)}, u32[]{:S(2)}) %collective-permute-start.3) | collective-permute-done | bytes 327712 | tf_op jit(solution)/shard_map/ppermute | solution.py:589
  20.0 1.8 %collective-permute-start.5 = (bf16[640,256]{1,0:T(8,128)(2,1)S(1)}, bf16[640,256]{1,0:T(8,128)(2,1)S(1)}, u32[]{:S(2)}, u32[]{:S(2)}) collective-permute-start(bf16[640,256]{1,0:T(8,128)(2,1)S(1)} %add_convert_fusion.1), channel_id=1, source_target_pairs={{0,2},{1,3},{2,0},{3,1},{4,6},{5,7},{6,4},{7,5},{8,10},{9,11},{10,... | collective-permute-start | bytes 983048 | tf_op jit(solution)/shard_map/ppermute | solution.py:589
  21.8 5.3 %tap_projection.3.refs_4_ = bf16[5,512,256]{2,1,0:T(8,128)(2,1)S(1)} custom-call(s32[26]{0:T(128)S(1)} %concatenate.3.where_ref, bf16[4,1600,128]{2,1,0:T(8,128)(2,1)S(1)} %get-tuple-element.42.tap_hbm, bf16[1600,2048]{1,0:T(8,128)(2,1)} %weight_hbm.3), custom_call_target="tpu_custom_call" | custom-call | flops 1024 | bytes 1024 | tf_op jit(solution)/shard_map/tap_projection/pallas_call | solution.py:335
  27.2 2.6 %collective-permute-done.5.refs_6_ = bf16[640,256]{1,0:T(8,128)(2,1)S(1)} collective-permute-done((bf16[640,256]{1,0:T(8,128)(2,1)S(1)}, bf16[640,256]{1,0:T(8,128)(2,1)S(1)}, u32[]{:S(2)}, u32[]{:S(2)}) %collective-permute-start.5) | collective-permute-done | bytes 327712 | tf_op jit(solution)/shard_map/ppermute | solution.py:589
  29.8 1.9 %kv_projection.1 = (bf16[512,256]{1,0:T(8,128)(2,1)S(1)}, bf16[512,256]{1,0:T(8,128)(2,1)S(1)}, bf16[512,256]{1,0:T(8,128)(2,1)S(1)}, bf16[512,256]{1,0:T(8,128)...) custom-call(s32[26]{0:T(128)S(1)} %concatenate.3.where_ref, ...), custom_call_target="tpu_custom_call" | custom-call | flops 1024 | bytes 1024 | tf_op jit(solution)/shard_map/kv_projection/pallas_call | solution.py:401
  32.2 1.0 %collective-permute-done.6 = bf16[512,256]{1,0:T(8,128)(2,1)S(1)} collective-permute-done((bf16[512,256]{1,0:T(8,128)(2,1)S(1)}, bf16[512,256]{1,0:T(8,128)(2,1)S(1)}, u32[]{:S(2)}, u32[]{:S(2)}) %collective-permute-start.6) | collective-permute-done | bytes 262176 | tf_op jit(solution)/shard_map/ppermute | solution.py:589
  33.4 1.8 %collective-permute-start.9 = (bf16[512,256]{1,0:T(8,128)(2,1)S(1)}, bf16[512,256]{1,0:T(8,128)(2,1)S(1)}, u32[]{:S(2)}, u32[]{:S(2)}) collective-permute-start(bf16[512,256]{1,0:T(8,128)(2,1)S(1)} %add_convert_fusion.5), channel_id=1, source_target_pairs={{0,2},{1,3},{2,0},{3,1},{4,6},{5,7},{6,4},{7,5},{8,10},{9,11},{10,... | collective-permute-start | bytes 786440 | tf_op jit(solution)/shard_map/ppermute | solution.py:589
  35.8 2.8 %prepare.1 = (bf16[512,2048]{1,0:T(8,128)(2,1)S(1)}, s32[24]{0:T(128)S(1)}) custom-call(s32[26]{0:T(128)S(1)} %concatenate.3.where_ref, f32[1,128]{1,0:T(1,128)S(1)} %bitcast.29, bf16[512,2048]{1,0:T(8,128)(2,1)S(1)} %copy-done), custom_call_target="tpu_custom_call" | custom-call | flops 1024 | bytes 1024 | tf_op jit(solution)/shard_map/prepare/pallas_call | solution.py:269
  38.6 3.2 %collective-permute-done.9.refs_1_ = bf16[512,256]{1,0:T(8,128)(2,1)S(1)} collective-permute-done((bf16[512,256]{1,0:T(8,128)(2,1)S(1)}, bf16[512,256]{1,0:T(8,128)(2,1)S(1)}, u32[]{:S(2)}, u32[]{:S(2)}) %collective-permute-start.9) | collective-permute-done | bytes 262176 | tf_op jit(solution)/shard_map/ppermute | solution.py:589
  41.8 1.7 %collective-permute-start.10 = (bf16[512,256]{1,0:T(8,128)(2,1)S(1)}, bf16[512,256]{1,0:T(8,128)(2,1)S(1)}, u32[]{:S(2)}, u32[]{:S(2)}) collective-permute-start(bf16[512,256]{1,0:T(8,128)(2,1)S(1)} %add_convert_fusion.3), channel_id=1, source_target_pairs={{0,2},{1,3},{2,0},{3,1},{4,6},{5,7},{6,4},{7,5},{8,10},{9,11},{10,... | collective-permute-start | bytes 786440 | tf_op jit(solution)/shard_map/ppermute | solution.py:589
  43.6 0.8 %finish_tiles.3 = (bf16[2,128,256]{2,1,0:T(8,128)(2,1)S(1)}, bf16[2,128,256]{2,1,0:T(8,128)(2,1)S(1)}, bf16[2,128,256]{2,1,0:T(8,128)(2,1)S(1)}, bf16[2,128,256]{2,1,0:T(8,128)(2,1)S(1)}) custom-call(s32[24]{0:T(128)S(1)} %get-tuple-element.48.meta_ref, f32[1,128]{1,0:T(1,128)S(1)} %bitcast.27, bf16[512,256]{1,0:T(8,128)(2,1)S(1)} %add_convert_fusion.2.refs_0_, ...), custom_call_target="tpu_custom_call" | custom-call | flops 1024 | bytes 1024 | tf_op jit(solution)/shard_map/finish_tiles/pallas_call | solution.py:444
  44.4 1.7 %collective-permute-start.15 = (bf16[2,128,256]{2,1,0:T(8,128)(2,1)S(1)}, bf16[2,128,256]{2,1,0:T(8,128)(2,1)S(1)}, u32[]{:S(2)}, u32[]{:S(2)}) collective-permute-start(bf16[2,128,256]{2,1,0:T(8,128)(2,1)S(1)} %get-tuple-element.62), channel_id=1, source_target_pairs={{0,4},{4,0},{8,12},{12,8},{1,5},{5,1},{9,13},{13,9},{2,6},{6,2},{1... | collective-permute-start | bytes 393224 | tf_op jit(solution)/shard_map/ppermute | solution.py:700
  46.1 2.7 %collective-permute-start.16 = (bf16[2,128,256]{2,1,0:T(8,128)(2,1)S(1)}, bf16[2,128,256]{2,1,0:T(8,128)(2,1)S(1)}, u32[]{:S(2)}, u32[]{:S(2)}) collective-permute-start(bf16[2,128,256]{2,1,0:T(8,128)(2,1)S(1)} %get-tuple-element.63), channel_id=1, source_target_pairs={{0,8},{4,12},{8,0},{12,4},{1,9},{5,13},{9,1},{13,5},{2,10},{6,14},... | collective-permute-start | bytes 393224 | tf_op jit(solution)/shard_map/ppermute | solution.py:700
  50.1 1.9 %collective-permute-start.11 = (bf16[2,128,256]{2,1,0:T(8,128)(2,1)S(1)}, bf16[2,128,256]{2,1,0:T(8,128)(2,1)S(1)}, u32[]{:S(2)}, u32[]{:S(2)}) collective-permute-start(bf16[2,128,256]{2,1,0:T(8,128)(2,1)S(1)} %get-tuple-element.56), channel_id=1, source_target_pairs={{0,4},{4,0},{8,12},{12,8},{1,5},{5,1},{9,13},{13,9},{2,6},{6,2},{1... | collective-permute-start | bytes 393224 | tf_op jit(solution)/shard_map/ppermute | solution.py:700
  51.9 2.6 %collective-permute-start.12 = (bf16[2,128,256]{2,1,0:T(8,128)(2,1)S(1)}, bf16[2,128,256]{2,1,0:T(8,128)(2,1)S(1)}, u32[]{:S(2)}, u32[]{:S(2)}) collective-permute-start(bf16[2,128,256]{2,1,0:T(8,128)(2,1)S(1)} %get-tuple-element.57), channel_id=1, source_target_pairs={{0,8},{4,12},{8,0},{12,4},{1,9},{5,13},{9,1},{13,5},{2,10},{6,14},... | collective-permute-start | bytes 393224 | tf_op jit(solution)/shard_map/ppermute | solution.py:700
  54.5 4.7 %collective-permute-done.16.refs_2_ = bf16[2,128,256]{2,1,0:T(8,128)(2,1)S(1)} collective-permute-done((bf16[2,128,256]{2,1,0:T(8,128)(2,1)S(1)}, bf16[2,128,256]{2,1,0:T(8,128)(2,1)S(1)}, u32[]{:S(2)}, u32[]{:S(2)}) %collective-permute-start.16) | collective-permute-done | bytes 131104 | tf_op jit(solution)/shard_map/ppermute | solution.py:700
  59.2 4.4 %attend_head.2.refs_4_ = bf16[512,2048]{1,0:T(8,128)(2,1)} custom-call(s32[24]{0:T(128)S(1)} %get-tuple-element.48.meta_ref, bf16[512,2048]{1,0:T(8,128)(2,1)S(1)} %get-tuple-element.49.query_ref, bf16[2,128,256]{2,1,0:T(8,128)(2,1)S(1)} %get-tuple-element.61.refs_0_, bf16[2,128,256]{2,1,0:T(8,128)(2,1)S(1)} %collective-permute-done.15.refs_1_, ...), custom_call_target="tpu_custom_call" | custom-call | flops 1024 | bytes 1024 | tf_op jit(solution)/shard_map/attend_head/pallas_call | solution.py:552
  63.6 5.9 %collective-permute-done.12.refs_2_ = bf16[2,128,256]{2,1,0:T(8,128)(2,1)S(1)} collective-permute-done((bf16[2,128,256]{2,1,0:T(8,128)(2,1)S(1)}, bf16[2,128,256]{2,1,0:T(8,128)(2,1)S(1)}, u32[]{:S(2)}, u32[]{:S(2)}) %collective-permute-start.12) | collective-permute-done | bytes 131104 | tf_op jit(solution)/shard_map/ppermute | solution.py:700
  69.5 4.6 %attend_head.3 = bf16[512,2048]{1,0:T(8,128)(2,1)} custom-call(s32[24]{0:T(128)S(1)} %get-tuple-element.48.meta_ref, bf16[512,2048]{1,0:T(8,128)(2,1)S(1)} %get-tuple-element.49.query_ref, bf16[2,128,256]{2,1,0:T(8,128)(2,1)S(1)} %get-tuple-element.55.refs_0_, ...), custom_call_target="tpu_custom_call", output_to_operand_aliasing={{}: (6, {})} | custom-call | flops 1024 | bytes 1024 | tf_op jit(solution)/shard_map/attend_head/pallas_call | solution.py:552
  (49 shorter events, 5.0 us)
Async XLA Ops:
  0.0 10.9 %collective-permute-start.1 = (bf16[4,320,128]{2,1,0:T(8,128)(2,1)}, bf16[4,320,128]{2,1,0:T(8,128)(2,1)S(1)}, u32[]{:S(2)}, u32[]{:S(2)}) collective-permute-start(bf16[4,320,128]{2,1,0:T(8,128)(2,1)} %bitcast.20), channel_id=1, source_target_pairs={{0,2},{1,3},{2,0},{3,1},{4,6},{5,7},{6,4},{7,5},{8,10},{9,11},{10,... | collective-permute-start | bytes 983048 | tf_op jit(solution)/shard_map/ppermute | solution.py:602
  3.0 7.9 %collective-permute-start = (bf16[4,320,128]{2,1,0:T(8,128)(2,1)}, bf16[4,320,128]{2,1,0:T(8,128)(2,1)S(1)}, u32[]{:S(2)}, u32[]{:S(2)}) collective-permute-start(bf16[4,320,128]{2,1,0:T(8,128)(2,1)} %bitcast.21), channel_id=1, source_target_pairs={{0,1},{1,0},{2,3},{3,2},{4,5},{5,4},{6,7},{7,6},{8,9},{9,8},{10,11... | collective-permute-start | bytes 983048 | tf_op jit(solution)/shard_map/ppermute | solution.py:647
  5.2 7.4 %copy-start.6 = (f32[1280]{0:T(1024)S(1)}, f32[1280]{0:T(1024)}, u32[]{:S(2)}) copy-start(f32[1280]{0:T(1024)} %param.21) | copy-start | bytes 15364
  10.9 1.6 %collective-permute-start.2 = (bf16[4,320,128]{2,1,0:T(8,128)(2,1)S(1)}, bf16[4,320,128]{2,1,0:T(8,128)(2,1)S(1)}, u32[]{:S(2)}, u32[]{:S(2)}) collective-permute-start(bf16[4,320,128]{2,1,0:T(8,128)(2,1)S(1)} %collective-permute-done.1.refs_2_), channel_id=1, source_target_pairs={{0,1},{1,0},{2,3},{3,2},{4,5},{5,4},{6,7},{7,6},{8,9},{9,8},{10,11... | collective-permute-start | bytes 983048 | tf_op jit(solution)/shard_map/ppermute | solution.py:606
  12.5 9.3 %copy-start.9 = (f32[320]{0:T(512)S(1)}, f32[320]{0:T(512)}, u32[]{:S(2)}) copy-start(f32[320]{0:T(512)} %param.23) | copy-start | bytes 3844
  18.2 1.7 %collective-permute-start.3 = (bf16[640,256]{1,0:T(8,128)(2,1)S(1)}, bf16[640,256]{1,0:T(8,128)(2,1)S(1)}, u32[]{:S(2)}, u32[]{:S(2)}) collective-permute-start(bf16[640,256]{1,0:T(8,128)(2,1)S(1)} %get-tuple-element.40), channel_id=1, source_target_pairs={{0,1},{1,0},{2,3},{3,2},{4,5},{5,4},{6,7},{7,6},{8,9},{9,8},{10,11... | collective-permute-start | bytes 983048 | tf_op jit(solution)/shard_map/ppermute | solution.py:589
  18.4 8.7 %collective-permute-start.4 = (bf16[640,256]{1,0:T(8,128)(2,1)S(1)}, bf16[640,256]{1,0:T(8,128)(2,1)S(1)}, u32[]{:S(2)}, u32[]{:S(2)}) collective-permute-start(bf16[640,256]{1,0:T(8,128)(2,1)S(1)} %get-tuple-element.44), channel_id=1, source_target_pairs={{0,1},{1,0},{2,3},{3,2},{4,5},{5,4},{6,7},{7,6},{8,9},{9,8},{10,11... | collective-permute-start | bytes 983048 | tf_op jit(solution)/shard_map/ppermute | solution.py:589
  20.0 9.8 %collective-permute-start.5 = (bf16[640,256]{1,0:T(8,128)(2,1)S(1)}, bf16[640,256]{1,0:T(8,128)(2,1)S(1)}, u32[]{:S(2)}, u32[]{:S(2)}) collective-permute-start(bf16[640,256]{1,0:T(8,128)(2,1)S(1)} %add_convert_fusion.1), channel_id=1, source_target_pairs={{0,2},{1,3},{2,0},{3,1},{4,6},{5,7},{6,4},{7,5},{8,10},{9,11},{10,... | collective-permute-start | bytes 983048 | tf_op jit(solution)/shard_map/ppermute | solution.py:589
  21.8 8.0 %copy-start.3 = (bf16[320,2048]{1,0:T(8,128)(2,1)S(1)}, bf16[320,2048]{1,0:T(8,128)(2,1)}, u32[]{:S(2)}) copy-start(bf16[320,2048]{1,0:T(8,128)(2,1)} %refs_2_.1) | copy-start | bytes 3932164
  27.2 8.6 %copy-start = (bf16[512,2048]{1,0:T(8,128)(2,1)S(1)}, bf16[512,2048]{1,0:T(8,128)(2,1)}, u32[]{:S(2)}) copy-start(bf16[512,2048]{1,0:T(8,128)(2,1)} %query_ref.1) | copy-start | bytes 6291460
  27.2 8.6 %copy-start.8 = (f32[128]{0:T(128)S(1)}, f32[128]{0:T(128)}, u32[]{:S(2)}) copy-start(f32[128]{0:T(128)} %param.27) | copy-start | bytes 1540
  31.7 1.6 %collective-permute-start.6 = (bf16[512,256]{1,0:T(8,128)(2,1)S(1)}, bf16[512,256]{1,0:T(8,128)(2,1)S(1)}, u32[]{:S(2)}, u32[]{:S(2)}) collective-permute-start(bf16[512,256]{1,0:T(8,128)(2,1)S(1)} %get-tuple-element.46), channel_id=1, source_target_pairs={{0,1},{1,0},{2,3},{3,2},{4,5},{5,4},{6,7},{7,6},{8,9},{9,8},{10,11... | collective-permute-start | bytes 786440 | tf_op jit(solution)/shard_map/ppermute | solution.py:589
  31.7 3.9 %collective-permute-start.8 = (bf16[512,256]{1,0:T(8,128)(2,1)S(1)}, bf16[512,256]{1,0:T(8,128)(2,1)S(1)}, u32[]{:S(2)}, u32[]{:S(2)}) collective-permute-start(bf16[512,256]{1,0:T(8,128)(2,1)S(1)} %get-tuple-element.53), channel_id=1, source_target_pairs={{0,1},{1,0},{2,3},{3,2},{4,5},{5,4},{6,7},{7,6},{8,9},{9,8},{10,11... | collective-permute-start | bytes 786440 | tf_op jit(solution)/shard_map/ppermute | solution.py:589
  33.3 10.3 %copy-start.7 = (f32[128]{0:T(128)S(1)}, f32[128]{0:T(128)}, u32[]{:S(2)}) copy-start(f32[128]{0:T(128)} %param.26) | copy-start | bytes 1540
  33.4 8.4 %collective-permute-start.9 = (bf16[512,256]{1,0:T(8,128)(2,1)S(1)}, bf16[512,256]{1,0:T(8,128)(2,1)S(1)}, u32[]{:S(2)}, u32[]{:S(2)}) collective-permute-start(bf16[512,256]{1,0:T(8,128)(2,1)S(1)} %add_convert_fusion.5), channel_id=1, source_target_pairs={{0,2},{1,3},{2,0},{3,1},{4,6},{5,7},{6,4},{7,5},{8,10},{9,11},{10,... | collective-permute-start | bytes 786440 | tf_op jit(solution)/shard_map/ppermute | solution.py:589
  35.2 8.4 %collective-permute-start.14 = (bf16[512,256]{1,0:T(8,128)(2,1)S(1)}, bf16[512,256]{1,0:T(8,128)(2,1)S(1)}, u32[]{:S(2)}, u32[]{:S(2)}) collective-permute-start(bf16[512,256]{1,0:T(8,128)(2,1)S(1)} %get-tuple-element.60), channel_id=1, source_target_pairs={{0,1},{1,0},{2,3},{3,2},{4,5},{5,4},{6,7},{7,6},{8,9},{9,8},{10,11... | collective-permute-start | bytes 786440 | tf_op jit(solution)/shard_map/ppermute | solution.py:589
  35.2 10.9 %collective-permute-start.7 = (bf16[512,256]{1,0:T(8,128)(2,1)S(1)}, bf16[512,256]{1,0:T(8,128)(2,1)S(1)}, u32[]{:S(2)}, u32[]{:S(2)}) collective-permute-start(bf16[512,256]{1,0:T(8,128)(2,1)S(1)} %get-tuple-element.51), channel_id=1, source_target_pairs={{0,1},{1,0},{2,3},{3,2},{4,5},{5,4},{6,7},{7,6},{8,9},{9,8},{10,11... | collective-permute-start | bytes 786440 | tf_op jit(solution)/shard_map/ppermute | solution.py:589
  41.8 7.5 %collective-permute-start.10 = (bf16[512,256]{1,0:T(8,128)(2,1)S(1)}, bf16[512,256]{1,0:T(8,128)(2,1)S(1)}, u32[]{:S(2)}, u32[]{:S(2)}) collective-permute-start(bf16[512,256]{1,0:T(8,128)(2,1)S(1)} %add_convert_fusion.3), channel_id=1, source_target_pairs={{0,2},{1,3},{2,0},{3,1},{4,6},{5,7},{6,4},{7,5},{8,10},{9,11},{10,... | collective-permute-start | bytes 786440 | tf_op jit(solution)/shard_map/ppermute | solution.py:589
  44.4 10.2 %collective-permute-start.15 = (bf16[2,128,256]{2,1,0:T(8,128)(2,1)S(1)}, bf16[2,128,256]{2,1,0:T(8,128)(2,1)S(1)}, u32[]{:S(2)}, u32[]{:S(2)}) collective-permute-start(bf16[2,128,256]{2,1,0:T(8,128)(2,1)S(1)} %get-tuple-element.62), channel_id=1, source_target_pairs={{0,4},{4,0},{8,12},{12,8},{1,5},{5,1},{9,13},{13,9},{2,6},{6,2},{1... | collective-permute-start | bytes 393224 | tf_op jit(solution)/shard_map/ppermute | solution.py:700
  46.1 13.1 %collective-permute-start.16 = (bf16[2,128,256]{2,1,0:T(8,128)(2,1)S(1)}, bf16[2,128,256]{2,1,0:T(8,128)(2,1)S(1)}, u32[]{:S(2)}, u32[]{:S(2)}) collective-permute-start(bf16[2,128,256]{2,1,0:T(8,128)(2,1)S(1)} %get-tuple-element.63), channel_id=1, source_target_pairs={{0,8},{4,12},{8,0},{12,4},{1,9},{5,13},{9,1},{13,5},{2,10},{6,14},... | collective-permute-start | bytes 393224 | tf_op jit(solution)/shard_map/ppermute | solution.py:700
  48.8 10.4 %collective-permute-start.17 = (bf16[2,128,256]{2,1,0:T(8,128)(2,1)S(1)}, bf16[2,128,256]{2,1,0:T(8,128)(2,1)S(1)}, u32[]{:S(2)}, u32[]{:S(2)}) collective-permute-start(bf16[2,128,256]{2,1,0:T(8,128)(2,1)S(1)} %get-tuple-element.64), channel_id=1, source_target_pairs={{0,12},{4,8},{8,4},{12,0},{1,13},{5,9},{9,5},{13,1},{2,14},{6,10},... | collective-permute-start | bytes 393224 | tf_op jit(solution)/shard_map/ppermute | solution.py:700
  50.1 13.5 %collective-permute-start.11 = (bf16[2,128,256]{2,1,0:T(8,128)(2,1)S(1)}, bf16[2,128,256]{2,1,0:T(8,128)(2,1)S(1)}, u32[]{:S(2)}, u32[]{:S(2)}) collective-permute-start(bf16[2,128,256]{2,1,0:T(8,128)(2,1)S(1)} %get-tuple-element.56), channel_id=1, source_target_pairs={{0,4},{4,0},{8,12},{12,8},{1,5},{5,1},{9,13},{13,9},{2,6},{6,2},{1... | collective-permute-start | bytes 393224 | tf_op jit(solution)/shard_map/ppermute | solution.py:700
  51.9 17.6 %collective-permute-start.12 = (bf16[2,128,256]{2,1,0:T(8,128)(2,1)S(1)}, bf16[2,128,256]{2,1,0:T(8,128)(2,1)S(1)}, u32[]{:S(2)}, u32[]{:S(2)}) collective-permute-start(bf16[2,128,256]{2,1,0:T(8,128)(2,1)S(1)} %get-tuple-element.57), channel_id=1, source_target_pairs={{0,8},{4,12},{8,0},{12,4},{1,9},{5,13},{9,1},{13,5},{2,10},{6,14},... | collective-permute-start | bytes 393224 | tf_op jit(solution)/shard_map/ppermute | solution.py:700
  54.5 15.0 %collective-permute-start.13 = (bf16[2,128,256]{2,1,0:T(8,128)(2,1)S(1)}, bf16[2,128,256]{2,1,0:T(8,128)(2,1)S(1)}, u32[]{:S(2)}, u32[]{:S(2)}) collective-permute-start(bf16[2,128,256]{2,1,0:T(8,128)(2,1)S(1)} %get-tuple-element.58), channel_id=1, source_target_pairs={{0,12},{4,8},{8,4},{12,0},{1,13},{5,9},{9,5},{13,1},{2,14},{6,10},... | collective-permute-start | bytes 393224 | tf_op jit(solution)/shard_map/ppermute | solution.py:700
  (4 other events, 23.5 us)

commit v3 on v2

--- a/solution.py
+++ b/solution.py
@@ -349,12 +349,7 @@
     )(where, tap_tiles, weights, *staged)
 
 
-def kv_kernel(head_count, dest_count, dup, part_count, term_counts, where_ref, *refs):
-    x_ref, bias_ref, weight_ref = refs[:3]
-    tap_blocks = [ref.at[n] for ref in refs[3 : 3 + part_count] for n in range(ref.shape[0])]
-    terms = refs[3 + part_count : 3 + part_count + sum(term_counts)]
-    outs = refs[3 + part_count + sum(term_counts) : -1]
-    encoded_ref = refs[-1]
+def encode(x_ref, bias_ref, term_counts, terms, encoded_ref):
     tiles, width, tile_rows = x_ref.shape
     half_tiles = tiles // len(term_counts)
     whole, tail, extra = tail_plan(half_tiles * tile_rows, width)
@@ -380,42 +375,46 @@
             total = jnp.concatenate([total, rest], axis=1)
         total = total + x_ref[tile].T.astype(F32) + bias
         encoded_ref[tile * tile_rows : (tile + 1) * tile_rows, :] = total.astype(BF16)
+
+
+def kv_kernel(head, head_count, dest_count, dup, taps_at, term_counts, where_ref, *refs):
+    weight_ref, refs = refs[0], refs[1:]
+    part_count = 1 + max(part for part, _ in taps_at)
+    tap_refs, refs = refs[:part_count], refs[part_count:]
+    outs = refs[-dest_count - 1 :] if head == 0 else refs[-dest_count:]
+    if head == 0:
+        encoded_ref = outs[-1]
+        encode(refs[0], refs[1], term_counts, refs[2 : 2 + sum(term_counts)], encoded_ref)
+    else:
+        encoded_ref = refs[0]
     block = 2 * HD
     mine = lax.div(where_ref[1], jnp.int32(dup))
-    for head in range(head_count):
-        for k in range(dest_count):
-            column = ((mine ^ k) * head_count + head) * block
-            weights = weight_ref[:, pl.ds(pl.multiple_of(column, block), block)]
-            value = jnp.dot(encoded_ref[...], weights, preferred_element_type=F32)
-            value = value + tap_blocks[head * dest_count + k][...].astype(F32)
-            outs[head * dest_count + k][...] = value.astype(BF16)
-
-
-def kv_projection(
-    where, x_tiles, b_down, weights, tap_parts, halves, head_count, dest_count, dup
-):
-    terms = [term for half in halves for term in half]
-    tiles, width, tile_rows = x_tiles.shape
-    rows = tiles * tile_rows
-    block = 2 * HD
-    outs = pl.pallas_call(
+    for k in range(dest_count):
+        column = ((mine ^ k) * head_count + head) * block
+        weights = weight_ref[:, pl.ds(pl.multiple_of(column, block), block)]
+        value = jnp.dot(encoded_ref[...], weights, preferred_element_type=F32)
+        part, n = taps_at[k]
+        value = value + tap_refs[part][n].astype(F32)
+        outs[k][...] = value.astype(BF16)
+
+
+def kv_projection(where, weights, tap_parts, taps_at, inputs, term_counts, head, head_count, dup):
+    tap_parts = tap_parts[: 1 + max(part for part, _ in taps_at)]
+    rows, dest_count, block = tap_parts[0].shape[1], len(taps_at), 2 * HD
+    outs = [jax.ShapeDtypeStruct((rows, block), BF16)] * dest_count
+    if head == 0:
+        outs.append(jax.ShapeDtypeStruct((rows, weights.shape[0]), BF16))
+    return pl.pallas_call(
         functools.partial(
-            kv_kernel,
-            head_count,
-            dest_count,
-            dup,
-            len(tap_parts),
-            tuple(len(half) for half in halves),
+            kv_kernel, head, head_count, dest_count, dup, tuple(taps_at), term_counts
         ),
-        out_shape=[jax.ShapeDtypeStruct((rows, block), BF16)] * (head_count * dest_count),
-        in_specs=[SMEM] + [VMEM] * (3 + len(tap_parts) + len(terms)),
-        out_specs=[VMEM] * (head_count * dest_count),
-        scratch_shapes=[pltpu.VMEM((rows, width), BF16)],
+        out_shape=outs,
+        in_specs=[SMEM] + [VMEM] * (1 + len(tap_parts) + len(inputs)),
+        out_specs=[VMEM] * len(outs),
         compiler_params=pltpu.CompilerParams(vmem_limit_bytes=24 * MIB),
         cost_estimate=LIGHT,
         name="kv_projection",
-    )(where, x_tiles, lane_rows(b_down), weights, *tap_parts, *terms)
-    return [outs[h * dest_count : (h + 1) * dest_count] for h in range(head_count)]
+    )(where, weights, *tap_parts, *inputs)
 
 
 def finish_kernel(term_count, picks, meta_ref, gain_ref, *refs):
@@ -664,17 +663,25 @@
     (last_taps,) = tap_projection(
         begun, tap_tiles, kv_w_taps, tap_blocks[early:], head_count, dup, ()
     )
-    kv_blocks = kv_projection(
-        where,
-        x_tiles,
-        b_down,
-        kv_w_out,
-        (first_taps, last_taps),
-        mlp_terms,
-        head_count,
-        dest_count,
-        dup,
-    )
+    taps_at = [(0, n) for n in range(early)]
+    taps_at += [(1, n) for n in range(len(tap_blocks) - early)]
+    kv_blocks = []
+    inputs = (x_tiles, lane_rows(b_down), *(term for half in mlp_terms for term in half))
+    for head in range(head_count):
+        made = kv_projection(
+            where,
+            kv_w_out,
+            (first_taps, last_taps),
+            taps_at[head * dest_count : (head + 1) * dest_count],
+            inputs,
+            tuple(len(half) for half in mlp_terms),
+            head,
+            head_count,
+            dup,
+        )
+        kv_blocks.append(made[:dest_count])
+        if head == 0:
+            inputs = (made[-1],)
     kv_terms, arrived = [], None
     for head in range(head_count):
         blocks = kv_blocks[head]

time: 74.5 us -> 73.3 us (0.984)
  Pallas kernels: 31.1 us -> 29.6 us
    pallas_call x2, Pallas kernels: 9 us -> 6.76 us  [attend_head(): pl.pallas_call(functools.partial(attend_kernel, group_count, sources, hea...]
    ppermute x9, waiting for transfers between devices: 8.23 us -> 7.03 us  [scatter_sum(): got[k ^ 1 << b] = lax.ppermute(sent, 'tp', pairs)]
    ppermute x6, waiting for transfers between devices: 10.6 us -> 11.7 us  [move(): return lax.ppermute(value, 'grp', xor_pairs(group_count, mask))]
    pallas_call x1 -> x2, Pallas kernels: 1.86 us -> 2.58 us  [kv_projection(): pl.pallas_call(functools.partial(kv_kernel, head, head_count, dest_count,...]
  transfers between devices with their start and end apart: 18 -> 18, of which waited for: 9 -> 8; matrix products, arithmetic and copies ran while one was open for 2% -> 2% of each run, Pallas kernels for 26% -> 26%
where the time goes in v3:
time: 73.3 us; the launch traced here: 72.7 us
  Pallas kernels  29.6 us (40%)
  waiting for transfers between devices  21.1 us (29%)
  starting transfers between devices  19 us (26%)
  local copies, waits for them, and re-layouts  2.24 us (3%)
    ppermute x6, waiting for transfers between devices, move(): return lax.ppermute(value, 'grp', xor_pairs(group_count, mask))  11.7 us
    pallas_call x2, Pallas kernels, tap_projection(): pl.pallas_call(functools.partial(tap_kernel, blocks, head_count, dup, len...  10.2 us
    ppermute x6, starting transfers between devices, move(): return lax.ppermute(value, 'grp', xor_pairs(group_count, mask))  8.97 us
    ppermute x9, waiting for transfers between devices, scatter_sum(): got[k ^ 1 << b] = lax.ppermute(sent, 'tp', pairs)  7.03 us
    ppermute x9, starting transfers between devices, scatter_sum(): got[k ^ 1 << b] = lax.ppermute(sent, 'tp', pairs)  7.02 us
    pallas_call x2, Pallas kernels, attend_head(): pl.pallas_call(functools.partial(attend_kernel, group_count, sources, hea...  6.76 us
    pallas_call x1, Pallas kernels, encoder_mlp(): pl.pallas_call(functools.partial(mlp_kernel, count, bases, tiles), out_sh...  5.66 us
    ppermute x1, starting transfers between devices, gather_half(): pieces[k | 1 << b] = lax.ppermute(pieces[k], 'tp', pairs)  2.97 us
  transfers between devices with their start and end apart: 18, of which 8 were waited for; matrix products, arithmetic and copies ran while one was open for 2% of the time, Pallas kernels for 26%

profile of v3, /device:TPU:0, one launch (start us, length us, event | category | flops | bytes accessed | tf_op | source)
XLA Modules:
  0.0 72.7 jit_solution(9002231202420677386)
XLA Ops:
  0.0 3.0 %collective-permute-start.1 = (bf16[4,320,128]{2,1,0:T(8,128)(2,1)}, bf16[4,320,128]{2,1,0:T(8,128)(2,1)S(1)}, u32[]{:S(2)}, u32[]{:S(2)}) collective-permute-start(bf16[4,320,128]{2,1,0:T(8,128)(2,1)} %bitcast.20), channel_id=1, source_target_pairs={{0,2},{1,3},{2,0},{3,1},{4,6},{5,7},{6,4},{7,5},{8,10},{9,11},{10,... | collective-permute-start | bytes 983048 | tf_op jit(solution)/shard_map/ppermute | solution.py:601
  3.7 1.4 %copy-done.2 = bf16[4,1,128,1600]{2,3,1,0:T(8,128)(2,1)S(1)} copy-done((bf16[4,1,128,1600]{2,3,1,0:T(8,128)(2,1)S(1)}, bf16[4,1,128,1600]{2,3,1,0:T(8,128)(2,1)}, u32[]{:S(2)}) %copy-start.2) | copy-done | bytes 1638424
  5.2 4.9 %tap_projection.2 = (bf16[3,512,256]{2,1,0:T(8,128)(2,1)S(1)}, bf16[1280,1280]{1,0:T(8,128)(2,1)S(1)}, bf16[1280,1280]{1,0:T(8,128)(2,1)S(1)}, bf16[4,1600,128]{2,1,0:T(8,128)(2,1)S(1)}) custom-call(s32[26]{0:T(128)S(1)} %concatenate.3.where_ref, bf16[4,1600,128]{2,1,0:T(8,128)(2,1)S(1)} %bitcast.19, bf16[1600,2048]{1,0:T(8,128)(2,1)} %weight_hbm.3, ...), custom_call_target="tpu_custom_call" | custom-call | flops 1024 | bytes 1024 | tf_op jit(solution)/shard_map/tap_projection/pallas_call | solution.py:335
  10.9 1.6 %collective-permute-done.2.refs_3_ = bf16[4,320,128]{2,1,0:T(8,128)(2,1)S(1)} collective-permute-done((bf16[4,320,128]{2,1,0:T(8,128)(2,1)S(1)}, bf16[4,320,128]{2,1,0:T(8,128)(2,1)S(1)}, u32[]{:S(2)}, u32[]{:S(2)}) %collective-permute-start.2) | collective-permute-done | bytes 327712 | tf_op jit(solution)/shard_map/ppermute | solution.py:605
  12.5 5.7 %encoder_mlp.1 = (bf16[640,256]{1,0:T(8,128)(2,1)S(1)}, bf16[640,256]{1,0:T(8,128)(2,1)S(1)}, bf16[640,256]{1,0:T(8,128)(2,1)S(1)}, bf16[640,256]{1,0:T(8,128)(2,1)S(1)}) custom-call(s32[26]{0:T(128)S(1)} %concatenate.3.where_ref, bf16[4,320,128]{2,1,0:T(8,128)(2,1)S(1)} %bitcast.22, bf16[4,320,128]{2,1,0:T(8,128)(2,1)S(1)} %collective-permute-done.refs_1_, ...), custom_call_target="tpu_custom_call" | custom-call | flops 1024 | bytes 1024 | tf_op jit(solution)/shard_map/encoder_mlp/pallas_call | solution.py:221
  18.8 1.1 %collective-permute-done.3 = bf16[640,256]{1,0:T(8,128)(2,1)S(1)} collective-permute-done((bf16[640,256]{1,0:T(8,128)(2,1)S(1)}, bf16[640,256]{1,0:T(8,128)(2,1)S(1)}, u32[]{:S(2)}, u32[]{:S(2)}) %collective-permute-start.3) | collective-permute-done | bytes 327712 | tf_op jit(solution)/shard_map/ppermute | solution.py:588
  20.0 1.8 %collective-permute-start.5 = (bf16[640,256]{1,0:T(8,128)(2,1)S(1)}, bf16[640,256]{1,0:T(8,128)(2,1)S(1)}, u32[]{:S(2)}, u32[]{:S(2)}) collective-permute-start(bf16[640,256]{1,0:T(8,128)(2,1)S(1)} %add_convert_fusion.1), channel_id=1, source_target_pairs={{0,2},{1,3},{2,0},{3,1},{4,6},{5,7},{6,4},{7,5},{8,10},{9,11},{10,... | collective-permute-start | bytes 983048 | tf_op jit(solution)/shard_map/ppermute | solution.py:588
  21.8 5.3 %tap_projection.3.refs_2_ = bf16[5,512,256]{2,1,0:T(8,128)(2,1)S(1)} custom-call(s32[26]{0:T(128)S(1)} %concatenate.3.where_ref, bf16[4,1600,128]{2,1,0:T(8,128)(2,1)S(1)} %get-tuple-element.43.tap_hbm, bf16[1600,2048]{1,0:T(8,128)(2,1)} %weight_hbm.3), custom_call_target="tpu_custom_call" | custom-call | flops 1024 | bytes 1024 | tf_op jit(solution)/shard_map/tap_projection/pallas_call | solution.py:335
  27.2 2.6 %collective-permute-done.5.refs_6_ = bf16[640,256]{1,0:T(8,128)(2,1)S(1)} collective-permute-done((bf16[640,256]{1,0:T(8,128)(2,1)S(1)}, bf16[640,256]{1,0:T(8,128)(2,1)S(1)}, u32[]{:S(2)}, u32[]{:S(2)}) %collective-permute-start.5) | collective-permute-done | bytes 327712 | tf_op jit(solution)/shard_map/ppermute | solution.py:588
  29.8 1.3 %kv_projection.2 = (bf16[512,256]{1,0:T(8,128)(2,1)S(1)}, bf16[512,256]{1,0:T(8,128)(2,1)S(1)}, bf16[512,256]{1,0:T(8,128)(2,1)S(1)}, bf16[512,256]{1,0:T(8,128)(2,1)S(1)}, bf16[512,320]{1,0:T(8,128)(2,1)S(1)}) custom-call(s32[26]{0:T(128)S(1)} %concatenate.3.where_ref, bf16[320,2048]{1,0:T(8,128)(2,1)S(1)} %copy-done, ...), custom_call_target="tpu_custom_call" | custom-call | flops 1024 | bytes 1024 | tf_op jit(solution)/shard_map/kv_projection/pallas_call | solution.py:407
  31.2 1.3 %kv_projection.3 = (bf16[512,256]{1,0:T(8,128)(2,1)S(1)}, bf16[512,256]{1,0:T(8,128)(2,1)S(1)}, bf16[512,256]{1,0:T(8,128)(2,1)S(1)}, bf16[512,256]{1,0:T(8,128)(2,1)S(1)}) custom-call(s32[26]{0:T(128)S(1)} %concatenate.3.where_ref, bf16[320,2048]{1,0:T(8,128)(2,1)S(1)} %copy-done, bf16[3,512,256]{2,1,0:T(8,128)(2,1)S(1)} %get-tuple-element.36.refs_1_, ...), custom_call_target="tpu_custom_call" | custom-call | flops 1024 | bytes 1024 | tf_op jit(solution)/shard_map/kv_projection/pallas_call | solution.py:407
  33.1 1.8 %collective-permute-start.9 = (bf16[512,256]{1,0:T(8,128)(2,1)S(1)}, bf16[512,256]{1,0:T(8,128)(2,1)S(1)}, u32[]{:S(2)}, u32[]{:S(2)}) collective-permute-start(bf16[512,256]{1,0:T(8,128)(2,1)S(1)} %add_convert_fusion.5), channel_id=1, source_target_pairs={{0,2},{1,3},{2,0},{3,1},{4,6},{5,7},{6,4},{7,5},{8,10},{9,11},{10,... | collective-permute-start | bytes 786440 | tf_op jit(solution)/shard_map/ppermute | solution.py:588
  35.5 2.8 %prepare.1 = (bf16[512,2048]{1,0:T(8,128)(2,1)S(1)}, s32[24]{0:T(128)S(1)}) custom-call(s32[26]{0:T(128)S(1)} %concatenate.3.where_ref, f32[1,128]{1,0:T(1,128)S(1)} %bitcast.29, bf16[512,2048]{1,0:T(8,128)(2,1)S(1)} %copy-done.1), custom_call_target="tpu_custom_call" | custom-call | flops 1024 | bytes 1024 | tf_op jit(solution)/shard_map/prepare/pallas_call | solution.py:269
  38.3 3.1 %collective-permute-done.9.refs_1_ = bf16[512,256]{1,0:T(8,128)(2,1)S(1)} collective-permute-done((bf16[512,256]{1,0:T(8,128)(2,1)S(1)}, bf16[512,256]{1,0:T(8,128)(2,1)S(1)}, u32[]{:S(2)}, u32[]{:S(2)}) %collective-permute-start.9) | collective-permute-done | bytes 262176 | tf_op jit(solution)/shard_map/ppermute | solution.py:588
  41.4 1.7 %collective-permute-start.10 = (bf16[512,256]{1,0:T(8,128)(2,1)S(1)}, bf16[512,256]{1,0:T(8,128)(2,1)S(1)}, u32[]{:S(2)}, u32[]{:S(2)}) collective-permute-start(bf16[512,256]{1,0:T(8,128)(2,1)S(1)} %add_convert_fusion.3), channel_id=1, source_target_pairs={{0,2},{1,3},{2,0},{3,1},{4,6},{5,7},{6,4},{7,5},{8,10},{9,11},{10,... | collective-permute-start | bytes 786440 | tf_op jit(solution)/shard_map/ppermute | solution.py:588
  43.3 0.8 %finish_tiles.3 = (bf16[2,128,256]{2,1,0:T(8,128)(2,1)S(1)}, bf16[2,128,256]{2,1,0:T(8,128)(2,1)S(1)}, bf16[2,128,256]{2,1,0:T(8,128)(2,1)S(1)}, bf16[2,128,256]{2,1,0:T(8,128)(2,1)S(1)}) custom-call(s32[24]{0:T(128)S(1)} %get-tuple-element.49.meta_ref, f32[1,128]{1,0:T(1,128)S(1)} %bitcast.27, bf16[512,256]{1,0:T(8,128)(2,1)S(1)} %add_convert_fusion.2.refs_0_, ...), custom_call_target="tpu_custom_call" | custom-call | flops 1024 | bytes 1024 | tf_op jit(solution)/shard_map/finish_tiles/pallas_call | solution.py:443
  44.1 1.6 %collective-permute-start.15 = (bf16[2,128,256]{2,1,0:T(8,128)(2,1)S(1)}, bf16[2,128,256]{2,1,0:T(8,128)(2,1)S(1)}, u32[]{:S(2)}, u32[]{:S(2)}) collective-permute-start(bf16[2,128,256]{2,1,0:T(8,128)(2,1)S(1)} %get-tuple-element.64), channel_id=1, source_target_pairs={{0,4},{4,0},{8,12},{12,8},{1,5},{5,1},{9,13},{13,9},{2,6},{6,2},{1... | collective-permute-start | bytes 393224 | tf_op jit(solution)/shard_map/ppermute | solution.py:707
  45.8 2.7 %collective-permute-start.16 = (bf16[2,128,256]{2,1,0:T(8,128)(2,1)S(1)}, bf16[2,128,256]{2,1,0:T(8,128)(2,1)S(1)}, u32[]{:S(2)}, u32[]{:S(2)}) collective-permute-start(bf16[2,128,256]{2,1,0:T(8,128)(2,1)S(1)} %get-tuple-element.65), channel_id=1, source_target_pairs={{0,8},{4,12},{8,0},{12,4},{1,9},{5,13},{9,1},{13,5},{2,10},{6,14},... | collective-permute-start | bytes 393224 | tf_op jit(solution)/shard_map/ppermute | solution.py:707
  49.6 1.9 %collective-permute-start.11 = (bf16[2,128,256]{2,1,0:T(8,128)(2,1)S(1)}, bf16[2,128,256]{2,1,0:T(8,128)(2,1)S(1)}, u32[]{:S(2)}, u32[]{:S(2)}) collective-permute-start(bf16[2,128,256]{2,1,0:T(8,128)(2,1)S(1)} %get-tuple-element.58), channel_id=1, source_target_pairs={{0,4},{4,0},{8,12},{12,8},{1,5},{5,1},{9,13},{13,9},{2,6},{6,2},{1... | collective-permute-start | bytes 393224 | tf_op jit(solution)/shard_map/ppermute | solution.py:707
  51.5 2.6 %collective-permute-start.12 = (bf16[2,128,256]{2,1,0:T(8,128)(2,1)S(1)}, bf16[2,128,256]{2,1,0:T(8,128)(2,1)S(1)}, u32[]{:S(2)}, u32[]{:S(2)}) collective-permute-start(bf16[2,128,256]{2,1,0:T(8,128)(2,1)S(1)} %get-tuple-element.59), channel_id=1, source_target_pairs={{0,8},{4,12},{8,0},{12,4},{1,9},{5,13},{9,1},{13,5},{2,10},{6,14},... | collective-permute-start | bytes 393224 | tf_op jit(solution)/shard_map/ppermute | solution.py:707
  54.1 4.7 %collective-permute-done.16.refs_2_ = bf16[2,128,256]{2,1,0:T(8,128)(2,1)S(1)} collective-permute-done((bf16[2,128,256]{2,1,0:T(8,128)(2,1)S(1)}, bf16[2,128,256]{2,1,0:T(8,128)(2,1)S(1)}, u32[]{:S(2)}, u32[]{:S(2)}) %collective-permute-start.16) | collective-permute-done | bytes 131104 | tf_op jit(solution)/shard_map/ppermute | solution.py:707
  58.8 3.3 %attend_head.2.refs_4_ = bf16[512,2048]{1,0:T(8,128)(2,1)} custom-call(s32[24]{0:T(128)S(1)} %get-tuple-element.49.meta_ref, bf16[512,2048]{1,0:T(8,128)(2,1)S(1)} %get-tuple-element.50.query_ref, bf16[2,128,256]{2,1,0:T(8,128)(2,1)S(1)} %get-tuple-element.63.refs_0_, bf16[2,128,256]{2,1,0:T(8,128)(2,1)S(1)} %collective-permute-done.15.refs_1_, ...), custom_call_target="tpu_custom_call" | custom-call | flops 1024 | bytes 1024 | tf_op jit(solution)/shard_map/attend_head/pallas_call | solution.py:551
  62.1 7.0 %collective-permute-done.12.refs_2_ = bf16[2,128,256]{2,1,0:T(8,128)(2,1)S(1)} collective-permute-done((bf16[2,128,256]{2,1,0:T(8,128)(2,1)S(1)}, bf16[2,128,256]{2,1,0:T(8,128)(2,1)S(1)}, u32[]{:S(2)}, u32[]{:S(2)}) %collective-permute-start.12) | collective-permute-done | bytes 131104 | tf_op jit(solution)/shard_map/ppermute | solution.py:707
  69.1 3.5 %attend_head.3 = bf16[512,2048]{1,0:T(8,128)(2,1)} custom-call(s32[24]{0:T(128)S(1)} %get-tuple-element.49.meta_ref, bf16[512,2048]{1,0:T(8,128)(2,1)S(1)} %get-tuple-element.50.query_ref, bf16[2,128,256]{2,1,0:T(8,128)(2,1)S(1)} %get-tuple-element.57.refs_0_, ...), custom_call_target="tpu_custom_call", output_to_operand_aliasing={{}: (6, {})} | custom-call | flops 1024 | bytes 1024 | tf_op jit(solution)/shard_map/attend_head/pallas_call | solution.py:551
  (50 shorter events, 4.9 us)
Async XLA Ops:
  0.0 10.9 %collective-permute-start.1 = (bf16[4,320,128]{2,1,0:T(8,128)(2,1)}, bf16[4,320,128]{2,1,0:T(8,128)(2,1)S(1)}, u32[]{:S(2)}, u32[]{:S(2)}) collective-permute-start(bf16[4,320,128]{2,1,0:T(8,128)(2,1)} %bitcast.20), channel_id=1, source_target_pairs={{0,2},{1,3},{2,0},{3,1},{4,6},{5,7},{6,4},{7,5},{8,10},{9,11},{10,... | collective-permute-start | bytes 983048 | tf_op jit(solution)/shard_map/ppermute | solution.py:601
  3.0 7.9 %collective-permute-start = (bf16[4,320,128]{2,1,0:T(8,128)(2,1)}, bf16[4,320,128]{2,1,0:T(8,128)(2,1)S(1)}, u32[]{:S(2)}, u32[]{:S(2)}) collective-permute-start(bf16[4,320,128]{2,1,0:T(8,128)(2,1)} %bitcast.21), channel_id=1, source_target_pairs={{0,1},{1,0},{2,3},{3,2},{4,5},{5,4},{6,7},{7,6},{8,9},{9,8},{10,11... | collective-permute-start | bytes 983048 | tf_op jit(solution)/shard_map/ppermute | solution.py:646
  5.2 7.4 %copy-start.4 = (f32[1280]{0:T(1024)S(1)}, f32[1280]{0:T(1024)}, u32[]{:S(2)}) copy-start(f32[1280]{0:T(1024)} %param.18) | copy-start | bytes 15364
  5.2 7.4 %copy-start.5 = (f32[1280]{0:T(1024)S(1)}, f32[1280]{0:T(1024)}, u32[]{:S(2)}) copy-start(f32[1280]{0:T(1024)} %param.19) | copy-start | bytes 15364
  5.2 7.4 %copy-start.6 = (f32[1280]{0:T(1024)S(1)}, f32[1280]{0:T(1024)}, u32[]{:S(2)}) copy-start(f32[1280]{0:T(1024)} %param.21) | copy-start | bytes 15364
  10.9 1.6 %collective-permute-start.2 = (bf16[4,320,128]{2,1,0:T(8,128)(2,1)S(1)}, bf16[4,320,128]{2,1,0:T(8,128)(2,1)S(1)}, u32[]{:S(2)}, u32[]{:S(2)}) collective-permute-start(bf16[4,320,128]{2,1,0:T(8,128)(2,1)S(1)} %collective-permute-done.1.refs_2_), channel_id=1, source_target_pairs={{0,1},{1,0},{2,3},{3,2},{4,5},{5,4},{6,7},{7,6},{8,9},{9,8},{10,11... | collective-permute-start | bytes 983048 | tf_op jit(solution)/shard_map/ppermute | solution.py:605
  12.5 9.2 %copy-start.9 = (f32[320]{0:T(512)S(1)}, f32[320]{0:T(512)}, u32[]{:S(2)}) copy-start(f32[320]{0:T(512)} %param.23) | copy-start | bytes 3844
  18.2 1.7 %collective-permute-start.3 = (bf16[640,256]{1,0:T(8,128)(2,1)S(1)}, bf16[640,256]{1,0:T(8,128)(2,1)S(1)}, u32[]{:S(2)}, u32[]{:S(2)}) collective-permute-start(bf16[640,256]{1,0:T(8,128)(2,1)S(1)} %get-tuple-element.41), channel_id=1, source_target_pairs={{0,1},{1,0},{2,3},{3,2},{4,5},{5,4},{6,7},{7,6},{8,9},{9,8},{10,11... | collective-permute-start | bytes 983048 | tf_op jit(solution)/shard_map/ppermute | solution.py:588
  18.4 8.7 %collective-permute-start.4 = (bf16[640,256]{1,0:T(8,128)(2,1)S(1)}, bf16[640,256]{1,0:T(8,128)(2,1)S(1)}, u32[]{:S(2)}, u32[]{:S(2)}) collective-permute-start(bf16[640,256]{1,0:T(8,128)(2,1)S(1)} %get-tuple-element.45), channel_id=1, source_target_pairs={{0,1},{1,0},{2,3},{3,2},{4,5},{5,4},{6,7},{7,6},{8,9},{9,8},{10,11... | collective-permute-start | bytes 983048 | tf_op jit(solution)/shard_map/ppermute | solution.py:588
  20.0 9.8 %collective-permute-start.5 = (bf16[640,256]{1,0:T(8,128)(2,1)S(1)}, bf16[640,256]{1,0:T(8,128)(2,1)S(1)}, u32[]{:S(2)}, u32[]{:S(2)}) collective-permute-start(bf16[640,256]{1,0:T(8,128)(2,1)S(1)} %add_convert_fusion.1), channel_id=1, source_target_pairs={{0,2},{1,3},{2,0},{3,1},{4,6},{5,7},{6,4},{7,5},{8,10},{9,11},{10,... | collective-permute-start | bytes 983048 | tf_op jit(solution)/shard_map/ppermute | solution.py:588
  21.8 8.0 %copy-start = (bf16[320,2048]{1,0:T(8,128)(2,1)S(1)}, bf16[320,2048]{1,0:T(8,128)(2,1)}, u32[]{:S(2)}) copy-start(bf16[320,2048]{1,0:T(8,128)(2,1)} %refs_0_.5) | copy-start | bytes 3932164
  31.1 1.9 %collective-permute-start.6 = (bf16[512,256]{1,0:T(8,128)(2,1)S(1)}, bf16[512,256]{1,0:T(8,128)(2,1)S(1)}, u32[]{:S(2)}, u32[]{:S(2)}) collective-permute-start(bf16[512,256]{1,0:T(8,128)(2,1)S(1)} %get-tuple-element.47), channel_id=1, source_target_pairs={{0,1},{1,0},{2,3},{3,2},{4,5},{5,4},{6,7},{7,6},{8,9},{9,8},{10,11... | collective-permute-start | bytes 786440 | tf_op jit(solution)/shard_map/ppermute | solution.py:588
  32.5 2.9 %collective-permute-start.8 = (bf16[512,256]{1,0:T(8,128)(2,1)S(1)}, bf16[512,256]{1,0:T(8,128)(2,1)S(1)}, u32[]{:S(2)}, u32[]{:S(2)}) collective-permute-start(bf16[512,256]{1,0:T(8,128)(2,1)S(1)} %get-tuple-element.55), channel_id=1, source_target_pairs={{0,1},{1,0},{2,3},{3,2},{4,5},{5,4},{6,7},{7,6},{8,9},{9,8},{10,11... | collective-permute-start | bytes 786440 | tf_op jit(solution)/shard_map/ppermute | solution.py:588
  33.0 10.2 %copy-start.7 = (f32[128]{0:T(128)S(1)}, f32[128]{0:T(128)}, u32[]{:S(2)}) copy-start(f32[128]{0:T(128)} %param.26) | copy-start | bytes 1540
  33.1 8.3 %collective-permute-start.9 = (bf16[512,256]{1,0:T(8,128)(2,1)S(1)}, bf16[512,256]{1,0:T(8,128)(2,1)S(1)}, u32[]{:S(2)}, u32[]{:S(2)}) collective-permute-start(bf16[512,256]{1,0:T(8,128)(2,1)S(1)} %add_convert_fusion.5), channel_id=1, source_target_pairs={{0,2},{1,3},{2,0},{3,1},{4,6},{5,7},{6,4},{7,5},{8,10},{9,11},{10,... | collective-permute-start | bytes 786440 | tf_op jit(solution)/shard_map/ppermute | solution.py:588
  34.9 8.3 %collective-permute-start.14 = (bf16[512,256]{1,0:T(8,128)(2,1)S(1)}, bf16[512,256]{1,0:T(8,128)(2,1)S(1)}, u32[]{:S(2)}, u32[]{:S(2)}) collective-permute-start(bf16[512,256]{1,0:T(8,128)(2,1)S(1)} %get-tuple-element.62), channel_id=1, source_target_pairs={{0,1},{1,0},{2,3},{3,2},{4,5},{5,4},{6,7},{7,6},{8,9},{9,8},{10,11... | collective-permute-start | bytes 786440 | tf_op jit(solution)/shard_map/ppermute | solution.py:588
  34.9 10.8 %collective-permute-start.7 = (bf16[512,256]{1,0:T(8,128)(2,1)S(1)}, bf16[512,256]{1,0:T(8,128)(2,1)S(1)}, u32[]{:S(2)}, u32[]{:S(2)}) collective-permute-start(bf16[512,256]{1,0:T(8,128)(2,1)S(1)} %get-tuple-element.53), channel_id=1, source_target_pairs={{0,1},{1,0},{2,3},{3,2},{4,5},{5,4},{6,7},{7,6},{8,9},{9,8},{10,11... | collective-permute-start | bytes 786440 | tf_op jit(solution)/shard_map/ppermute | solution.py:588
  41.4 7.4 %collective-permute-start.10 = (bf16[512,256]{1,0:T(8,128)(2,1)S(1)}, bf16[512,256]{1,0:T(8,128)(2,1)S(1)}, u32[]{:S(2)}, u32[]{:S(2)}) collective-permute-start(bf16[512,256]{1,0:T(8,128)(2,1)S(1)} %add_convert_fusion.3), channel_id=1, source_target_pairs={{0,2},{1,3},{2,0},{3,1},{4,6},{5,7},{6,4},{7,5},{8,10},{9,11},{10,... | collective-permute-start | bytes 786440 | tf_op jit(solution)/shard_map/ppermute | solution.py:588
  44.1 10.0 %collective-permute-start.15 = (bf16[2,128,256]{2,1,0:T(8,128)(2,1)S(1)}, bf16[2,128,256]{2,1,0:T(8,128)(2,1)S(1)}, u32[]{:S(2)}, u32[]{:S(2)}) collective-permute-start(bf16[2,128,256]{2,1,0:T(8,128)(2,1)S(1)} %get-tuple-element.64), channel_id=1, source_target_pairs={{0,4},{4,0},{8,12},{12,8},{1,5},{5,1},{9,13},{13,9},{2,6},{6,2},{1... | collective-permute-start | bytes 393224 | tf_op jit(solution)/shard_map/ppermute | solution.py:707
  45.8 13.0 %collective-permute-start.16 = (bf16[2,128,256]{2,1,0:T(8,128)(2,1)S(1)}, bf16[2,128,256]{2,1,0:T(8,128)(2,1)S(1)}, u32[]{:S(2)}, u32[]{:S(2)}) collective-permute-start(bf16[2,128,256]{2,1,0:T(8,128)(2,1)S(1)} %get-tuple-element.65), channel_id=1, source_target_pairs={{0,8},{4,12},{8,0},{12,4},{1,9},{5,13},{9,1},{13,5},{2,10},{6,14},... | collective-permute-start | bytes 393224 | tf_op jit(solution)/shard_map/ppermute | solution.py:707
  48.4 10.3 %collective-permute-start.17 = (bf16[2,128,256]{2,1,0:T(8,128)(2,1)S(1)}, bf16[2,128,256]{2,1,0:T(8,128)(2,1)S(1)}, u32[]{:S(2)}, u32[]{:S(2)}) collective-permute-start(bf16[2,128,256]{2,1,0:T(8,128)(2,1)S(1)} %get-tuple-element.66), channel_id=1, source_target_pairs={{0,12},{4,8},{8,4},{12,0},{1,13},{5,9},{9,5},{13,1},{2,14},{6,10},... | collective-permute-start | bytes 393224 | tf_op jit(solution)/shard_map/ppermute | solution.py:707
  49.6 12.4 %collective-permute-start.11 = (bf16[2,128,256]{2,1,0:T(8,128)(2,1)S(1)}, bf16[2,128,256]{2,1,0:T(8,128)(2,1)S(1)}, u32[]{:S(2)}, u32[]{:S(2)}) collective-permute-start(bf16[2,128,256]{2,1,0:T(8,128)(2,1)S(1)} %get-tuple-element.58), channel_id=1, source_target_pairs={{0,4},{4,0},{8,12},{12,8},{1,5},{5,1},{9,13},{13,9},{2,6},{6,2},{1... | collective-permute-start | bytes 393224 | tf_op jit(solution)/shard_map/ppermute | solution.py:707
  51.5 17.5 %collective-permute-start.12 = (bf16[2,128,256]{2,1,0:T(8,128)(2,1)S(1)}, bf16[2,128,256]{2,1,0:T(8,128)(2,1)S(1)}, u32[]{:S(2)}, u32[]{:S(2)}) collective-permute-start(bf16[2,128,256]{2,1,0:T(8,128)(2,1)S(1)} %get-tuple-element.59), channel_id=1, source_target_pairs={{0,8},{4,12},{8,0},{12,4},{1,9},{5,13},{9,1},{13,5},{2,10},{6,14},... | collective-permute-start | bytes 393224 | tf_op jit(solution)/shard_map/ppermute | solution.py:707
  54.1 15.0 %collective-permute-start.13 = (bf16[2,128,256]{2,1,0:T(8,128)(2,1)S(1)}, bf16[2,128,256]{2,1,0:T(8,128)(2,1)S(1)}, u32[]{:S(2)}, u32[]{:S(2)}) collective-permute-start(bf16[2,128,256]{2,1,0:T(8,128)(2,1)S(1)} %get-tuple-element.60), channel_id=1, source_target_pairs={{0,12},{4,8},{8,4},{12,0},{1,13},{5,9},{9,5},{13,1},{2,14},{6,10},... | collective-permute-start | bytes 393224 | tf_op jit(solution)/shard_map/ppermute | solution.py:707
  (4 other events, 17.4 us)

commit v4 on v3

--- a/solution.py
+++ b/solution.py
@@ -710,11 +710,11 @@
         terms = kv_terms[head]
         if one_large:
             star = place["star"]
-            picks = tuple((send + d, star) for d in range(group_count))
+            order = (0, 2, 3, 1)
+            picks = tuple((send + d, star) for d in order)
             made = finish_tiles(meta, k_gain, terms, picks)
-            moved = {d: move(made[d], d) for d in (2, 3, 1)}
-            tiles = (made[0],) + tuple(moved[d] for d in (1, 2, 3))
-            sources = tuple((d, group_count + d) for d in range(group_count))
+            tiles = tuple(move(tile, d) if d else tile for tile, d in zip(made, order))
+            sources = tuple((d, group_count + d) for d in order)
         else:
             picks = tuple(
                 tuple(send + s * group_count + d for s in range(slots)) for d in range(group_count)

time: 73.3 us -> 72.4 us (0.988)
  waiting for transfers between devices: 21.1 us -> 18.1 us
  Pallas kernels: 29.6 us -> 31.5 us
    ppermute x6, waiting for transfers between devices: 11.7 us -> 8.56 us  [move(): return lax.ppermute(value, 'grp', xor_pairs(group_count, mask))]
    pallas_call x2, Pallas kernels: 6.76 us -> 8.69 us  [attend_head(): pl.pallas_call(functools.partial(attend_kernel, group_count, sources, hea...]
  transfers between devices with their start and end apart: 18 -> 18, of which waited for: 8 -> 8; matrix products, arithmetic and copies ran while one was open for 2% -> 2% of each run, Pallas kernels for 26% -> 28%
where the time goes in v4:
time: 72.4 us; the launch traced here: 72 us
  Pallas kernels  31.5 us (44%)
  starting transfers between devices  19.3 us (27%)
  waiting for transfers between devices  18.1 us (25%)
  local copies, waits for them, and re-layouts  2.24 us (3%)
    pallas_call x2, Pallas kernels, tap_projection(): pl.pallas_call(functools.partial(tap_kernel, blocks, head_count, dup, len...  10.2 us
    ppermute x6, starting transfers between devices, move(): return lax.ppermute(value, 'grp', xor_pairs(group_count, mask))  9.31 us
    pallas_call x2, Pallas kernels, attend_head(): pl.pallas_call(functools.partial(attend_kernel, group_count, sources, hea...  8.69 us
    ppermute x6, waiting for transfers between devices, move(): return lax.ppermute(value, 'grp', xor_pairs(group_count, mask))  8.56 us
    ppermute x9, waiting for transfers between devices, scatter_sum(): got[k ^ 1 << b] = lax.ppermute(sent, 'tp', pairs)  7.17 us
    ppermute x9, starting transfers between devices, scatter_sum(): got[k ^ 1 << b] = lax.ppermute(sent, 'tp', pairs)  7.02 us
    pallas_call x1, Pallas kernels, encoder_mlp(): pl.pallas_call(functools.partial(mlp_kernel, count, bases, tiles), out_sh...  5.66 us
    ppermute x1, starting transfers between devices, gather_half(): pieces[k | 1 << b] = lax.ppermute(pieces[k], 'tp', pairs)  2.97 us
  transfers between devices with their start and end apart: 18, of which 8 were waited for; matrix products, arithmetic and copies ran while one was open for 2% of the time, Pallas kernels for 28%

profile of v4, /device:TPU:0, one launch (start us, length us, event | category | flops | bytes accessed | tf_op | source)
XLA Modules:
  0.0 72.0 jit_solution(12434227426221426169)
XLA Ops:
  0.0 3.0 %collective-permute-start.1 = (bf16[4,320,128]{2,1,0:T(8,128)(2,1)}, bf16[4,320,128]{2,1,0:T(8,128)(2,1)S(1)}, u32[]{:S(2)}, u32[]{:S(2)}) collective-permute-start(bf16[4,320,128]{2,1,0:T(8,128)(2,1)} %bitcast.20), channel_id=1, source_target_pairs={{0,2},{1,3},{2,0},{3,1},{4,6},{5,7},{6,4},{7,5},{8,10},{9,11},{10,... | collective-permute-start | bytes 983048 | tf_op jit(solution)/shard_map/ppermute | solution.py:601
  3.7 1.4 %copy-done.2 = bf16[4,1,128,1600]{2,3,1,0:T(8,128)(2,1)S(1)} copy-done((bf16[4,1,128,1600]{2,3,1,0:T(8,128)(2,1)S(1)}, bf16[4,1,128,1600]{2,3,1,0:T(8,128)(2,1)}, u32[]{:S(2)}) %copy-start.2) | copy-done | bytes 1638424
  5.2 4.9 %tap_projection.2 = (bf16[3,512,256]{2,1,0:T(8,128)(2,1)S(1)}, bf16[1280,1280]{1,0:T(8,128)(2,1)S(1)}, bf16[1280,1280]{1,0:T(8,128)(2,1)S(1)}, bf16[4,1600,128]{2,1,0:T(8,128)(2,1)S(1)}) custom-call(s32[26]{0:T(128)S(1)} %concatenate.3.where_ref, bf16[4,1600,128]{2,1,0:T(8,128)(2,1)S(1)} %bitcast.19, bf16[1600,2048]{1,0:T(8,128)(2,1)} %weight_hbm.3, ...), custom_call_target="tpu_custom_call" | custom-call | flops 1024 | bytes 1024 | tf_op jit(solution)/shard_map/tap_projection/pallas_call | solution.py:335
  10.9 1.6 %collective-permute-done.2.refs_3_ = bf16[4,320,128]{2,1,0:T(8,128)(2,1)S(1)} collective-permute-done((bf16[4,320,128]{2,1,0:T(8,128)(2,1)S(1)}, bf16[4,320,128]{2,1,0:T(8,128)(2,1)S(1)}, u32[]{:S(2)}, u32[]{:S(2)}) %collective-permute-start.2) | collective-permute-done | bytes 327712 | tf_op jit(solution)/shard_map/ppermute | solution.py:605
  12.5 5.7 %encoder_mlp.1 = (bf16[640,256]{1,0:T(8,128)(2,1)S(1)}, bf16[640,256]{1,0:T(8,128)(2,1)S(1)}, bf16[640,256]{1,0:T(8,128)(2,1)S(1)}, bf16[640,256]{1,0:T(8,128)(2,1)S(1)}) custom-call(s32[26]{0:T(128)S(1)} %concatenate.3.where_ref, bf16[4,320,128]{2,1,0:T(8,128)(2,1)S(1)} %bitcast.22, bf16[4,320,128]{2,1,0:T(8,128)(2,1)S(1)} %collective-permute-done.refs_1_, ...), custom_call_target="tpu_custom_call" | custom-call | flops 1024 | bytes 1024 | tf_op jit(solution)/shard_map/encoder_mlp/pallas_call | solution.py:221
  18.8 1.1 %collective-permute-done.3 = bf16[640,256]{1,0:T(8,128)(2,1)S(1)} collective-permute-done((bf16[640,256]{1,0:T(8,128)(2,1)S(1)}, bf16[640,256]{1,0:T(8,128)(2,1)S(1)}, u32[]{:S(2)}, u32[]{:S(2)}) %collective-permute-start.3) | collective-permute-done | bytes 327712 | tf_op jit(solution)/shard_map/ppermute | solution.py:588
  20.0 1.8 %collective-permute-start.5 = (bf16[640,256]{1,0:T(8,128)(2,1)S(1)}, bf16[640,256]{1,0:T(8,128)(2,1)S(1)}, u32[]{:S(2)}, u32[]{:S(2)}) collective-permute-start(bf16[640,256]{1,0:T(8,128)(2,1)S(1)} %add_convert_fusion.1), channel_id=1, source_target_pairs={{0,2},{1,3},{2,0},{3,1},{4,6},{5,7},{6,4},{7,5},{8,10},{9,11},{10,... | collective-permute-start | bytes 983048 | tf_op jit(solution)/shard_map/ppermute | solution.py:588
  21.8 5.3 %tap_projection.3.refs_2_ = bf16[5,512,256]{2,1,0:T(8,128)(2,1)S(1)} custom-call(s32[26]{0:T(128)S(1)} %concatenate.3.where_ref, bf16[4,1600,128]{2,1,0:T(8,128)(2,1)S(1)} %get-tuple-element.43.tap_hbm, bf16[1600,2048]{1,0:T(8,128)(2,1)} %weight_hbm.3), custom_call_target="tpu_custom_call" | custom-call | flops 1024 | bytes 1024 | tf_op jit(solution)/shard_map/tap_projection/pallas_call | solution.py:335
  27.2 2.6 %collective-permute-done.5.refs_6_ = bf16[640,256]{1,0:T(8,128)(2,1)S(1)} collective-permute-done((bf16[640,256]{1,0:T(8,128)(2,1)S(1)}, bf16[640,256]{1,0:T(8,128)(2,1)S(1)}, u32[]{:S(2)}, u32[]{:S(2)}) %collective-permute-start.5) | collective-permute-done | bytes 327712 | tf_op jit(solution)/shard_map/ppermute | solution.py:588
  29.8 1.3 %kv_projection.2 = (bf16[512,256]{1,0:T(8,128)(2,1)S(1)}, bf16[512,256]{1,0:T(8,128)(2,1)S(1)}, bf16[512,256]{1,0:T(8,128)(2,1)S(1)}, bf16[512,256]{1,0:T(8,128)(2,1)S(1)}, bf16[512,320]{1,0:T(8,128)(2,1)S(1)}) custom-call(s32[26]{0:T(128)S(1)} %concatenate.3.where_ref, bf16[320,2048]{1,0:T(8,128)(2,1)S(1)} %copy-done, ...), custom_call_target="tpu_custom_call" | custom-call | flops 1024 | bytes 1024 | tf_op jit(solution)/shard_map/kv_projection/pallas_call | solution.py:407
  31.2 1.3 %kv_projection.3 = (bf16[512,256]{1,0:T(8,128)(2,1)S(1)}, bf16[512,256]{1,0:T(8,128)(2,1)S(1)}, bf16[512,256]{1,0:T(8,128)(2,1)S(1)}, bf16[512,256]{1,0:T(8,128)(2,1)S(1)}) custom-call(s32[26]{0:T(128)S(1)} %concatenate.3.where_ref, bf16[320,2048]{1,0:T(8,128)(2,1)S(1)} %copy-done, bf16[3,512,256]{2,1,0:T(8,128)(2,1)S(1)} %get-tuple-element.36.refs_1_, ...), custom_call_target="tpu_custom_call" | custom-call | flops 1024 | bytes 1024 | tf_op jit(solution)/shard_map/kv_projection/pallas_call | solution.py:407
  33.1 1.8 %collective-permute-start.9 = (bf16[512,256]{1,0:T(8,128)(2,1)S(1)}, bf16[512,256]{1,0:T(8,128)(2,1)S(1)}, u32[]{:S(2)}, u32[]{:S(2)}) collective-permute-start(bf16[512,256]{1,0:T(8,128)(2,1)S(1)} %add_convert_fusion.5), channel_id=1, source_target_pairs={{0,2},{1,3},{2,0},{3,1},{4,6},{5,7},{6,4},{7,5},{8,10},{9,11},{10,... | collective-permute-start | bytes 786440 | tf_op jit(solution)/shard_map/ppermute | solution.py:588
  35.5 2.8 %prepare.1 = (bf16[512,2048]{1,0:T(8,128)(2,1)S(1)}, s32[24]{0:T(128)S(1)}) custom-call(s32[26]{0:T(128)S(1)} %concatenate.3.where_ref, f32[1,128]{1,0:T(1,128)S(1)} %bitcast.29, bf16[512,2048]{1,0:T(8,128)(2,1)S(1)} %copy-done.1), custom_call_target="tpu_custom_call" | custom-call | flops 1024 | bytes 1024 | tf_op jit(solution)/shard_map/prepare/pallas_call | solution.py:269
  38.3 3.1 %collective-permute-done.9.refs_1_ = bf16[512,256]{1,0:T(8,128)(2,1)S(1)} collective-permute-done((bf16[512,256]{1,0:T(8,128)(2,1)S(1)}, bf16[512,256]{1,0:T(8,128)(2,1)S(1)}, u32[]{:S(2)}, u32[]{:S(2)}) %collective-permute-start.9) | collective-permute-done | bytes 262176 | tf_op jit(solution)/shard_map/ppermute | solution.py:588
  41.4 1.7 %collective-permute-start.10 = (bf16[512,256]{1,0:T(8,128)(2,1)S(1)}, bf16[512,256]{1,0:T(8,128)(2,1)S(1)}, u32[]{:S(2)}, u32[]{:S(2)}) collective-permute-start(bf16[512,256]{1,0:T(8,128)(2,1)S(1)} %add_convert_fusion.3), channel_id=1, source_target_pairs={{0,2},{1,3},{2,0},{3,1},{4,6},{5,7},{6,4},{7,5},{8,10},{9,11},{10,... | collective-permute-start | bytes 786440 | tf_op jit(solution)/shard_map/ppermute | solution.py:588
  43.3 0.8 %finish_tiles.3 = (bf16[2,128,256]{2,1,0:T(8,128)(2,1)S(1)}, bf16[2,128,256]{2,1,0:T(8,128)(2,1)S(1)}, bf16[2,128,256]{2,1,0:T(8,128)(2,1)S(1)}, bf16[2,128,256]{2,1,0:T(8,128)(2,1)S(1)}) custom-call(s32[24]{0:T(128)S(1)} %get-tuple-element.49.meta_ref, f32[1,128]{1,0:T(1,128)S(1)} %bitcast.27, bf16[512,256]{1,0:T(8,128)(2,1)S(1)} %add_convert_fusion.2.refs_0_, ...), custom_call_target="tpu_custom_call" | custom-call | flops 1024 | bytes 1024 | tf_op jit(solution)/shard_map/finish_tiles/pallas_call | solution.py:443
  44.1 2.7 %collective-permute-start.15 = (bf16[2,128,256]{2,1,0:T(8,128)(2,1)S(1)}, bf16[2,128,256]{2,1,0:T(8,128)(2,1)S(1)}, u32[]{:S(2)}, u32[]{:S(2)}) collective-permute-start(bf16[2,128,256]{2,1,0:T(8,128)(2,1)S(1)} %get-tuple-element.64), channel_id=1, source_target_pairs={{0,8},{4,12},{8,0},{12,4},{1,9},{5,13},{9,1},{13,5},{2,10},{6,14},... | collective-permute-start | bytes 393224 | tf_op jit(solution)/shard_map/ppermute | solution.py:707
  46.8 1.4 %collective-permute-start.16 = (bf16[2,128,256]{2,1,0:T(8,128)(2,1)S(1)}, bf16[2,128,256]{2,1,0:T(8,128)(2,1)S(1)}, u32[]{:S(2)}, u32[]{:S(2)}) collective-permute-start(bf16[2,128,256]{2,1,0:T(8,128)(2,1)S(1)} %get-tuple-element.65), channel_id=1, source_target_pairs={{0,12},{4,8},{8,4},{12,0},{1,13},{5,9},{9,5},{13,1},{2,14},{6,10},... | collective-permute-start | bytes 393224 | tf_op jit(solution)/shard_map/ppermute | solution.py:707
  49.6 2.9 %collective-permute-start.11 = (bf16[2,128,256]{2,1,0:T(8,128)(2,1)S(1)}, bf16[2,128,256]{2,1,0:T(8,128)(2,1)S(1)}, u32[]{:S(2)}, u32[]{:S(2)}) collective-permute-start(bf16[2,128,256]{2,1,0:T(8,128)(2,1)S(1)} %get-tuple-element.58), channel_id=1, source_target_pairs={{0,8},{4,12},{8,0},{12,4},{1,9},{5,13},{9,1},{13,5},{2,10},{6,14},... | collective-permute-start | bytes 393224 | tf_op jit(solution)/shard_map/ppermute | solution.py:707
  52.5 1.3 %collective-permute-start.12 = (bf16[2,128,256]{2,1,0:T(8,128)(2,1)S(1)}, bf16[2,128,256]{2,1,0:T(8,128)(2,1)S(1)}, u32[]{:S(2)}, u32[]{:S(2)}) collective-permute-start(bf16[2,128,256]{2,1,0:T(8,128)(2,1)S(1)} %get-tuple-element.59), channel_id=1, source_target_pairs={{0,12},{4,8},{8,4},{12,0},{1,13},{5,9},{9,5},{13,1},{2,14},{6,10},... | collective-permute-start | bytes 393224 | tf_op jit(solution)/shard_map/ppermute | solution.py:707
  53.9 3.0 %collective-permute-done.15.refs_1_ = bf16[2,128,256]{2,1,0:T(8,128)(2,1)S(1)} collective-permute-done((bf16[2,128,256]{2,1,0:T(8,128)(2,1)S(1)}, bf16[2,128,256]{2,1,0:T(8,128)(2,1)S(1)}, u32[]{:S(2)}, u32[]{:S(2)}) %collective-permute-start.15) | collective-permute-done | bytes 131104 | tf_op jit(solution)/shard_map/ppermute | solution.py:707
  57.5 4.2 %attend_head.2.refs_4_ = bf16[512,2048]{1,0:T(8,128)(2,1)} custom-call(s32[24]{0:T(128)S(1)} %get-tuple-element.49.meta_ref, bf16[512,2048]{1,0:T(8,128)(2,1)S(1)} %get-tuple-element.50.query_ref, bf16[2,128,256]{2,1,0:T(8,128)(2,1)S(1)} %get-tuple-element.63.refs_0_, bf16[2,128,256]{2,1,0:T(8,128)(2,1)S(1)} %collective-permute-done.15.refs_1_, ...), custom_call_target="tpu_custom_call" | custom-call | flops 1024 | bytes 1024 | tf_op jit(solution)/shard_map/attend_head/pallas_call | solution.py:551
  61.8 5.6 %collective-permute-done.11.refs_1_ = bf16[2,128,256]{2,1,0:T(8,128)(2,1)S(1)} collective-permute-done((bf16[2,128,256]{2,1,0:T(8,128)(2,1)S(1)}, bf16[2,128,256]{2,1,0:T(8,128)(2,1)S(1)}, u32[]{:S(2)}, u32[]{:S(2)}) %collective-permute-start.11) | collective-permute-done | bytes 131104 | tf_op jit(solution)/shard_map/ppermute | solution.py:707
  67.4 4.5 %attend_head.3 = bf16[512,2048]{1,0:T(8,128)(2,1)} custom-call(s32[24]{0:T(128)S(1)} %get-tuple-element.49.meta_ref, bf16[512,2048]{1,0:T(8,128)(2,1)S(1)} %get-tuple-element.50.query_ref, bf16[2,128,256]{2,1,0:T(8,128)(2,1)S(1)} %get-tuple-element.57.refs_0_, ...), custom_call_target="tpu_custom_call", output_to_operand_aliasing={{}: (6, {})} | custom-call | flops 1024 | bytes 1024 | tf_op jit(solution)/shard_map/attend_head/pallas_call | solution.py:551
  (50 shorter events, 5.8 us)
Async XLA Ops:
  0.0 10.9 %collective-permute-start.1 = (bf16[4,320,128]{2,1,0:T(8,128)(2,1)}, bf16[4,320,128]{2,1,0:T(8,128)(2,1)S(1)}, u32[]{:S(2)}, u32[]{:S(2)}) collective-permute-start(bf16[4,320,128]{2,1,0:T(8,128)(2,1)} %bitcast.20), channel_id=1, source_target_pairs={{0,2},{1,3},{2,0},{3,1},{4,6},{5,7},{6,4},{7,5},{8,10},{9,11},{10,... | collective-permute-start | bytes 983048 | tf_op jit(solution)/shard_map/ppermute | solution.py:601
  3.0 7.9 %collective-permute-start = (bf16[4,320,128]{2,1,0:T(8,128)(2,1)}, bf16[4,320,128]{2,1,0:T(8,128)(2,1)S(1)}, u32[]{:S(2)}, u32[]{:S(2)}) collective-permute-start(bf16[4,320,128]{2,1,0:T(8,128)(2,1)} %bitcast.21), channel_id=1, source_target_pairs={{0,1},{1,0},{2,3},{3,2},{4,5},{5,4},{6,7},{7,6},{8,9},{9,8},{10,11... | collective-permute-start | bytes 983048 | tf_op jit(solution)/shard_map/ppermute | solution.py:646
  5.2 7.4 %copy-start.4 = (f32[1280]{0:T(1024)S(1)}, f32[1280]{0:T(1024)}, u32[]{:S(2)}) copy-start(f32[1280]{0:T(1024)} %param.18) | copy-start | bytes 15364
  5.2 7.4 %copy-start.5 = (f32[1280]{0:T(1024)S(1)}, f32[1280]{0:T(1024)}, u32[]{:S(2)}) copy-start(f32[1280]{0:T(1024)} %param.19) | copy-start | bytes 15364
  5.2 7.4 %copy-start.6 = (f32[1280]{0:T(1024)S(1)}, f32[1280]{0:T(1024)}, u32[]{:S(2)}) copy-start(f32[1280]{0:T(1024)} %param.21) | copy-start | bytes 15364
  10.9 1.6 %collective-permute-start.2 = (bf16[4,320,128]{2,1,0:T(8,128)(2,1)S(1)}, bf16[4,320,128]{2,1,0:T(8,128)(2,1)S(1)}, u32[]{:S(2)}, u32[]{:S(2)}) collective-permute-start(bf16[4,320,128]{2,1,0:T(8,128)(2,1)S(1)} %collective-permute-done.1.refs_2_), channel_id=1, source_target_pairs={{0,1},{1,0},{2,3},{3,2},{4,5},{5,4},{6,7},{7,6},{8,9},{9,8},{10,11... | collective-permute-start | bytes 983048 | tf_op jit(solution)/shard_map/ppermute | solution.py:605
  12.5 9.2 %copy-start.9 = (f32[320]{0:T(512)S(1)}, f32[320]{0:T(512)}, u32[]{:S(2)}) copy-start(f32[320]{0:T(512)} %param.23) | copy-start | bytes 3844
  18.2 1.7 %collective-permute-start.3 = (bf16[640,256]{1,0:T(8,128)(2,1)S(1)}, bf16[640,256]{1,0:T(8,128)(2,1)S(1)}, u32[]{:S(2)}, u32[]{:S(2)}) collective-permute-start(bf16[640,256]{1,0:T(8,128)(2,1)S(1)} %get-tuple-element.41), channel_id=1, source_target_pairs={{0,1},{1,0},{2,3},{3,2},{4,5},{5,4},{6,7},{7,6},{8,9},{9,8},{10,11... | collective-permute-start | bytes 983048 | tf_op jit(solution)/shard_map/ppermute | solution.py:588
  18.4 8.7 %collective-permute-start.4 = (bf16[640,256]{1,0:T(8,128)(2,1)S(1)}, bf16[640,256]{1,0:T(8,128)(2,1)S(1)}, u32[]{:S(2)}, u32[]{:S(2)}) collective-permute-start(bf16[640,256]{1,0:T(8,128)(2,1)S(1)} %get-tuple-element.45), channel_id=1, source_target_pairs={{0,1},{1,0},{2,3},{3,2},{4,5},{5,4},{6,7},{7,6},{8,9},{9,8},{10,11... | collective-permute-start | bytes 983048 | tf_op jit(solution)/shard_map/ppermute | solution.py:588
  20.0 9.8 %collective-permute-start.5 = (bf16[640,256]{1,0:T(8,128)(2,1)S(1)}, bf16[640,256]{1,0:T(8,128)(2,1)S(1)}, u32[]{:S(2)}, u32[]{:S(2)}) collective-permute-start(bf16[640,256]{1,0:T(8,128)(2,1)S(1)} %add_convert_fusion.1), channel_id=1, source_target_pairs={{0,2},{1,3},{2,0},{3,1},{4,6},{5,7},{6,4},{7,5},{8,10},{9,11},{10,... | collective-permute-start | bytes 983048 | tf_op jit(solution)/shard_map/ppermute | solution.py:588
  21.8 8.0 %copy-start = (bf16[320,2048]{1,0:T(8,128)(2,1)S(1)}, bf16[320,2048]{1,0:T(8,128)(2,1)}, u32[]{:S(2)}) copy-start(bf16[320,2048]{1,0:T(8,128)(2,1)} %refs_0_.5) | copy-start | bytes 3932164
  31.1 1.9 %collective-permute-start.6 = (bf16[512,256]{1,0:T(8,128)(2,1)S(1)}, bf16[512,256]{1,0:T(8,128)(2,1)S(1)}, u32[]{:S(2)}, u32[]{:S(2)}) collective-permute-start(bf16[512,256]{1,0:T(8,128)(2,1)S(1)} %get-tuple-element.47), channel_id=1, source_target_pairs={{0,1},{1,0},{2,3},{3,2},{4,5},{5,4},{6,7},{7,6},{8,9},{9,8},{10,11... | collective-permute-start | bytes 786440 | tf_op jit(solution)/shard_map/ppermute | solution.py:588
  32.5 2.9 %collective-permute-start.8 = (bf16[512,256]{1,0:T(8,128)(2,1)S(1)}, bf16[512,256]{1,0:T(8,128)(2,1)S(1)}, u32[]{:S(2)}, u32[]{:S(2)}) collective-permute-start(bf16[512,256]{1,0:T(8,128)(2,1)S(1)} %get-tuple-element.55), channel_id=1, source_target_pairs={{0,1},{1,0},{2,3},{3,2},{4,5},{5,4},{6,7},{7,6},{8,9},{9,8},{10,11... | collective-permute-start | bytes 786440 | tf_op jit(solution)/shard_map/ppermute | solution.py:588
  33.0 10.2 %copy-start.7 = (f32[128]{0:T(128)S(1)}, f32[128]{0:T(128)}, u32[]{:S(2)}) copy-start(f32[128]{0:T(128)} %param.26) | copy-start | bytes 1540
  33.1 8.3 %collective-permute-start.9 = (bf16[512,256]{1,0:T(8,128)(2,1)S(1)}, bf16[512,256]{1,0:T(8,128)(2,1)S(1)}, u32[]{:S(2)}, u32[]{:S(2)}) collective-permute-start(bf16[512,256]{1,0:T(8,128)(2,1)S(1)} %add_convert_fusion.5), channel_id=1, source_target_pairs={{0,2},{1,3},{2,0},{3,1},{4,6},{5,7},{6,4},{7,5},{8,10},{9,11},{10,... | collective-permute-start | bytes 786440 | tf_op jit(solution)/shard_map/ppermute | solution.py:588
  34.9 8.3 %collective-permute-start.14 = (bf16[512,256]{1,0:T(8,128)(2,1)S(1)}, bf16[512,256]{1,0:T(8,128)(2,1)S(1)}, u32[]{:S(2)}, u32[]{:S(2)}) collective-permute-start(bf16[512,256]{1,0:T(8,128)(2,1)S(1)} %get-tuple-element.62), channel_id=1, source_target_pairs={{0,1},{1,0},{2,3},{3,2},{4,5},{5,4},{6,7},{7,6},{8,9},{9,8},{10,11... | collective-permute-start | bytes 786440 | tf_op jit(solution)/shard_map/ppermute | solution.py:588
  34.9 11.8 %collective-permute-start.7 = (bf16[512,256]{1,0:T(8,128)(2,1)S(1)}, bf16[512,256]{1,0:T(8,128)(2,1)S(1)}, u32[]{:S(2)}, u32[]{:S(2)}) collective-permute-start(bf16[512,256]{1,0:T(8,128)(2,1)S(1)} %get-tuple-element.53), channel_id=1, source_target_pairs={{0,1},{1,0},{2,3},{3,2},{4,5},{5,4},{6,7},{7,6},{8,9},{9,8},{10,11... | collective-permute-start | bytes 786440 | tf_op jit(solution)/shard_map/ppermute | solution.py:588
  41.4 7.4 %collective-permute-start.10 = (bf16[512,256]{1,0:T(8,128)(2,1)S(1)}, bf16[512,256]{1,0:T(8,128)(2,1)S(1)}, u32[]{:S(2)}, u32[]{:S(2)}) collective-permute-start(bf16[512,256]{1,0:T(8,128)(2,1)S(1)} %add_convert_fusion.3), channel_id=1, source_target_pairs={{0,2},{1,3},{2,0},{3,1},{4,6},{5,7},{6,4},{7,5},{8,10},{9,11},{10,... | collective-permute-start | bytes 786440 | tf_op jit(solution)/shard_map/ppermute | solution.py:588
  44.1 12.8 %collective-permute-start.15 = (bf16[2,128,256]{2,1,0:T(8,128)(2,1)S(1)}, bf16[2,128,256]{2,1,0:T(8,128)(2,1)S(1)}, u32[]{:S(2)}, u32[]{:S(2)}) collective-permute-start(bf16[2,128,256]{2,1,0:T(8,128)(2,1)S(1)} %get-tuple-element.64), channel_id=1, source_target_pairs={{0,8},{4,12},{8,0},{12,4},{1,9},{5,13},{9,1},{13,5},{2,10},{6,14},... | collective-permute-start | bytes 393224 | tf_op jit(solution)/shard_map/ppermute | solution.py:707
  46.8 10.7 %collective-permute-start.16 = (bf16[2,128,256]{2,1,0:T(8,128)(2,1)S(1)}, bf16[2,128,256]{2,1,0:T(8,128)(2,1)S(1)}, u32[]{:S(2)}, u32[]{:S(2)}) collective-permute-start(bf16[2,128,256]{2,1,0:T(8,128)(2,1)S(1)} %get-tuple-element.65), channel_id=1, source_target_pairs={{0,12},{4,8},{8,4},{12,0},{1,13},{5,9},{9,5},{13,1},{2,14},{6,10},... | collective-permute-start | bytes 393224 | tf_op jit(solution)/shard_map/ppermute | solution.py:707
  48.2 9.3 %collective-permute-start.17 = (bf16[2,128,256]{2,1,0:T(8,128)(2,1)S(1)}, bf16[2,128,256]{2,1,0:T(8,128)(2,1)S(1)}, u32[]{:S(2)}, u32[]{:S(2)}) collective-permute-start(bf16[2,128,256]{2,1,0:T(8,128)(2,1)S(1)} %get-tuple-element.66), channel_id=1, source_target_pairs={{0,4},{4,0},{8,12},{12,8},{1,5},{5,1},{9,13},{13,9},{2,6},{6,2},{1... | collective-permute-start | bytes 393224 | tf_op jit(solution)/shard_map/ppermute | solution.py:707
  49.6 17.7 %collective-permute-start.11 = (bf16[2,128,256]{2,1,0:T(8,128)(2,1)S(1)}, bf16[2,128,256]{2,1,0:T(8,128)(2,1)S(1)}, u32[]{:S(2)}, u32[]{:S(2)}) collective-permute-start(bf16[2,128,256]{2,1,0:T(8,128)(2,1)S(1)} %get-tuple-element.58), channel_id=1, source_target_pairs={{0,8},{4,12},{8,0},{12,4},{1,9},{5,13},{9,1},{13,5},{2,10},{6,14},... | collective-permute-start | bytes 393224 | tf_op jit(solution)/shard_map/ppermute | solution.py:707
  52.5 14.9 %collective-permute-start.12 = (bf16[2,128,256]{2,1,0:T(8,128)(2,1)S(1)}, bf16[2,128,256]{2,1,0:T(8,128)(2,1)S(1)}, u32[]{:S(2)}, u32[]{:S(2)}) collective-permute-start(bf16[2,128,256]{2,1,0:T(8,128)(2,1)S(1)} %get-tuple-element.59), channel_id=1, source_target_pairs={{0,12},{4,8},{8,4},{12,0},{1,13},{5,9},{9,5},{13,1},{2,14},{6,10},... | collective-permute-start | bytes 393224 | tf_op jit(solution)/shard_map/ppermute | solution.py:707
  56.8 10.6 %collective-permute-start.13 = (bf16[2,128,256]{2,1,0:T(8,128)(2,1)S(1)}, bf16[2,128,256]{2,1,0:T(8,128)(2,1)S(1)}, u32[]{:S(2)}, u32[]{:S(2)}) collective-permute-start(bf16[2,128,256]{2,1,0:T(8,128)(2,1)S(1)} %get-tuple-element.60), channel_id=1, source_target_pairs={{0,4},{4,0},{8,12},{12,8},{1,5},{5,1},{9,13},{13,9},{2,6},{6,2},{1... | collective-permute-start | bytes 393224 | tf_op jit(solution)/shard_map/ppermute | solution.py:707
  (4 other events, 17.4 us)

commit v5 on v4

--- a/solution.py
+++ b/solution.py
@@ -16,7 +16,7 @@
 ROW_BLOCK = 128
 HIDDEN_BLOCK = 256
 HEAD_GROUP = 8
-HALVES = 1
+HALVES = 2
 TAPS_EARLY = 3
 VALUE_SHIFT = 2.0**-24
 epsilon = 1e-05
@@ -162,7 +162,7 @@
     }
 
 
-def mlp_kernel(piece_count, bases, tiles, where_ref, *refs):
+def mlp_kernel(piece_count, base, tiles, where_ref, *refs):
     pieces = refs[:piece_count]
     gain_ref, bias_ref, up_bias_ref, up_ref, down_ref = refs[piece_count : piece_count + 5]
     outs = refs[piece_count + 5 : 2 * piece_count + 5]
@@ -179,7 +179,7 @@
     for tile in range(tiles):
         for k, piece in enumerate(pieces):
             start = pl.multiple_of((index ^ k) * width, math.gcd(width, LANES))
-            cat_ref[pl.ds(start, width), :] = piece[bases[k] + tile]
+            cat_ref[pl.ds(start, width), :] = piece[base + tile]
         values = cat_ref[...].T.astype(F32)
         average = jnp.sum(values, axis=1, keepdims=True) * (1.0 / channels)
         centered = values - average
@@ -212,14 +212,14 @@
                 out[take, :] = block
 
 
-def encoder_mlp(where, pieces, bases, tiles, ln_gain, ln_bias, w_up, b_up, w_down):
+def encoder_mlp(where, pieces, base, tiles, ln_gain, ln_bias, w_up, b_up, w_down):
     _, width, tile_rows = pieces[0].shape
     rows = tiles * tile_rows
     count = len(pieces)
     channels, hidden_width = w_up.shape
     shape = sent_shape(rows, width)
     return pl.pallas_call(
-        functools.partial(mlp_kernel, count, bases, tiles),
+        functools.partial(mlp_kernel, count, base, tiles),
         out_shape=[jax.ShapeDtypeStruct(shape, BF16)] * count,
         in_specs=[SMEM] + [VMEM] * (count + 5),
         out_specs=[VMEM] * count,
@@ -592,9 +592,9 @@
     return [blocks[0]], blocks[0]
 
 
-def gather_half(whole, own, first, count, ready):
+def gather_pieces(whole, count, ready):
     bits = bits_of(count)
-    pieces = {0: own}
+    pieces = {0: whole[0]}
     for b in reversed(range(1, bits)):
         pairs = xor_pairs(count, 1 << b)
         for k in sorted(pieces):
@@ -604,8 +604,7 @@
         if k:
             pieces[k | 1] = lax.ppermute(after(pieces[k], ready), "tp", pairs)
     pieces[0], pieces[1] = whole
-    bases = tuple(first if k < 2 else 0 for k in range(count))
-    return [pieces[k] for k in range(count)], bases
+    return [pieces[k] for k in range(count)]
 
 
 def local(
@@ -640,9 +639,6 @@
 
     halves = HALVES if tiles_local % HALVES == 0 else 1
     tiles = tiles_local // halves
-    own_halves = [x_tiles[:tiles]] + [
-        after(x_tiles, where)[h * tiles : (h + 1) * tiles] for h in range(1, halves)
-    ]
     whole = [x_tiles, lax.ppermute(x_tiles, "tp", xor_pairs(tp_count, 1))]
 
     tap_blocks = [(h, k) for h in range(head_count) for k in range(dest_count)]
@@ -650,16 +646,15 @@
     first_taps, w_up, w_down, tap_tiles = tap_projection(
         where, tap_tiles, kv_w_taps, tap_blocks[:early], head_count, dup, (w_up, w_down)
     )
-    mlp_terms = []
-    ready, begun = first_taps, where
+    pieces = gather_pieces(whole, tp_count, first_taps)
+    mlp_terms, begun = [], where
     for half in range(halves):
-        pieces, bases = gather_half(whole, own_halves[half], half * tiles, tp_count, ready)
         mlp_blocks = encoder_mlp(
-            begun, pieces, bases, tiles, ln_gain, ln_bias, w_up, b_up, w_down
+            begun, pieces, half * tiles, tiles, ln_gain, ln_bias, w_up, b_up, w_down
         )
         terms, sent = scatter_sum(mlp_blocks, tp_count, 0)
         mlp_terms.append(terms)
-        ready, begun = mlp_blocks[0], after(where, sent)
+        begun = after(where, sent)
     (last_taps,) = tap_projection(
         begun, tap_tiles, kv_w_taps, tap_blocks[early:], head_count, dup, ()
     )

time: 72.4 us -> 72.8 us (level); the launches traced: 72 us -> 71.4 us
  waiting for transfers between devices: 18.1 us -> 19.2 us
  Pallas kernels: 31.5 us -> 30.6 us
  starting transfers between devices: 19.3 us -> 18.5 us
    pallas_call x2, Pallas kernels: 8.69 us -> 6.68 us  [attend_head(): pl.pallas_call(functools.partial(attend_kernel, group_count, sources, hea...]
    pallas_call x1 -> x2, Pallas kernels: 5.66 us -> 6.88 us  [encoder_mlp(): pl.pallas_call(functools.partial(mlp_kernel, count, base, tiles), out_sha...]
    ppermute x9 -> x12, waiting for transfers between devices: 7.17 us -> 7.72 us  [scatter_sum(): got[k ^ 1 << b] = lax.ppermute(sent, 'tp', pairs)]
    ppermute x9 -> x12, starting transfers between devices: 7.02 us -> 6.49 us  [scatter_sum(): got[k ^ 1 << b] = lax.ppermute(sent, 'tp', pairs)]
  transfers between devices with their start and end apart: 18 -> 21, of which waited for: 8 -> 9; matrix products, arithmetic and copies ran while one was open for 2% -> 2% of each run, Pallas kernels for 28% -> 31%
where the time goes in v5:
time: 72.8 us; the launch traced here: 71.4 us
  Pallas kernels  30.6 us (42%)
  waiting for transfers between devices  19.2 us (26%)
  starting transfers between devices  18.5 us (25%)
  local copies, waits for them, and re-layouts  2.24 us (3%)
    pallas_call x2, Pallas kernels, tap_projection(): pl.pallas_call(functools.partial(tap_kernel, blocks, head_count, dup, len...  10.2 us
    ppermute x6, waiting for transfers between devices, move(): return lax.ppermute(value, 'grp', xor_pairs(group_count, mask))  9.1 us
    ppermute x6, starting transfers between devices, move(): return lax.ppermute(value, 'grp', xor_pairs(group_count, mask))  9.06 us
    ppermute x12, waiting for transfers between devices, scatter_sum(): got[k ^ 1 << b] = lax.ppermute(sent, 'tp', pairs)  7.72 us
    pallas_call x2, Pallas kernels, encoder_mlp(): pl.pallas_call(functools.partial(mlp_kernel, count, base, tiles), out_sha...  6.88 us
    pallas_call x2, Pallas kernels, attend_head(): pl.pallas_call(functools.partial(attend_kernel, group_count, sources, hea...  6.68 us
    ppermute x12, starting transfers between devices, scatter_sum(): got[k ^ 1 << b] = lax.ppermute(sent, 'tp', pairs)  6.49 us
    ppermute x1, starting transfers between devices, gather_pieces(): pieces[k | 1 << b] = lax.ppermute(pieces[k], 'tp', pairs)  2.97 us
  transfers between devices with their start and end apart: 21, of which 9 were waited for; matrix products, arithmetic and copies ran while one was open for 2% of the time, Pallas kernels for 31%

profile of v5, /device:TPU:0, one launch (start us, length us, event | category | flops | bytes accessed | tf_op | source)
XLA Modules:
  0.0 71.4 jit_solution(10323785441341495530)
XLA Ops:
  0.0 3.0 %collective-permute-start.1 = (bf16[4,320,128]{2,1,0:T(8,128)(2,1)}, bf16[4,320,128]{2,1,0:T(8,128)(2,1)S(1)}, u32[]{:S(2)}, u32[]{:S(2)}) collective-permute-start(bf16[4,320,128]{2,1,0:T(8,128)(2,1)} %bitcast.19), channel_id=1, source_target_pairs={{0,2},{1,3},{2,0},{3,1},{4,6},{5,7},{6,4},{7,5},{8,10},{9,11},{10,... | collective-permute-start | bytes 983048 | tf_op jit(solution)/shard_map/ppermute | solution.py:601
  3.7 1.4 %copy-done.3 = bf16[4,1,128,1600]{2,3,1,0:T(8,128)(2,1)S(1)} copy-done((bf16[4,1,128,1600]{2,3,1,0:T(8,128)(2,1)S(1)}, bf16[4,1,128,1600]{2,3,1,0:T(8,128)(2,1)}, u32[]{:S(2)}) %copy-start.3) | copy-done | bytes 1638424
  5.2 4.9 %tap_projection.2 = (bf16[3,512,256]{2,1,0:T(8,128)(2,1)S(1)}, bf16[1280,1280]{1,0:T(8,128)(2,1)S(1)}, bf16[1280,1280]{1,0:T(8,128)(2,1)S(1)}, bf16[4,1600,128]{2,1,0:T(8,128)(2,1)S(1)}) custom-call(s32[26]{0:T(128)S(1)} %concatenate.3.where_ref, bf16[4,1600,128]{2,1,0:T(8,128)(2,1)S(1)} %bitcast.24, bf16[1600,2048]{1,0:T(8,128)(2,1)} %weight_hbm.3, ...), custom_call_target="tpu_custom_call" | custom-call | flops 1024 | bytes 1024 | tf_op jit(solution)/shard_map/tap_projection/pallas_call | solution.py:335
  10.9 1.6 %collective-permute-done.2.refs_3_ = bf16[4,320,128]{2,1,0:T(8,128)(2,1)S(1)} collective-permute-done((bf16[4,320,128]{2,1,0:T(8,128)(2,1)S(1)}, bf16[4,320,128]{2,1,0:T(8,128)(2,1)S(1)}, u32[]{:S(2)}, u32[]{:S(2)}) %collective-permute-start.2) | collective-permute-done | bytes 327712 | tf_op jit(solution)/shard_map/ppermute | solution.py:605
  12.5 3.5 %encoder_mlp.2 = (bf16[320,256]{1,0:T(8,128)(2,1)S(1)}, bf16[320,256]{1,0:T(8,128)(2,1)S(1)}, bf16[320,256]{1,0:T(8,128)(2,1)S(1)}, bf16[320,256]{1,0:T(8,128)(2,1)S(1)}) custom-call(s32[26]{0:T(128)S(1)} %concatenate.3.where_ref, bf16[4,320,128]{2,1,0:T(8,128)(2,1)S(1)} %bitcast.21, bf16[4,320,128]{2,1,0:T(8,128)(2,1)S(1)} %collective-permute-done.refs_1_, ...), custom_call_target="tpu_custom_call" | custom-call | flops 1024 | bytes 1024 | tf_op jit(solution)/shard_map/encoder_mlp/pallas_call | solution.py:221
  17.5 1.8 %collective-permute-start.6 = (bf16[320,256]{1,0:T(8,128)(2,1)S(1)}, bf16[320,256]{1,0:T(8,128)(2,1)S(1)}, u32[]{:S(2)}, u32[]{:S(2)}) collective-permute-start(bf16[320,256]{1,0:T(8,128)(2,1)S(1)} %add_convert_fusion.7), channel_id=1, source_target_pairs={{0,2},{1,3},{2,0},{3,1},{4,6},{5,7},{6,4},{7,5},{8,10},{9,11},{10,... | collective-permute-start | bytes 491528 | tf_op jit(solution)/shard_map/ppermute | solution.py:588
  19.3 3.4 %encoder_mlp.3 = (bf16[320,256]{1,0:T(8,128)(2,1)S(1)}, bf16[320,256]{1,0:T(8,128)(2,1)S(1)}, bf16[320,256]{1,0:T(8,128)(2,1)S(1)}, bf16[320,256]{1,0:T(8,128)(2,1)S(1)}) custom-call(s32[26]{0:T(128)S(1)} %concatenate.3.where_ref, bf16[4,320,128]{2,1,0:T(8,128)(2,1)S(1)} %bitcast.22, bf16[4,320,128]{2,1,0:T(8,128)(2,1)S(1)} %collective-permute-done.refs_1_, ...), custom_call_target="tpu_custom_call" | custom-call | flops 1024 | bytes 1024 | tf_op jit(solution)/shard_map/encoder_mlp/pallas_call | solution.py:221
  23.3 1.1 %collective-permute-done.4 = bf16[320,256]{1,0:T(8,128)(2,1)S(1)} collective-permute-done((bf16[320,256]{1,0:T(8,128)(2,1)S(1)}, bf16[320,256]{1,0:T(8,128)(2,1)S(1)}, u32[]{:S(2)}, u32[]{:S(2)}) %collective-permute-start.4) | collective-permute-done | bytes 163872 | tf_op jit(solution)/shard_map/ppermute | solution.py:588
  24.8 5.3 %tap_projection.3.refs_2_ = bf16[5,512,256]{2,1,0:T(8,128)(2,1)S(1)} custom-call(s32[26]{0:T(128)S(1)} %concatenate.3.where_ref, bf16[4,1600,128]{2,1,0:T(8,128)(2,1)S(1)} %get-tuple-element.51.tap_hbm, bf16[1600,2048]{1,0:T(8,128)(2,1)} %weight_hbm.3), custom_call_target="tpu_custom_call" | custom-call | flops 1024 | bytes 1024 | tf_op jit(solution)/shard_map/tap_projection/pallas_call | solution.py:335
  30.9 1.3 %kv_projection.2 = (bf16[512,256]{1,0:T(8,128)(2,1)S(1)}, bf16[512,256]{1,0:T(8,128)(2,1)S(1)}, bf16[512,256]{1,0:T(8,128)(2,1)S(1)}, bf16[512,256]{1,0:T(8,128)(2,1)S(1)}, bf16[512,320]{1,0:T(8,128)(2,1)S(1)}) custom-call(s32[26]{0:T(128)S(1)} %concatenate.3.where_ref, bf16[320,2048]{1,0:T(8,128)(2,1)S(1)} %copy-done, ...), custom_call_target="tpu_custom_call" | custom-call | flops 1024 | bytes 1024 | tf_op jit(solution)/shard_map/kv_projection/pallas_call | solution.py:407
  32.3 1.3 %kv_projection.3 = (bf16[512,256]{1,0:T(8,128)(2,1)S(1)}, bf16[512,256]{1,0:T(8,128)(2,1)S(1)}, bf16[512,256]{1,0:T(8,128)(2,1)S(1)}, bf16[512,256]{1,0:T(8,128)(2,1)S(1)}) custom-call(s32[26]{0:T(128)S(1)} %concatenate.3.where_ref, bf16[320,2048]{1,0:T(8,128)(2,1)S(1)} %copy-done, bf16[3,512,256]{2,1,0:T(8,128)(2,1)S(1)} %get-tuple-element.41.refs_1_, ...), custom_call_target="tpu_custom_call" | custom-call | flops 1024 | bytes 1024 | tf_op jit(solution)/shard_map/kv_projection/pallas_call | solution.py:407
  34.2 1.1 %collective-permute-start.12 = (bf16[512,256]{1,0:T(8,128)(2,1)S(1)}, bf16[512,256]{1,0:T(8,128)(2,1)S(1)}, u32[]{:S(2)}, u32[]{:S(2)}) collective-permute-start(bf16[512,256]{1,0:T(8,128)(2,1)S(1)} %add_convert_fusion.3), channel_id=1, source_target_pairs={{0,2},{1,3},{2,0},{3,1},{4,6},{5,7},{6,4},{7,5},{8,10},{9,11},{10,... | collective-permute-start | bytes 786440 | tf_op jit(solution)/shard_map/ppermute | solution.py:588
  35.9 2.6 %prepare.1 = (bf16[512,2048]{1,0:T(8,128)(2,1)S(1)}, s32[24]{0:T(128)S(1)}) custom-call(s32[26]{0:T(128)S(1)} %concatenate.3.where_ref, f32[1,128]{1,0:T(1,128)S(1)} %bitcast.33, bf16[512,2048]{1,0:T(8,128)(2,1)S(1)} %copy-done.2), custom_call_target="tpu_custom_call" | custom-call | flops 1024 | bytes 1024 | tf_op jit(solution)/shard_map/prepare/pallas_call | solution.py:269
  38.5 4.0 %collective-permute-done.12.refs_1_ = bf16[512,256]{1,0:T(8,128)(2,1)S(1)} collective-permute-done((bf16[512,256]{1,0:T(8,128)(2,1)S(1)}, bf16[512,256]{1,0:T(8,128)(2,1)S(1)}, u32[]{:S(2)}, u32[]{:S(2)}) %collective-permute-start.12) | collective-permute-done | bytes 262176 | tf_op jit(solution)/shard_map/ppermute | solution.py:588
  42.5 1.0 %collective-permute-start.13 = (bf16[512,256]{1,0:T(8,128)(2,1)S(1)}, bf16[512,256]{1,0:T(8,128)(2,1)S(1)}, u32[]{:S(2)}, u32[]{:S(2)}) collective-permute-start(bf16[512,256]{1,0:T(8,128)(2,1)S(1)} %add_convert_fusion.1), channel_id=1, source_target_pairs={{0,2},{1,3},{2,0},{3,1},{4,6},{5,7},{6,4},{7,5},{8,10},{9,11},{10,... | collective-permute-start | bytes 786440 | tf_op jit(solution)/shard_map/ppermute | solution.py:588
  44.4 2.6 %collective-permute-start.18 = (bf16[2,128,256]{2,1,0:T(8,128)(2,1)S(1)}, bf16[2,128,256]{2,1,0:T(8,128)(2,1)S(1)}, u32[]{:S(2)}, u32[]{:S(2)}) collective-permute-start(bf16[2,128,256]{2,1,0:T(8,128)(2,1)S(1)} %get-tuple-element.74), channel_id=1, source_target_pairs={{0,8},{4,12},{8,0},{12,4},{1,9},{5,13},{9,1},{13,5},{2,10},{6,14},... | collective-permute-start | bytes 393224 | tf_op jit(solution)/shard_map/ppermute | solution.py:702
  47.2 1.4 %collective-permute-start.19 = (bf16[2,128,256]{2,1,0:T(8,128)(2,1)S(1)}, bf16[2,128,256]{2,1,0:T(8,128)(2,1)S(1)}, u32[]{:S(2)}, u32[]{:S(2)}) collective-permute-start(bf16[2,128,256]{2,1,0:T(8,128)(2,1)S(1)} %get-tuple-element.75), channel_id=1, source_target_pairs={{0,12},{4,8},{8,4},{12,0},{1,13},{5,9},{9,5},{13,1},{2,14},{6,10},... | collective-permute-start | bytes 393224 | tf_op jit(solution)/shard_map/ppermute | solution.py:702
  48.9 1.0 %collective-permute-done.13.refs_1_ = bf16[512,256]{1,0:T(8,128)(2,1)S(1)} collective-permute-done((bf16[512,256]{1,0:T(8,128)(2,1)S(1)}, bf16[512,256]{1,0:T(8,128)(2,1)S(1)}, u32[]{:S(2)}, u32[]{:S(2)}) %collective-permute-start.13) | collective-permute-done | bytes 262176 | tf_op jit(solution)/shard_map/ppermute | solution.py:588
  50.7 2.6 %collective-permute-start.14 = (bf16[2,128,256]{2,1,0:T(8,128)(2,1)S(1)}, bf16[2,128,256]{2,1,0:T(8,128)(2,1)S(1)}, u32[]{:S(2)}, u32[]{:S(2)}) collective-permute-start(bf16[2,128,256]{2,1,0:T(8,128)(2,1)S(1)} %get-tuple-element.68), channel_id=1, source_target_pairs={{0,8},{4,12},{8,0},{12,4},{1,9},{5,13},{9,1},{13,5},{2,10},{6,14},... | collective-permute-start | bytes 393224 | tf_op jit(solution)/shard_map/ppermute | solution.py:702
  53.4 1.4 %collective-permute-start.15 = (bf16[2,128,256]{2,1,0:T(8,128)(2,1)S(1)}, bf16[2,128,256]{2,1,0:T(8,128)(2,1)S(1)}, u32[]{:S(2)}, u32[]{:S(2)}) collective-permute-start(bf16[2,128,256]{2,1,0:T(8,128)(2,1)S(1)} %get-tuple-element.69), channel_id=1, source_target_pairs={{0,12},{4,8},{8,4},{12,0},{1,13},{5,9},{9,5},{13,1},{2,14},{6,10},... | collective-permute-start | bytes 393224 | tf_op jit(solution)/shard_map/ppermute | solution.py:702
  54.7 2.5 %collective-permute-done.18.refs_1_ = bf16[2,128,256]{2,1,0:T(8,128)(2,1)S(1)} collective-permute-done((bf16[2,128,256]{2,1,0:T(8,128)(2,1)S(1)}, bf16[2,128,256]{2,1,0:T(8,128)(2,1)S(1)}, u32[]{:S(2)}, u32[]{:S(2)}) %collective-permute-start.18) | collective-permute-done | bytes 131104 | tf_op jit(solution)/shard_map/ppermute | solution.py:702
  57.9 3.2 %attend_head.2.refs_4_ = bf16[512,2048]{1,0:T(8,128)(2,1)} custom-call(s32[24]{0:T(128)S(1)} %get-tuple-element.59.meta_ref, bf16[512,2048]{1,0:T(8,128)(2,1)S(1)} %get-tuple-element.60.query_ref, bf16[2,128,256]{2,1,0:T(8,128)(2,1)S(1)} %get-tuple-element.73.refs_0_, bf16[2,128,256]{2,1,0:T(8,128)(2,1)S(1)} %collective-permute-done.18.refs_1_, ...), custom_call_target="tpu_custom_call" | custom-call | flops 1024 | bytes 1024 | tf_op jit(solution)/shard_map/attend_head/pallas_call | solution.py:551
  61.1 6.6 %collective-permute-done.14.refs_1_ = bf16[2,128,256]{2,1,0:T(8,128)(2,1)S(1)} collective-permute-done((bf16[2,128,256]{2,1,0:T(8,128)(2,1)S(1)}, bf16[2,128,256]{2,1,0:T(8,128)(2,1)S(1)}, u32[]{:S(2)}, u32[]{:S(2)}) %collective-permute-start.14) | collective-permute-done | bytes 131104 | tf_op jit(solution)/shard_map/ppermute | solution.py:702
  67.8 3.5 %attend_head.3 = bf16[512,2048]{1,0:T(8,128)(2,1)} custom-call(s32[24]{0:T(128)S(1)} %get-tuple-element.59.meta_ref, bf16[512,2048]{1,0:T(8,128)(2,1)S(1)} %get-tuple-element.60.query_ref, bf16[2,128,256]{2,1,0:T(8,128)(2,1)S(1)} %get-tuple-element.67.refs_0_, ...), custom_call_target="tpu_custom_call", output_to_operand_aliasing={{}: (6, {})} | custom-call | flops 1024 | bytes 1024 | tf_op jit(solution)/shard_map/attend_head/pallas_call | solution.py:551
  (59 shorter events, 8.8 us)
Async XLA Ops:
  0.0 10.9 %collective-permute-start.1 = (bf16[4,320,128]{2,1,0:T(8,128)(2,1)}, bf16[4,320,128]{2,1,0:T(8,128)(2,1)S(1)}, u32[]{:S(2)}, u32[]{:S(2)}) collective-permute-start(bf16[4,320,128]{2,1,0:T(8,128)(2,1)} %bitcast.19), channel_id=1, source_target_pairs={{0,2},{1,3},{2,0},{3,1},{4,6},{5,7},{6,4},{7,5},{8,10},{9,11},{10,... | collective-permute-start | bytes 983048 | tf_op jit(solution)/shard_map/ppermute | solution.py:601
  3.0 7.9 %collective-permute-start = (bf16[4,320,128]{2,1,0:T(8,128)(2,1)}, bf16[4,320,128]{2,1,0:T(8,128)(2,1)S(1)}, u32[]{:S(2)}, u32[]{:S(2)}) collective-permute-start(bf16[4,320,128]{2,1,0:T(8,128)(2,1)} %bitcast.20), channel_id=1, source_target_pairs={{0,1},{1,0},{2,3},{3,2},{4,5},{5,4},{6,7},{7,6},{8,9},{9,8},{10,11... | collective-permute-start | bytes 983048 | tf_op jit(solution)/shard_map/ppermute | solution.py:642
  5.2 7.4 %copy-start.5 = (f32[1280]{0:T(1024)S(1)}, f32[1280]{0:T(1024)}, u32[]{:S(2)}) copy-start(f32[1280]{0:T(1024)} %param.19) | copy-start | bytes 15364
  5.2 7.4 %copy-start.6 = (f32[1280]{0:T(1024)S(1)}, f32[1280]{0:T(1024)}, u32[]{:S(2)}) copy-start(f32[1280]{0:T(1024)} %param.21) | copy-start | bytes 15364
  10.9 1.6 %collective-permute-start.2 = (bf16[4,320,128]{2,1,0:T(8,128)(2,1)S(1)}, bf16[4,320,128]{2,1,0:T(8,128)(2,1)S(1)}, u32[]{:S(2)}, u32[]{:S(2)}) collective-permute-start(bf16[4,320,128]{2,1,0:T(8,128)(2,1)S(1)} %collective-permute-done.1.refs_2_), channel_id=1, source_target_pairs={{0,1},{1,0},{2,3},{3,2},{4,5},{5,4},{6,7},{7,6},{8,9},{9,8},{10,11... | collective-permute-start | bytes 983048 | tf_op jit(solution)/shard_map/ppermute | solution.py:605
  16.0 1.4 %collective-permute-start.3 = (bf16[320,256]{1,0:T(8,128)(2,1)S(1)}, bf16[320,256]{1,0:T(8,128)(2,1)S(1)}, u32[]{:S(2)}, u32[]{:S(2)}) collective-permute-start(bf16[320,256]{1,0:T(8,128)(2,1)S(1)} %get-tuple-element.46), channel_id=1, source_target_pairs={{0,1},{1,0},{2,3},{3,2},{4,5},{5,4},{6,7},{7,6},{8,9},{9,8},{10,11... | collective-permute-start | bytes 491528 | tf_op jit(solution)/shard_map/ppermute | solution.py:588
  16.2 7.1 %collective-permute-start.5 = (bf16[320,256]{1,0:T(8,128)(2,1)S(1)}, bf16[320,256]{1,0:T(8,128)(2,1)S(1)}, u32[]{:S(2)}, u32[]{:S(2)}) collective-permute-start(bf16[320,256]{1,0:T(8,128)(2,1)S(1)} %get-tuple-element.53), channel_id=1, source_target_pairs={{0,1},{1,0},{2,3},{3,2},{4,5},{5,4},{6,7},{7,6},{8,9},{9,8},{10,11... | collective-permute-start | bytes 491528 | tf_op jit(solution)/shard_map/ppermute | solution.py:588
  17.5 12.7 %collective-permute-start.6 = (bf16[320,256]{1,0:T(8,128)(2,1)S(1)}, bf16[320,256]{1,0:T(8,128)(2,1)S(1)}, u32[]{:S(2)}, u32[]{:S(2)}) collective-permute-start(bf16[320,256]{1,0:T(8,128)(2,1)S(1)} %add_convert_fusion.7), channel_id=1, source_target_pairs={{0,2},{1,3},{2,0},{3,1},{4,6},{5,7},{6,4},{7,5},{8,10},{9,11},{10,... | collective-permute-start | bytes 491528 | tf_op jit(solution)/shard_map/ppermute | solution.py:588
  22.7 7.4 %collective-permute-start.7 = (bf16[320,256]{1,0:T(8,128)(2,1)S(1)}, bf16[320,256]{1,0:T(8,128)(2,1)S(1)}, u32[]{:S(2)}, u32[]{:S(2)}) collective-permute-start(bf16[320,256]{1,0:T(8,128)(2,1)S(1)} %get-tuple-element.55), channel_id=1, source_target_pairs={{0,1},{1,0},{2,3},{3,2},{4,5},{5,4},{6,7},{7,6},{8,9},{9,8},{10,11... | collective-permute-start | bytes 491528 | tf_op jit(solution)/shard_map/ppermute | solution.py:588
  22.8 1.6 %collective-permute-start.4 = (bf16[320,256]{1,0:T(8,128)(2,1)S(1)}, bf16[320,256]{1,0:T(8,128)(2,1)S(1)}, u32[]{:S(2)}, u32[]{:S(2)}) collective-permute-start(bf16[320,256]{1,0:T(8,128)(2,1)S(1)} %get-tuple-element.49), channel_id=1, source_target_pairs={{0,1},{1,0},{2,3},{3,2},{4,5},{5,4},{6,7},{7,6},{8,9},{9,8},{10,11... | collective-permute-start | bytes 491528 | tf_op jit(solution)/shard_map/ppermute | solution.py:588
  24.4 6.4 %collective-permute-start.8 = (bf16[320,256]{1,0:T(8,128)(2,1)S(1)}, bf16[320,256]{1,0:T(8,128)(2,1)S(1)}, u32[]{:S(2)}, u32[]{:S(2)}) collective-permute-start(bf16[320,256]{1,0:T(8,128)(2,1)S(1)} %add_convert_fusion.6), channel_id=1, source_target_pairs={{0,2},{1,3},{2,0},{3,1},{4,6},{5,7},{6,4},{7,5},{8,10},{9,11},{10,... | collective-permute-start | bytes 491528 | tf_op jit(solution)/shard_map/ppermute | solution.py:588
  32.2 1.9 %collective-permute-start.9 = (bf16[512,256]{1,0:T(8,128)(2,1)S(1)}, bf16[512,256]{1,0:T(8,128)(2,1)S(1)}, u32[]{:S(2)}, u32[]{:S(2)}) collective-permute-start(bf16[512,256]{1,0:T(8,128)(2,1)S(1)} %get-tuple-element.57), channel_id=1, source_target_pairs={{0,1},{1,0},{2,3},{3,2},{4,5},{5,4},{6,7},{7,6},{8,9},{9,8},{10,11... | collective-permute-start | bytes 786440 | tf_op jit(solution)/shard_map/ppermute | solution.py:588
  33.6 2.2 %collective-permute-start.11 = (bf16[512,256]{1,0:T(8,128)(2,1)S(1)}, bf16[512,256]{1,0:T(8,128)(2,1)S(1)}, u32[]{:S(2)}, u32[]{:S(2)}) collective-permute-start(bf16[512,256]{1,0:T(8,128)(2,1)S(1)} %get-tuple-element.65), channel_id=1, source_target_pairs={{0,1},{1,0},{2,3},{3,2},{4,5},{5,4},{6,7},{7,6},{8,9},{9,8},{10,11... | collective-permute-start | bytes 786440 | tf_op jit(solution)/shard_map/ppermute | solution.py:588
  34.1 9.5 %copy-start.7 = (f32[128]{0:T(128)S(1)}, f32[128]{0:T(128)}, u32[]{:S(2)}) copy-start(f32[128]{0:T(128)} %param.26) | copy-start | bytes 1540
  34.2 8.3 %collective-permute-start.12 = (bf16[512,256]{1,0:T(8,128)(2,1)S(1)}, bf16[512,256]{1,0:T(8,128)(2,1)S(1)}, u32[]{:S(2)}, u32[]{:S(2)}) collective-permute-start(bf16[512,256]{1,0:T(8,128)(2,1)S(1)} %add_convert_fusion.3), channel_id=1, source_target_pairs={{0,2},{1,3},{2,0},{3,1},{4,6},{5,7},{6,4},{7,5},{8,10},{9,11},{10,... | collective-permute-start | bytes 786440 | tf_op jit(solution)/shard_map/ppermute | solution.py:588
  35.3 8.3 %collective-permute-start.17 = (bf16[512,256]{1,0:T(8,128)(2,1)S(1)}, bf16[512,256]{1,0:T(8,128)(2,1)S(1)}, u32[]{:S(2)}, u32[]{:S(2)}) collective-permute-start(bf16[512,256]{1,0:T(8,128)(2,1)S(1)} %get-tuple-element.72), channel_id=1, source_target_pairs={{0,1},{1,0},{2,3},{3,2},{4,5},{5,4},{6,7},{7,6},{8,9},{9,8},{10,11... | collective-permute-start | bytes 786440 | tf_op jit(solution)/shard_map/ppermute | solution.py:588
  35.3 11.8 %collective-permute-start.10 = (bf16[512,256]{1,0:T(8,128)(2,1)S(1)}, bf16[512,256]{1,0:T(8,128)(2,1)S(1)}, u32[]{:S(2)}, u32[]{:S(2)}) collective-permute-start(bf16[512,256]{1,0:T(8,128)(2,1)S(1)} %get-tuple-element.63), channel_id=1, source_target_pairs={{0,1},{1,0},{2,3},{3,2},{4,5},{5,4},{6,7},{7,6},{8,9},{9,8},{10,11... | collective-permute-start | bytes 786440 | tf_op jit(solution)/shard_map/ppermute | solution.py:588
  42.5 7.4 %collective-permute-start.13 = (bf16[512,256]{1,0:T(8,128)(2,1)S(1)}, bf16[512,256]{1,0:T(8,128)(2,1)S(1)}, u32[]{:S(2)}, u32[]{:S(2)}) collective-permute-start(bf16[512,256]{1,0:T(8,128)(2,1)S(1)} %add_convert_fusion.1), channel_id=1, source_target_pairs={{0,2},{1,3},{2,0},{3,1},{4,6},{5,7},{6,4},{7,5},{8,10},{9,11},{10,... | collective-permute-start | bytes 786440 | tf_op jit(solution)/shard_map/ppermute | solution.py:588
  44.4 12.8 %collective-permute-start.18 = (bf16[2,128,256]{2,1,0:T(8,128)(2,1)S(1)}, bf16[2,128,256]{2,1,0:T(8,128)(2,1)S(1)}, u32[]{:S(2)}, u32[]{:S(2)}) collective-permute-start(bf16[2,128,256]{2,1,0:T(8,128)(2,1)S(1)} %get-tuple-element.74), channel_id=1, source_target_pairs={{0,8},{4,12},{8,0},{12,4},{1,9},{5,13},{9,1},{13,5},{2,10},{6,14},... | collective-permute-start | bytes 393224 | tf_op jit(solution)/shard_map/ppermute | solution.py:702
  47.2 10.7 %collective-permute-start.19 = (bf16[2,128,256]{2,1,0:T(8,128)(2,1)S(1)}, bf16[2,128,256]{2,1,0:T(8,128)(2,1)S(1)}, u32[]{:S(2)}, u32[]{:S(2)}) collective-permute-start(bf16[2,128,256]{2,1,0:T(8,128)(2,1)S(1)} %get-tuple-element.75), channel_id=1, source_target_pairs={{0,12},{4,8},{8,4},{12,0},{1,13},{5,9},{9,5},{13,1},{2,14},{6,10},... | collective-permute-start | bytes 393224 | tf_op jit(solution)/shard_map/ppermute | solution.py:702
  48.6 9.3 %collective-permute-start.20 = (bf16[2,128,256]{2,1,0:T(8,128)(2,1)S(1)}, bf16[2,128,256]{2,1,0:T(8,128)(2,1)S(1)}, u32[]{:S(2)}, u32[]{:S(2)}) collective-permute-start(bf16[2,128,256]{2,1,0:T(8,128)(2,1)S(1)} %get-tuple-element.76), channel_id=1, source_target_pairs={{0,4},{4,0},{8,12},{12,8},{1,5},{5,1},{9,13},{13,9},{2,6},{6,2},{1... | collective-permute-start | bytes 393224 | tf_op jit(solution)/shard_map/ppermute | solution.py:702
  50.7 17.0 %collective-permute-start.14 = (bf16[2,128,256]{2,1,0:T(8,128)(2,1)S(1)}, bf16[2,128,256]{2,1,0:T(8,128)(2,1)S(1)}, u32[]{:S(2)}, u32[]{:S(2)}) collective-permute-start(bf16[2,128,256]{2,1,0:T(8,128)(2,1)S(1)} %get-tuple-element.68), channel_id=1, source_target_pairs={{0,8},{4,12},{8,0},{12,4},{1,9},{5,13},{9,1},{13,5},{2,10},{6,14},... | collective-permute-start | bytes 393224 | tf_op jit(solution)/shard_map/ppermute | solution.py:702
  53.4 14.4 %collective-permute-start.15 = (bf16[2,128,256]{2,1,0:T(8,128)(2,1)S(1)}, bf16[2,128,256]{2,1,0:T(8,128)(2,1)S(1)}, u32[]{:S(2)}, u32[]{:S(2)}) collective-permute-start(bf16[2,128,256]{2,1,0:T(8,128)(2,1)S(1)} %get-tuple-element.69), channel_id=1, source_target_pairs={{0,12},{4,8},{8,4},{12,0},{1,13},{5,9},{9,5},{13,1},{2,14},{6,10},... | collective-permute-start | bytes 393224 | tf_op jit(solution)/shard_map/ppermute | solution.py:702
  57.2 10.6 %collective-permute-start.16 = (bf16[2,128,256]{2,1,0:T(8,128)(2,1)S(1)}, bf16[2,128,256]{2,1,0:T(8,128)(2,1)S(1)}, u32[]{:S(2)}, u32[]{:S(2)}) collective-permute-start(bf16[2,128,256]{2,1,0:T(8,128)(2,1)S(1)} %get-tuple-element.70), channel_id=1, source_target_pairs={{0,4},{4,0},{8,12},{12,8},{1,5},{5,1},{9,13},{13,9},{2,6},{6,2},{1... | collective-permute-start | bytes 393224 | tf_op jit(solution)/shard_map/ppermute | solution.py:702
  (7 other events, 33.0 us)

commit v6 on v5

--- a/solution.py
+++ b/solution.py
@@ -17,7 +17,7 @@
 HIDDEN_BLOCK = 256
 HEAD_GROUP = 8
 HALVES = 2
-TAPS_EARLY = 3
+TAPS_EARLY = 4
 VALUE_SHIFT = 2.0**-24
 epsilon = 1e-05
 

time: 72.8 us -> 77.5 us (1.065)
  the two profiles are of different devices: /device:TPU:0 before, /device:TPU:17 now
where the time goes in v6:
time: 77.5 us; the launch traced here: 77 us
  Pallas kernels  32.8 us (42%)
  waiting for transfers between devices  20.6 us (27%)
  starting transfers between devices  20.5 us (26%)
  local copies, waits for them, and re-layouts  2.24 us (3%)
    ppermute x12, waiting for transfers between devices, scatter_sum(): got[k ^ 1 << b] = lax.ppermute(sent, 'tp', pairs)  12.7 us
    ppermute x6, starting transfers between devices, move(): return lax.ppermute(value, 'grp', xor_pairs(group_count, mask))  12.6 us
    pallas_call x2, Pallas kernels, tap_projection(): pl.pallas_call(functools.partial(tap_kernel, blocks, head_count, dup, len...  10.1 us
    pallas_call x2, Pallas kernels, attend_head(): pl.pallas_call(functools.partial(attend_kernel, group_count, sources, hea...  9.11 us
    pallas_call x2, Pallas kernels, encoder_mlp(): pl.pallas_call(functools.partial(mlp_kernel, count, base, tiles), out_sha...  6.87 us
    ppermute x6, waiting for transfers between devices, move(): return lax.ppermute(value, 'grp', xor_pairs(group_count, mask))  6.51 us
    ppermute x12, starting transfers between devices, scatter_sum(): got[k ^ 1 << b] = lax.ppermute(sent, 'tp', pairs)  5.31 us
    pallas_call x1, Pallas kernels, prepare(): pl.pallas_call(functools.partial(prepare_kernel, group_count, tiles_local...  2.62 us
  transfers between devices with their start and end apart: 21, of which 9 were waited for; matrix products, arithmetic and copies ran while one was open for 2% of the time, Pallas kernels for 30%

profile of v6, /device:TPU:17, one launch (start us, length us, event | category | flops | bytes accessed | tf_op | source)
XLA Modules:
  0.0 77.0 jit_solution(14978579348969799015)
XLA Ops:
  0.0 1.2 %collective-permute-start.1 = (bf16[4,320,128]{2,1,0:T(8,128)(2,1)}, bf16[4,320,128]{2,1,0:T(8,128)(2,1)S(1)}, u32[]{:S(2)}, u32[]{:S(2)}) collective-permute-start(bf16[4,320,128]{2,1,0:T(8,128)(2,1)} %bitcast.19), channel_id=1, source_target_pairs={{0,2},{1,3},{2,0},{3,1},{4,6},{5,7},{6,4},{7,5},{8,10},{9,11},{10,... | collective-permute-start | bytes 983048 | tf_op jit(solution)/shard_map/ppermute | solution.py:601
  3.0 1.4 %copy-done.3 = bf16[4,1,128,1600]{2,3,1,0:T(8,128)(2,1)S(1)} copy-done((bf16[4,1,128,1600]{2,3,1,0:T(8,128)(2,1)S(1)}, bf16[4,1,128,1600]{2,3,1,0:T(8,128)(2,1)}, u32[]{:S(2)}) %copy-start.3) | copy-done | bytes 1638424
  4.4 5.5 %tap_projection.2 = (bf16[4,512,256]{2,1,0:T(8,128)(2,1)S(1)}, bf16[1280,1280]{1,0:T(8,128)(2,1)S(1)}, bf16[1280,1280]{1,0:T(8,128)(2,1)S(1)}, bf16[4,1600,128]{2,1,0:T(8,128)(2,1)S(1)}) custom-call(s32[26]{0:T(128)S(1)} %concatenate.3.where_ref, bf16[4,1600,128]{2,1,0:T(8,128)(2,1)S(1)} %bitcast.24, bf16[1600,2048]{1,0:T(8,128)(2,1)} %weight_hbm.3, ...), custom_call_target="tpu_custom_call" | custom-call | flops 1024 | bytes 1024 | tf_op jit(solution)/shard_map/tap_projection/pallas_call | solution.py:335
  10.3 1.3 %collective-permute-done.2.refs_3_ = bf16[4,320,128]{2,1,0:T(8,128)(2,1)S(1)} collective-permute-done((bf16[4,320,128]{2,1,0:T(8,128)(2,1)S(1)}, bf16[4,320,128]{2,1,0:T(8,128)(2,1)S(1)}, u32[]{:S(2)}, u32[]{:S(2)}) %collective-permute-start.2) | collective-permute-done | bytes 327712 | tf_op jit(solution)/shard_map/ppermute | solution.py:605
  11.7 3.4 %encoder_mlp.2 = (bf16[320,256]{1,0:T(8,128)(2,1)S(1)}, bf16[320,256]{1,0:T(8,128)(2,1)S(1)}, bf16[320,256]{1,0:T(8,128)(2,1)S(1)}, bf16[320,256]{1,0:T(8,128)(2,1)S(1)}) custom-call(s32[26]{0:T(128)S(1)} %concatenate.3.where_ref, bf16[4,320,128]{2,1,0:T(8,128)(2,1)S(1)} %bitcast.21, bf16[4,320,128]{2,1,0:T(8,128)(2,1)S(1)} %collective-permute-done.refs_1_, ...), custom_call_target="tpu_custom_call" | custom-call | flops 1024 | bytes 1024 | tf_op jit(solution)/shard_map/encoder_mlp/pallas_call | solution.py:221
  16.6 1.2 %collective-permute-start.5 = (bf16[320,256]{1,0:T(8,128)(2,1)S(1)}, bf16[320,256]{1,0:T(8,128)(2,1)S(1)}, u32[]{:S(2)}, u32[]{:S(2)}) collective-permute-start(bf16[320,256]{1,0:T(8,128)(2,1)S(1)} %add_convert_fusion.6), channel_id=1, source_target_pairs={{0,2},{1,3},{2,0},{3,1},{4,6},{5,7},{6,4},{7,5},{8,10},{9,11},{10,... | collective-permute-start | bytes 491528 | tf_op jit(solution)/shard_map/ppermute | solution.py:588
  17.8 3.4 %encoder_mlp.3 = (bf16[320,256]{1,0:T(8,128)(2,1)S(1)}, bf16[320,256]{1,0:T(8,128)(2,1)S(1)}, bf16[320,256]{1,0:T(8,128)(2,1)S(1)}, bf16[320,256]{1,0:T(8,128)(2,1)S(1)}) custom-call(s32[26]{0:T(128)S(1)} %concatenate.3.where_ref, bf16[4,320,128]{2,1,0:T(8,128)(2,1)S(1)} %bitcast.22, bf16[4,320,128]{2,1,0:T(8,128)(2,1)S(1)} %collective-permute-done.refs_1_, ...), custom_call_target="tpu_custom_call" | custom-call | flops 1024 | bytes 1024 | tf_op jit(solution)/shard_map/encoder_mlp/pallas_call | solution.py:221
  22.1 1.3 %collective-permute-done.7 = bf16[320,256]{1,0:T(8,128)(2,1)S(1)} collective-permute-done((bf16[320,256]{1,0:T(8,128)(2,1)S(1)}, bf16[320,256]{1,0:T(8,128)(2,1)S(1)}, u32[]{:S(2)}, u32[]{:S(2)}) %collective-permute-start.7) | collective-permute-done | bytes 163872 | tf_op jit(solution)/shard_map/ppermute | solution.py:588
  23.8 5.3 %collective-permute-done.8.refs_7_ = bf16[320,256]{1,0:T(8,128)(2,1)S(1)} collective-permute-done((bf16[320,256]{1,0:T(8,128)(2,1)S(1)}, bf16[320,256]{1,0:T(8,128)(2,1)S(1)}, u32[]{:S(2)}, u32[]{:S(2)}) %collective-permute-start.8) | collective-permute-done | bytes 163872 | tf_op jit(solution)/shard_map/ppermute | solution.py:588
  29.1 1.3 %kv_projection.2 = (bf16[512,256]{1,0:T(8,128)(2,1)S(1)}, bf16[512,256]{1,0:T(8,128)(2,1)S(1)}, bf16[512,256]{1,0:T(8,128)(2,1)S(1)}, bf16[512,256]{1,0:T(8,128)(2,1)S(1)}, bf16[512,320]{1,0:T(8,128)(2,1)S(1)}) custom-call(s32[26]{0:T(128)S(1)} %concatenate.3.where_ref, bf16[320,2048]{1,0:T(8,128)(2,1)S(1)} %copy-done, ...), custom_call_target="tpu_custom_call" | custom-call | flops 1024 | bytes 1024 | tf_op jit(solution)/shard_map/kv_projection/pallas_call | solution.py:407
  30.4 1.1 %collective-permute-start.9 = (bf16[512,256]{1,0:T(8,128)(2,1)S(1)}, bf16[512,256]{1,0:T(8,128)(2,1)S(1)}, u32[]{:S(2)}, u32[]{:S(2)}) collective-permute-start(bf16[512,256]{1,0:T(8,128)(2,1)S(1)} %get-tuple-element.55), channel_id=1, source_target_pairs={{0,1},{1,0},{2,3},{3,2},{4,5},{5,4},{6,7},{7,6},{8,9},{9,8},{10,11... | collective-permute-start | bytes 786440 | tf_op jit(solution)/shard_map/ppermute | solution.py:588
  31.5 4.5 %tap_projection.3.refs_2_ = bf16[4,512,256]{2,1,0:T(8,128)(2,1)S(1)} custom-call(s32[26]{0:T(128)S(1)} %concatenate.3.where_ref, bf16[4,1600,128]{2,1,0:T(8,128)(2,1)S(1)} %get-tuple-element.60.tap_hbm, bf16[1600,2048]{1,0:T(8,128)(2,1)} %weight_hbm.3), custom_call_target="tpu_custom_call" | custom-call | flops 1024 | bytes 1024 | tf_op jit(solution)/shard_map/tap_projection/pallas_call | solution.py:335
  36.0 1.3 %kv_projection.3 = (bf16[512,256]{1,0:T(8,128)(2,1)S(1)}, bf16[512,256]{1,0:T(8,128)(2,1)S(1)}, bf16[512,256]{1,0:T(8,128)(2,1)S(1)}, bf16[512,256]{1,0:T(8,128)(2,1)S(1)}) custom-call(s32[26]{0:T(128)S(1)} %concatenate.3.where_ref, bf16[320,2048]{1,0:T(8,128)(2,1)S(1)} %copy-done, bf16[4,512,256]{2,1,0:T(8,128)(2,1)S(1)} %get-tuple-element.41.refs_1_, ...), custom_call_target="tpu_custom_call" | custom-call | flops 1024 | bytes 1024 | tf_op jit(solution)/shard_map/kv_projection/pallas_call | solution.py:407
  39.0 2.6 %prepare.1 = (bf16[512,2048]{1,0:T(8,128)(2,1)S(1)}, s32[24]{0:T(128)S(1)}) custom-call(s32[26]{0:T(128)S(1)} %concatenate.3.where_ref, f32[1,128]{1,0:T(1,128)S(1)} %bitcast.33, bf16[512,2048]{1,0:T(8,128)(2,1)S(1)} %copy-done.2), custom_call_target="tpu_custom_call" | custom-call | flops 1024 | bytes 1024 | tf_op jit(solution)/shard_map/prepare/pallas_call | solution.py:269
  41.6 3.3 %collective-permute-done.12.refs_1_ = bf16[512,256]{1,0:T(8,128)(2,1)S(1)} collective-permute-done((bf16[512,256]{1,0:T(8,128)(2,1)S(1)}, bf16[512,256]{1,0:T(8,128)(2,1)S(1)}, u32[]{:S(2)}, u32[]{:S(2)}) %collective-permute-start.12) | collective-permute-done | bytes 262176 | tf_op jit(solution)/shard_map/ppermute | solution.py:588
  46.2 2.5 %collective-permute-start.19 = (bf16[2,128,256]{2,1,0:T(8,128)(2,1)S(1)}, bf16[2,128,256]{2,1,0:T(8,128)(2,1)S(1)}, u32[]{:S(2)}, u32[]{:S(2)}) collective-permute-start(bf16[2,128,256]{2,1,0:T(8,128)(2,1)S(1)} %get-tuple-element.75), channel_id=1, source_target_pairs={{0,12},{4,8},{8,4},{12,0},{1,13},{5,9},{9,5},{13,1},{2,14},{6,10},... | collective-permute-start | bytes 393224 | tf_op jit(solution)/shard_map/ppermute | solution.py:702
  48.8 1.1 %collective-permute-start.20 = (bf16[2,128,256]{2,1,0:T(8,128)(2,1)S(1)}, bf16[2,128,256]{2,1,0:T(8,128)(2,1)S(1)}, u32[]{:S(2)}, u32[]{:S(2)}) collective-permute-start(bf16[2,128,256]{2,1,0:T(8,128)(2,1)S(1)} %get-tuple-element.76), channel_id=1, source_target_pairs={{0,4},{4,0},{8,12},{12,8},{1,5},{5,1},{9,13},{13,9},{2,6},{6,2},{1... | collective-permute-start | bytes 393224 | tf_op jit(solution)/shard_map/ppermute | solution.py:702
  49.8 1.6 %collective-permute-done.13.refs_1_ = bf16[512,256]{1,0:T(8,128)(2,1)S(1)} collective-permute-done((bf16[512,256]{1,0:T(8,128)(2,1)S(1)}, bf16[512,256]{1,0:T(8,128)(2,1)S(1)}, u32[]{:S(2)}, u32[]{:S(2)}) %collective-permute-start.13) | collective-permute-done | bytes 262176 | tf_op jit(solution)/shard_map/ppermute | solution.py:588
  52.4 2.4 %collective-permute-start.15 = (bf16[2,128,256]{2,1,0:T(8,128)(2,1)S(1)}, bf16[2,128,256]{2,1,0:T(8,128)(2,1)S(1)}, u32[]{:S(2)}, u32[]{:S(2)}) collective-permute-start(bf16[2,128,256]{2,1,0:T(8,128)(2,1)S(1)} %get-tuple-element.69), channel_id=1, source_target_pairs={{0,12},{4,8},{8,4},{12,0},{1,13},{5,9},{9,5},{13,1},{2,14},{6,10},... | collective-permute-start | bytes 393224 | tf_op jit(solution)/shard_map/ppermute | solution.py:702
  54.8 6.4 %collective-permute-start.16 = (bf16[2,128,256]{2,1,0:T(8,128)(2,1)S(1)}, bf16[2,128,256]{2,1,0:T(8,128)(2,1)S(1)}, u32[]{:S(2)}, u32[]{:S(2)}) collective-permute-start(bf16[2,128,256]{2,1,0:T(8,128)(2,1)S(1)} %get-tuple-element.70), channel_id=1, source_target_pairs={{0,4},{4,0},{8,12},{12,8},{1,5},{5,1},{9,13},{13,9},{2,6},{6,2},{1... | collective-permute-start | bytes 393224 | tf_op jit(solution)/shard_map/ppermute | solution.py:702
  61.2 5.3 %collective-permute-done.19.refs_2_ = bf16[2,128,256]{2,1,0:T(8,128)(2,1)S(1)} collective-permute-done((bf16[2,128,256]{2,1,0:T(8,128)(2,1)S(1)}, bf16[2,128,256]{2,1,0:T(8,128)(2,1)S(1)}, u32[]{:S(2)}, u32[]{:S(2)}) %collective-permute-start.19) | collective-permute-done | bytes 131104 | tf_op jit(solution)/shard_map/ppermute | solution.py:702
  66.5 4.4 %attend_head.2.refs_4_ = bf16[512,2048]{1,0:T(8,128)(2,1)} custom-call(s32[24]{0:T(128)S(1)} %get-tuple-element.57.meta_ref, bf16[512,2048]{1,0:T(8,128)(2,1)S(1)} %get-tuple-element.58.query_ref, bf16[2,128,256]{2,1,0:T(8,128)(2,1)S(1)} %get-tuple-element.73.refs_0_, bf16[2,128,256]{2,1,0:T(8,128)(2,1)S(1)} %collective-permute-done.18.refs_1_, ...), custom_call_target="tpu_custom_call" | custom-call | flops 1024 | bytes 1024 | tf_op jit(solution)/shard_map/attend_head/pallas_call | solution.py:551
  71.0 1.2 %collective-permute-done.15.refs_2_ = bf16[2,128,256]{2,1,0:T(8,128)(2,1)S(1)} collective-permute-done((bf16[2,128,256]{2,1,0:T(8,128)(2,1)S(1)}, bf16[2,128,256]{2,1,0:T(8,128)(2,1)S(1)}, u32[]{:S(2)}, u32[]{:S(2)}) %collective-permute-start.15) | collective-permute-done | bytes 131104 | tf_op jit(solution)/shard_map/ppermute | solution.py:702
  72.2 4.7 %attend_head.3 = bf16[512,2048]{1,0:T(8,128)(2,1)} custom-call(s32[24]{0:T(128)S(1)} %get-tuple-element.57.meta_ref, bf16[512,2048]{1,0:T(8,128)(2,1)S(1)} %get-tuple-element.58.query_ref, bf16[2,128,256]{2,1,0:T(8,128)(2,1)S(1)} %get-tuple-element.67.refs_0_, ...), custom_call_target="tpu_custom_call", output_to_operand_aliasing={{}: (6, {})} | custom-call | flops 1024 | bytes 1024 | tf_op jit(solution)/shard_map/attend_head/pallas_call | solution.py:551
  (59 shorter events, 8.6 us)
Async XLA Ops:
  0.0 10.0 %collective-permute-start.1 = (bf16[4,320,128]{2,1,0:T(8,128)(2,1)}, bf16[4,320,128]{2,1,0:T(8,128)(2,1)S(1)}, u32[]{:S(2)}, u32[]{:S(2)}) collective-permute-start(bf16[4,320,128]{2,1,0:T(8,128)(2,1)} %bitcast.19), channel_id=1, source_target_pairs={{0,2},{1,3},{2,0},{3,1},{4,6},{5,7},{6,4},{7,5},{8,10},{9,11},{10,... | collective-permute-start | bytes 983048 | tf_op jit(solution)/shard_map/ppermute | solution.py:601
  1.2 9.1 %collective-permute-start = (bf16[4,320,128]{2,1,0:T(8,128)(2,1)}, bf16[4,320,128]{2,1,0:T(8,128)(2,1)S(1)}, u32[]{:S(2)}, u32[]{:S(2)}) collective-permute-start(bf16[4,320,128]{2,1,0:T(8,128)(2,1)} %bitcast.20), channel_id=1, source_target_pairs={{0,1},{1,0},{2,3},{3,2},{4,5},{5,4},{6,7},{7,6},{8,9},{9,8},{10,11... | collective-permute-start | bytes 983048 | tf_op jit(solution)/shard_map/ppermute | solution.py:642
  4.4 7.3 %copy-start.6 = (f32[1280]{0:T(1024)S(1)}, f32[1280]{0:T(1024)}, u32[]{:S(2)}) copy-start(f32[1280]{0:T(1024)} %param.21) | copy-start | bytes 15364
  10.0 1.7 %collective-permute-start.2 = (bf16[4,320,128]{2,1,0:T(8,128)(2,1)S(1)}, bf16[4,320,128]{2,1,0:T(8,128)(2,1)S(1)}, u32[]{:S(2)}, u32[]{:S(2)}) collective-permute-start(bf16[4,320,128]{2,1,0:T(8,128)(2,1)S(1)} %collective-permute-done.1.refs_2_), channel_id=1, source_target_pairs={{0,1},{1,0},{2,3},{3,2},{4,5},{5,4},{6,7},{7,6},{8,9},{9,8},{10,11... | collective-permute-start | bytes 983048 | tf_op jit(solution)/shard_map/ppermute | solution.py:605
  15.1 1.4 %collective-permute-start.4 = (bf16[320,256]{1,0:T(8,128)(2,1)S(1)}, bf16[320,256]{1,0:T(8,128)(2,1)S(1)}, u32[]{:S(2)}, u32[]{:S(2)}) collective-permute-start(bf16[320,256]{1,0:T(8,128)(2,1)S(1)} %get-tuple-element.48), channel_id=1, source_target_pairs={{0,1},{1,0},{2,3},{3,2},{4,5},{5,4},{6,7},{7,6},{8,9},{9,8},{10,11... | collective-permute-start | bytes 491528 | tf_op jit(solution)/shard_map/ppermute | solution.py:588
  15.5 6.6 %collective-permute-start.3 = (bf16[320,256]{1,0:T(8,128)(2,1)S(1)}, bf16[320,256]{1,0:T(8,128)(2,1)S(1)}, u32[]{:S(2)}, u32[]{:S(2)}) collective-permute-start(bf16[320,256]{1,0:T(8,128)(2,1)S(1)} %get-tuple-element.46), channel_id=1, source_target_pairs={{0,1},{1,0},{2,3},{3,2},{4,5},{5,4},{6,7},{7,6},{8,9},{9,8},{10,11... | collective-permute-start | bytes 491528 | tf_op jit(solution)/shard_map/ppermute | solution.py:588
  16.6 7.1 %collective-permute-start.5 = (bf16[320,256]{1,0:T(8,128)(2,1)S(1)}, bf16[320,256]{1,0:T(8,128)(2,1)S(1)}, u32[]{:S(2)}, u32[]{:S(2)}) collective-permute-start(bf16[320,256]{1,0:T(8,128)(2,1)S(1)} %add_convert_fusion.6), channel_id=1, source_target_pairs={{0,2},{1,3},{2,0},{3,1},{4,6},{5,7},{6,4},{7,5},{8,10},{9,11},{10,... | collective-permute-start | bytes 491528 | tf_op jit(solution)/shard_map/ppermute | solution.py:588
  21.3 7.8 %copy-start = (bf16[320,2048]{1,0:T(8,128)(2,1)S(1)}, bf16[320,2048]{1,0:T(8,128)(2,1)}, u32[]{:S(2)}) copy-start(bf16[320,2048]{1,0:T(8,128)(2,1)} %refs_0_.5) | copy-start | bytes 3932164
  21.3 2.4 %collective-permute-start.6 = (bf16[320,256]{1,0:T(8,128)(2,1)S(1)}, bf16[320,256]{1,0:T(8,128)(2,1)S(1)}, u32[]{:S(2)}, u32[]{:S(2)}) collective-permute-start(bf16[320,256]{1,0:T(8,128)(2,1)S(1)} %get-tuple-element.51), channel_id=1, source_target_pairs={{0,1},{1,0},{2,3},{3,2},{4,5},{5,4},{6,7},{7,6},{8,9},{9,8},{10,11... | collective-permute-start | bytes 491528 | tf_op jit(solution)/shard_map/ppermute | solution.py:588
  22.0 1.4 %collective-permute-start.7 = (bf16[320,256]{1,0:T(8,128)(2,1)S(1)}, bf16[320,256]{1,0:T(8,128)(2,1)S(1)}, u32[]{:S(2)}, u32[]{:S(2)}) collective-permute-start(bf16[320,256]{1,0:T(8,128)(2,1)S(1)} %get-tuple-element.53), channel_id=1, source_target_pairs={{0,1},{1,0},{2,3},{3,2},{4,5},{5,4},{6,7},{7,6},{8,9},{9,8},{10,11... | collective-permute-start | bytes 491528 | tf_op jit(solution)/shard_map/ppermute | solution.py:588
  23.4 5.6 %collective-permute-start.8 = (bf16[320,256]{1,0:T(8,128)(2,1)S(1)}, bf16[320,256]{1,0:T(8,128)(2,1)S(1)}, u32[]{:S(2)}, u32[]{:S(2)}) collective-permute-start(bf16[320,256]{1,0:T(8,128)(2,1)S(1)} %add_convert_fusion.4), channel_id=1, source_target_pairs={{0,2},{1,3},{2,0},{3,1},{4,6},{5,7},{6,4},{7,5},{8,10},{9,11},{10,... | collective-permute-start | bytes 491528 | tf_op jit(solution)/shard_map/ppermute | solution.py:588
  30.4 7.0 %collective-permute-start.9 = (bf16[512,256]{1,0:T(8,128)(2,1)S(1)}, bf16[512,256]{1,0:T(8,128)(2,1)S(1)}, u32[]{:S(2)}, u32[]{:S(2)}) collective-permute-start(bf16[512,256]{1,0:T(8,128)(2,1)S(1)} %get-tuple-element.55), channel_id=1, source_target_pairs={{0,1},{1,0},{2,3},{3,2},{4,5},{5,4},{6,7},{7,6},{8,9},{9,8},{10,11... | collective-permute-start | bytes 786440 | tf_op jit(solution)/shard_map/ppermute | solution.py:588
  37.3 1.6 %collective-permute-start.11 = (bf16[512,256]{1,0:T(8,128)(2,1)S(1)}, bf16[512,256]{1,0:T(8,128)(2,1)S(1)}, u32[]{:S(2)}, u32[]{:S(2)}) collective-permute-start(bf16[512,256]{1,0:T(8,128)(2,1)S(1)} %get-tuple-element.65), channel_id=1, source_target_pairs={{0,1},{1,0},{2,3},{3,2},{4,5},{5,4},{6,7},{7,6},{8,9},{9,8},{10,11... | collective-permute-start | bytes 786440 | tf_op jit(solution)/shard_map/ppermute | solution.py:588
  37.4 7.9 %copy-start.7 = (f32[128]{0:T(128)S(1)}, f32[128]{0:T(128)}, u32[]{:S(2)}) copy-start(f32[128]{0:T(128)} %param.26) | copy-start | bytes 1540
  37.5 7.5 %collective-permute-start.12 = (bf16[512,256]{1,0:T(8,128)(2,1)S(1)}, bf16[512,256]{1,0:T(8,128)(2,1)S(1)}, u32[]{:S(2)}, u32[]{:S(2)}) collective-permute-start(bf16[512,256]{1,0:T(8,128)(2,1)S(1)} %add_convert_fusion.3), channel_id=1, source_target_pairs={{0,2},{1,3},{2,0},{3,1},{4,6},{5,7},{6,4},{7,5},{8,10},{9,11},{10,... | collective-permute-start | bytes 786440 | tf_op jit(solution)/shard_map/ppermute | solution.py:588
  37.8 7.4 %collective-permute-start.17 = (bf16[512,256]{1,0:T(8,128)(2,1)S(1)}, bf16[512,256]{1,0:T(8,128)(2,1)S(1)}, u32[]{:S(2)}, u32[]{:S(2)}) collective-permute-start(bf16[512,256]{1,0:T(8,128)(2,1)S(1)} %get-tuple-element.72), channel_id=1, source_target_pairs={{0,1},{1,0},{2,3},{3,2},{4,5},{5,4},{6,7},{7,6},{8,9},{9,8},{10,11... | collective-permute-start | bytes 786440 | tf_op jit(solution)/shard_map/ppermute | solution.py:588
  38.5 7.6 %collective-permute-start.10 = (bf16[512,256]{1,0:T(8,128)(2,1)S(1)}, bf16[512,256]{1,0:T(8,128)(2,1)S(1)}, u32[]{:S(2)}, u32[]{:S(2)}) collective-permute-start(bf16[512,256]{1,0:T(8,128)(2,1)S(1)} %get-tuple-element.63), channel_id=1, source_target_pairs={{0,1},{1,0},{2,3},{3,2},{4,5},{5,4},{6,7},{7,6},{8,9},{9,8},{10,11... | collective-permute-start | bytes 786440 | tf_op jit(solution)/shard_map/ppermute | solution.py:588
  45.0 6.5 %collective-permute-start.13 = (bf16[512,256]{1,0:T(8,128)(2,1)S(1)}, bf16[512,256]{1,0:T(8,128)(2,1)S(1)}, u32[]{:S(2)}, u32[]{:S(2)}) collective-permute-start(bf16[512,256]{1,0:T(8,128)(2,1)S(1)} %add_convert_fusion.1), channel_id=1, source_target_pairs={{0,2},{1,3},{2,0},{3,1},{4,6},{5,7},{6,4},{7,5},{8,10},{9,11},{10,... | collective-permute-start | bytes 786440 | tf_op jit(solution)/shard_map/ppermute | solution.py:588
  46.1 8.7 %collective-permute-start.18 = (bf16[2,128,256]{2,1,0:T(8,128)(2,1)S(1)}, bf16[2,128,256]{2,1,0:T(8,128)(2,1)S(1)}, u32[]{:S(2)}, u32[]{:S(2)}) collective-permute-start(bf16[2,128,256]{2,1,0:T(8,128)(2,1)S(1)} %get-tuple-element.74), channel_id=1, source_target_pairs={{0,8},{4,12},{8,0},{12,4},{1,9},{5,13},{9,1},{13,5},{2,10},{6,14},... | collective-permute-start | bytes 393224 | tf_op jit(solution)/shard_map/ppermute | solution.py:702
  46.2 20.3 %collective-permute-start.19 = (bf16[2,128,256]{2,1,0:T(8,128)(2,1)S(1)}, bf16[2,128,256]{2,1,0:T(8,128)(2,1)S(1)}, u32[]{:S(2)}, u32[]{:S(2)}) collective-permute-start(bf16[2,128,256]{2,1,0:T(8,128)(2,1)S(1)} %get-tuple-element.75), channel_id=1, source_target_pairs={{0,12},{4,8},{8,4},{12,0},{1,13},{5,9},{9,5},{13,1},{2,14},{6,10},... | collective-permute-start | bytes 393224 | tf_op jit(solution)/shard_map/ppermute | solution.py:702
  48.8 17.7 %collective-permute-start.20 = (bf16[2,128,256]{2,1,0:T(8,128)(2,1)S(1)}, bf16[2,128,256]{2,1,0:T(8,128)(2,1)S(1)}, u32[]{:S(2)}, u32[]{:S(2)}) collective-permute-start(bf16[2,128,256]{2,1,0:T(8,128)(2,1)S(1)} %get-tuple-element.76), channel_id=1, source_target_pairs={{0,4},{4,0},{8,12},{12,8},{1,5},{5,1},{9,13},{13,9},{2,6},{6,2},{1... | collective-permute-start | bytes 393224 | tf_op jit(solution)/shard_map/ppermute | solution.py:702
  52.2 18.7 %collective-permute-start.14 = (bf16[2,128,256]{2,1,0:T(8,128)(2,1)S(1)}, bf16[2,128,256]{2,1,0:T(8,128)(2,1)S(1)}, u32[]{:S(2)}, u32[]{:S(2)}) collective-permute-start(bf16[2,128,256]{2,1,0:T(8,128)(2,1)S(1)} %get-tuple-element.68), channel_id=1, source_target_pairs={{0,8},{4,12},{8,0},{12,4},{1,9},{5,13},{9,1},{13,5},{2,10},{6,14},... | collective-permute-start | bytes 393224 | tf_op jit(solution)/shard_map/ppermute | solution.py:702
  52.4 19.8 %collective-permute-start.15 = (bf16[2,128,256]{2,1,0:T(8,128)(2,1)S(1)}, bf16[2,128,256]{2,1,0:T(8,128)(2,1)S(1)}, u32[]{:S(2)}, u32[]{:S(2)}) collective-permute-start(bf16[2,128,256]{2,1,0:T(8,128)(2,1)S(1)} %get-tuple-element.69), channel_id=1, source_target_pairs={{0,12},{4,8},{8,4},{12,0},{1,13},{5,9},{9,5},{13,1},{2,14},{6,10},... | collective-permute-start | bytes 393224 | tf_op jit(solution)/shard_map/ppermute | solution.py:702
  54.8 17.4 %collective-permute-start.16 = (bf16[2,128,256]{2,1,0:T(8,128)(2,1)S(1)}, bf16[2,128,256]{2,1,0:T(8,128)(2,1)S(1)}, u32[]{:S(2)}, u32[]{:S(2)}) collective-permute-start(bf16[2,128,256]{2,1,0:T(8,128)(2,1)S(1)} %get-tuple-element.70), channel_id=1, source_target_pairs={{0,4},{4,0},{8,12},{12,8},{1,5},{5,1},{9,13},{13,9},{2,6},{6,2},{1... | collective-permute-start | bytes 393224 | tf_op jit(solution)/shard_map/ppermute | solution.py:702
  (7 other events, 33.0 us)

commit v7 on v4

--- a/solution.py
+++ b/solution.py
@@ -710,11 +710,16 @@
         terms = kv_terms[head]
         if one_large:
             star = place["star"]
-            order = (0, 2, 3, 1)
-            picks = tuple((send + d, star) for d in order)
-            made = finish_tiles(meta, k_gain, terms, picks)
-            tiles = tuple(move(tile, d) if d else tile for tile, d in zip(made, order))
-            sources = tuple((d, group_count + d) for d in order)
+            direct = head == head_count - 1
+            picks = ((send, star), (send + 2, star))
+            picks += ((send + 3, star) if direct else (send + 3,), (send + 1, star))
+            own, middle, far, near = finish_tiles(meta, k_gain, terms, picks)
+            middle_got, far_got, near_got = move(middle, 2), move(far, 3), move(near, 1)
+            tiles = (own, middle_got, far_got, near_got)
+            sources = ((0, 4), (2, 6), (3, 7) if direct else (3,), (1, 5))
+            if not direct:
+                tiles += (move(after(middle_got[1:], far_got), 1),)
+                sources += ((7,),)
         else:
             picks = tuple(
                 tuple(send + s * group_count + d for s in range(slots)) for d in range(group_count)

time: 72.4 us -> 73.6 us (1.017)
  starting transfers between devices: 19.3 us -> 25.1 us
  waiting for transfers between devices: 18.1 us -> 14.8 us
  Pallas kernels: 31.5 us -> 30.5 us
    ppermute x6 -> x7, starting transfers between devices: 9.31 us -> 15.1 us  [move(): return lax.ppermute(value, 'grp', xor_pairs(group_count, mask))]
    ppermute x6 -> x7, waiting for transfers between devices: 8.56 us -> 5.21 us  [move(): return lax.ppermute(value, 'grp', xor_pairs(group_count, mask))]
    pallas_call x2, Pallas kernels: 8.69 us -> 7.62 us  [attend_head(): pl.pallas_call(functools.partial(attend_kernel, group_count, sources, hea...]
  transfers between devices with their start and end apart: 18 -> 19, of which waited for: 8 -> 8; matrix products, arithmetic and copies ran while one was open for 2% -> 2% of each run, Pallas kernels for 28% -> 27%
where the time goes in v7:
time: 73.6 us; the launch traced here: 73.4 us
  Pallas kernels  30.5 us (41%)
  starting transfers between devices  25.1 us (34%)
  waiting for transfers between devices  14.8 us (20%)
  local copies, waits for them, and re-layouts  2.24 us (3%)
    ppermute x7, starting transfers between devices, move(): return lax.ppermute(value, 'grp', xor_pairs(group_count, mask))  15.1 us
    pallas_call x2, Pallas kernels, tap_projection(): pl.pallas_call(functools.partial(tap_kernel, blocks, head_count, dup, len...  10.2 us
    pallas_call x2, Pallas kernels, attend_head(): pl.pallas_call(functools.partial(attend_kernel, group_count, sources, hea...  7.62 us
    ppermute x9, waiting for transfers between devices, scatter_sum(): got[k ^ 1 << b] = lax.ppermute(sent, 'tp', pairs)  7.18 us
    ppermute x9, starting transfers between devices, scatter_sum(): got[k ^ 1 << b] = lax.ppermute(sent, 'tp', pairs)  7.02 us
    pallas_call x1, Pallas kernels, encoder_mlp(): pl.pallas_call(functools.partial(mlp_kernel, count, bases, tiles), out_sh...  5.66 us
    ppermute x7, waiting for transfers between devices, move(): return lax.ppermute(value, 'grp', xor_pairs(group_count, mask))  5.21 us
    ppermute x1, starting transfers between devices, gather_half(): pieces[k | 1 << b] = lax.ppermute(pieces[k], 'tp', pairs)  2.97 us
  transfers between devices with their start and end apart: 19, of which 8 were waited for; matrix products, arithmetic and copies ran while one was open for 2% of the time, Pallas kernels for 27%

profile of v7, /device:TPU:0, one launch (start us, length us, event | category | flops | bytes accessed | tf_op | source)
XLA Modules:
  0.0 73.4 jit_solution(5149729060671014952)
XLA Ops:
  0.0 3.0 %collective-permute-start.1 = (bf16[4,320,128]{2,1,0:T(8,128)(2,1)}, bf16[4,320,128]{2,1,0:T(8,128)(2,1)S(1)}, u32[]{:S(2)}, u32[]{:S(2)}) collective-permute-start(bf16[4,320,128]{2,1,0:T(8,128)(2,1)} %bitcast.20), channel_id=1, source_target_pairs={{0,2},{1,3},{2,0},{3,1},{4,6},{5,7},{6,4},{7,5},{8,10},{9,11},{10,... | collective-permute-start | bytes 983048 | tf_op jit(solution)/shard_map/ppermute | solution.py:601
  3.7 1.4 %copy-done.2 = bf16[4,1,128,1600]{2,3,1,0:T(8,128)(2,1)S(1)} copy-done((bf16[4,1,128,1600]{2,3,1,0:T(8,128)(2,1)S(1)}, bf16[4,1,128,1600]{2,3,1,0:T(8,128)(2,1)}, u32[]{:S(2)}) %copy-start.2) | copy-done | bytes 1638424
  5.2 4.9 %tap_projection.2 = (bf16[3,512,256]{2,1,0:T(8,128)(2,1)S(1)}, bf16[1280,1280]{1,0:T(8,128)(2,1)S(1)}, bf16[1280,1280]{1,0:T(8,128)(2,1)S(1)}, bf16[4,1600,128]{2,1,0:T(8,128)(2,1)S(1)}) custom-call(s32[26]{0:T(128)S(1)} %concatenate.3.where_ref, bf16[4,1600,128]{2,1,0:T(8,128)(2,1)S(1)} %bitcast.19, bf16[1600,2048]{1,0:T(8,128)(2,1)} %weight_hbm.3, ...), custom_call_target="tpu_custom_call" | custom-call | flops 1024 | bytes 1024 | tf_op jit(solution)/shard_map/tap_projection/pallas_call | solution.py:335
  10.9 1.6 %collective-permute-done.2.refs_3_ = bf16[4,320,128]{2,1,0:T(8,128)(2,1)S(1)} collective-permute-done((bf16[4,320,128]{2,1,0:T(8,128)(2,1)S(1)}, bf16[4,320,128]{2,1,0:T(8,128)(2,1)S(1)}, u32[]{:S(2)}, u32[]{:S(2)}) %collective-permute-start.2) | collective-permute-done | bytes 327712 | tf_op jit(solution)/shard_map/ppermute | solution.py:605
  12.5 5.7 %encoder_mlp.1 = (bf16[640,256]{1,0:T(8,128)(2,1)S(1)}, bf16[640,256]{1,0:T(8,128)(2,1)S(1)}, bf16[640,256]{1,0:T(8,128)(2,1)S(1)}, bf16[640,256]{1,0:T(8,128)(2,1)S(1)}) custom-call(s32[26]{0:T(128)S(1)} %concatenate.3.where_ref, bf16[4,320,128]{2,1,0:T(8,128)(2,1)S(1)} %bitcast.22, bf16[4,320,128]{2,1,0:T(8,128)(2,1)S(1)} %collective-permute-done.refs_1_, ...), custom_call_target="tpu_custom_call" | custom-call | flops 1024 | bytes 1024 | tf_op jit(solution)/shard_map/encoder_mlp/pallas_call | solution.py:221
  18.8 1.1 %collective-permute-done.3 = bf16[640,256]{1,0:T(8,128)(2,1)S(1)} collective-permute-done((bf16[640,256]{1,0:T(8,128)(2,1)S(1)}, bf16[640,256]{1,0:T(8,128)(2,1)S(1)}, u32[]{:S(2)}, u32[]{:S(2)}) %collective-permute-start.3) | collective-permute-done | bytes 327712 | tf_op jit(solution)/shard_map/ppermute | solution.py:588
  20.0 1.8 %collective-permute-start.5 = (bf16[640,256]{1,0:T(8,128)(2,1)S(1)}, bf16[640,256]{1,0:T(8,128)(2,1)S(1)}, u32[]{:S(2)}, u32[]{:S(2)}) collective-permute-start(bf16[640,256]{1,0:T(8,128)(2,1)S(1)} %add_convert_fusion.1), channel_id=1, source_target_pairs={{0,2},{1,3},{2,0},{3,1},{4,6},{5,7},{6,4},{7,5},{8,10},{9,11},{10,... | collective-permute-start | bytes 983048 | tf_op jit(solution)/shard_map/ppermute | solution.py:588
  21.8 5.3 %tap_projection.3.refs_2_ = bf16[5,512,256]{2,1,0:T(8,128)(2,1)S(1)} custom-call(s32[26]{0:T(128)S(1)} %concatenate.3.where_ref, bf16[4,1600,128]{2,1,0:T(8,128)(2,1)S(1)} %get-tuple-element.44.tap_hbm, bf16[1600,2048]{1,0:T(8,128)(2,1)} %weight_hbm.3), custom_call_target="tpu_custom_call" | custom-call | flops 1024 | bytes 1024 | tf_op jit(solution)/shard_map/tap_projection/pallas_call | solution.py:335
  27.2 2.6 %collective-permute-done.5.refs_6_ = bf16[640,256]{1,0:T(8,128)(2,1)S(1)} collective-permute-done((bf16[640,256]{1,0:T(8,128)(2,1)S(1)}, bf16[640,256]{1,0:T(8,128)(2,1)S(1)}, u32[]{:S(2)}, u32[]{:S(2)}) %collective-permute-start.5) | collective-permute-done | bytes 327712 | tf_op jit(solution)/shard_map/ppermute | solution.py:588
  29.8 1.3 %kv_projection.2 = (bf16[512,256]{1,0:T(8,128)(2,1)S(1)}, bf16[512,256]{1,0:T(8,128)(2,1)S(1)}, bf16[512,256]{1,0:T(8,128)(2,1)S(1)}, bf16[512,256]{1,0:T(8,128)(2,1)S(1)}, bf16[512,320]{1,0:T(8,128)(2,1)S(1)}) custom-call(s32[26]{0:T(128)S(1)} %concatenate.3.where_ref, bf16[320,2048]{1,0:T(8,128)(2,1)S(1)} %copy-done, ...), custom_call_target="tpu_custom_call" | custom-call | flops 1024 | bytes 1024 | tf_op jit(solution)/shard_map/kv_projection/pallas_call | solution.py:407
  31.2 1.3 %kv_projection.3 = (bf16[512,256]{1,0:T(8,128)(2,1)S(1)}, bf16[512,256]{1,0:T(8,128)(2,1)S(1)}, bf16[512,256]{1,0:T(8,128)(2,1)S(1)}, bf16[512,256]{1,0:T(8,128)(2,1)S(1)}) custom-call(s32[26]{0:T(128)S(1)} %concatenate.3.where_ref, bf16[320,2048]{1,0:T(8,128)(2,1)S(1)} %copy-done, bf16[3,512,256]{2,1,0:T(8,128)(2,1)S(1)} %get-tuple-element.37.refs_1_, ...), custom_call_target="tpu_custom_call" | custom-call | flops 1024 | bytes 1024 | tf_op jit(solution)/shard_map/kv_projection/pallas_call | solution.py:407
  33.1 1.8 %collective-permute-start.9 = (bf16[512,256]{1,0:T(8,128)(2,1)S(1)}, bf16[512,256]{1,0:T(8,128)(2,1)S(1)}, u32[]{:S(2)}, u32[]{:S(2)}) collective-permute-start(bf16[512,256]{1,0:T(8,128)(2,1)S(1)} %add_convert_fusion.5), channel_id=1, source_target_pairs={{0,2},{1,3},{2,0},{3,1},{4,6},{5,7},{6,4},{7,5},{8,10},{9,11},{10,... | collective-permute-start | bytes 786440 | tf_op jit(solution)/shard_map/ppermute | solution.py:588
  35.5 2.8 %prepare.1 = (bf16[512,2048]{1,0:T(8,128)(2,1)S(1)}, s32[24]{0:T(128)S(1)}) custom-call(s32[26]{0:T(128)S(1)} %concatenate.3.where_ref, f32[1,128]{1,0:T(1,128)S(1)} %bitcast.29, bf16[512,2048]{1,0:T(8,128)(2,1)S(1)} %copy-done.1), custom_call_target="tpu_custom_call" | custom-call | flops 1024 | bytes 1024 | tf_op jit(solution)/shard_map/prepare/pallas_call | solution.py:269
  38.3 3.1 %collective-permute-done.9.refs_1_ = bf16[512,256]{1,0:T(8,128)(2,1)S(1)} collective-permute-done((bf16[512,256]{1,0:T(8,128)(2,1)S(1)}, bf16[512,256]{1,0:T(8,128)(2,1)S(1)}, u32[]{:S(2)}, u32[]{:S(2)}) %collective-permute-start.9) | collective-permute-done | bytes 262176 | tf_op jit(solution)/shard_map/ppermute | solution.py:588
  41.4 1.7 %collective-permute-start.10 = (bf16[512,256]{1,0:T(8,128)(2,1)S(1)}, bf16[512,256]{1,0:T(8,128)(2,1)S(1)}, u32[]{:S(2)}, u32[]{:S(2)}) collective-permute-start(bf16[512,256]{1,0:T(8,128)(2,1)S(1)} %add_convert_fusion.3), channel_id=1, source_target_pairs={{0,2},{1,3},{2,0},{3,1},{4,6},{5,7},{6,4},{7,5},{8,10},{9,11},{10,... | collective-permute-start | bytes 786440 | tf_op jit(solution)/shard_map/ppermute | solution.py:588
  44.1 2.7 %collective-permute-start.15 = (bf16[2,128,256]{2,1,0:T(8,128)(2,1)S(1)}, bf16[2,128,256]{2,1,0:T(8,128)(2,1)S(1)}, u32[]{:S(2)}, u32[]{:S(2)}) collective-permute-start(bf16[2,128,256]{2,1,0:T(8,128)(2,1)S(1)} %get-tuple-element.65), channel_id=1, source_target_pairs={{0,8},{4,12},{8,0},{12,4},{1,9},{5,13},{9,1},{13,5},{2,10},{6,14},... | collective-permute-start | bytes 393224 | tf_op jit(solution)/shard_map/ppermute | solution.py:707
  46.8 1.4 %collective-permute-start.16 = (bf16[1,128,256]{2,1,0:T(8,128)(2,1)S(1)}, bf16[1,128,256]{2,1,0:T(8,128)(2,1)S(1)}, u32[]{:S(2)}, u32[]{:S(2)}) collective-permute-start(bf16[1,128,256]{2,1,0:T(8,128)(2,1)S(1)} %get-tuple-element.66), channel_id=1, source_target_pairs={{0,12},{4,8},{8,4},{12,0},{1,13},{5,9},{9,5},{13,1},{2,14},{6,10},... | collective-permute-start | bytes 196616 | tf_op jit(solution)/shard_map/ppermute | solution.py:707
  49.6 2.9 %collective-permute-start.11 = (bf16[2,128,256]{2,1,0:T(8,128)(2,1)S(1)}, bf16[2,128,256]{2,1,0:T(8,128)(2,1)S(1)}, u32[]{:S(2)}, u32[]{:S(2)}) collective-permute-start(bf16[2,128,256]{2,1,0:T(8,128)(2,1)S(1)} %get-tuple-element.59), channel_id=1, source_target_pairs={{0,8},{4,12},{8,0},{12,4},{1,9},{5,13},{9,1},{13,5},{2,10},{6,14},... | collective-permute-start | bytes 393224 | tf_op jit(solution)/shard_map/ppermute | solution.py:707
  52.5 1.3 %collective-permute-start.12 = (bf16[2,128,256]{2,1,0:T(8,128)(2,1)S(1)}, bf16[2,128,256]{2,1,0:T(8,128)(2,1)S(1)}, u32[]{:S(2)}, u32[]{:S(2)}) collective-permute-start(bf16[2,128,256]{2,1,0:T(8,128)(2,1)S(1)} %get-tuple-element.60), channel_id=1, source_target_pairs={{0,12},{4,8},{8,4},{12,0},{1,13},{5,9},{9,5},{13,1},{2,14},{6,10},... | collective-permute-start | bytes 393224 | tf_op jit(solution)/shard_map/ppermute | solution.py:707
  53.9 1.5 %collective-permute-done.15.refs_1_ = bf16[2,128,256]{2,1,0:T(8,128)(2,1)S(1)} collective-permute-done((bf16[2,128,256]{2,1,0:T(8,128)(2,1)S(1)}, bf16[2,128,256]{2,1,0:T(8,128)(2,1)S(1)}, u32[]{:S(2)}, u32[]{:S(2)}) %collective-permute-start.15) | collective-permute-done | bytes 131104 | tf_op jit(solution)/shard_map/ppermute | solution.py:707
  55.9 6.1 %collective-permute-start.18 = (bf16[1,128,256]{2,1,0:T(8,128)(2,1)S(1)}, bf16[1,128,256]{2,1,0:T(8,128)(2,1)S(1)}, u32[]{:S(2)}, u32[]{:S(2)}) collective-permute-start(bf16[1,128,256]{2,1,0:T(8,128)(2,1)S(1)} %slice.4), channel_id=1, source_target_pairs={{0,4},{4,0},{8,12},{12,8},{1,5},{5,1},{9,13},{13,9},{2,6},{6,2},{1... | collective-permute-start | bytes 196616 | tf_op jit(solution)/shard_map/ppermute | solution.py:707
  61.9 3.7 %collective-permute-done.18.refs_4_ = bf16[1,128,256]{2,1,0:T(8,128)(2,1)S(1)} collective-permute-done((bf16[1,128,256]{2,1,0:T(8,128)(2,1)S(1)}, bf16[1,128,256]{2,1,0:T(8,128)(2,1)S(1)}, u32[]{:S(2)}, u32[]{:S(2)}) %collective-permute-start.18) | collective-permute-done | bytes 65568 | tf_op jit(solution)/shard_map/ppermute | solution.py:707
  65.6 3.7 %attend_head.2.refs_4_ = bf16[512,2048]{1,0:T(8,128)(2,1)} custom-call(s32[24]{0:T(128)S(1)} %get-tuple-element.50.meta_ref, bf16[512,2048]{1,0:T(8,128)(2,1)S(1)} %get-tuple-element.51.query_ref, bf16[2,128,256]{2,1,0:T(8,128)(2,1)S(1)} %get-tuple-element.64.refs_0_, bf16[2,128,256]{2,1,0:T(8,128)(2,1)S(1)} %collective-permute-done.15.refs_1_, ...), custom_call_target="tpu_custom_call" | custom-call | flops 1024 | bytes 1024 | tf_op jit(solution)/shard_map/attend_head/pallas_call | solution.py:551
  69.3 3.9 %attend_head.3 = bf16[512,2048]{1,0:T(8,128)(2,1)} custom-call(s32[24]{0:T(128)S(1)} %get-tuple-element.50.meta_ref, bf16[512,2048]{1,0:T(8,128)(2,1)S(1)} %get-tuple-element.51.query_ref, bf16[2,128,256]{2,1,0:T(8,128)(2,1)S(1)} %get-tuple-element.58.refs_0_, ...), custom_call_target="tpu_custom_call", output_to_operand_aliasing={{}: (6, {})} | custom-call | flops 1024 | bytes 1024 | tf_op jit(solution)/shard_map/attend_head/pallas_call | solution.py:551
  (53 shorter events, 6.4 us)
Async XLA Ops:
  0.0 10.9 %collective-permute-start.1 = (bf16[4,320,128]{2,1,0:T(8,128)(2,1)}, bf16[4,320,128]{2,1,0:T(8,128)(2,1)S(1)}, u32[]{:S(2)}, u32[]{:S(2)}) collective-permute-start(bf16[4,320,128]{2,1,0:T(8,128)(2,1)} %bitcast.20), channel_id=1, source_target_pairs={{0,2},{1,3},{2,0},{3,1},{4,6},{5,7},{6,4},{7,5},{8,10},{9,11},{10,... | collective-permute-start | bytes 983048 | tf_op jit(solution)/shard_map/ppermute | solution.py:601
  3.0 7.9 %collective-permute-start = (bf16[4,320,128]{2,1,0:T(8,128)(2,1)}, bf16[4,320,128]{2,1,0:T(8,128)(2,1)S(1)}, u32[]{:S(2)}, u32[]{:S(2)}) collective-permute-start(bf16[4,320,128]{2,1,0:T(8,128)(2,1)} %bitcast.21), channel_id=1, source_target_pairs={{0,1},{1,0},{2,3},{3,2},{4,5},{5,4},{6,7},{7,6},{8,9},{9,8},{10,11... | collective-permute-start | bytes 983048 | tf_op jit(solution)/shard_map/ppermute | solution.py:646
  5.2 7.4 %copy-start.5 = (f32[1280]{0:T(1024)S(1)}, f32[1280]{0:T(1024)}, u32[]{:S(2)}) copy-start(f32[1280]{0:T(1024)} %param.19) | copy-start | bytes 15364
  5.2 7.4 %copy-start.6 = (f32[1280]{0:T(1024)S(1)}, f32[1280]{0:T(1024)}, u32[]{:S(2)}) copy-start(f32[1280]{0:T(1024)} %param.21) | copy-start | bytes 15364
  10.9 1.6 %collective-permute-start.2 = (bf16[4,320,128]{2,1,0:T(8,128)(2,1)S(1)}, bf16[4,320,128]{2,1,0:T(8,128)(2,1)S(1)}, u32[]{:S(2)}, u32[]{:S(2)}) collective-permute-start(bf16[4,320,128]{2,1,0:T(8,128)(2,1)S(1)} %collective-permute-done.1.refs_2_), channel_id=1, source_target_pairs={{0,1},{1,0},{2,3},{3,2},{4,5},{5,4},{6,7},{7,6},{8,9},{9,8},{10,11... | collective-permute-start | bytes 983048 | tf_op jit(solution)/shard_map/ppermute | solution.py:605
  12.5 9.2 %copy-start.9 = (f32[320]{0:T(512)S(1)}, f32[320]{0:T(512)}, u32[]{:S(2)}) copy-start(f32[320]{0:T(512)} %param.23) | copy-start | bytes 3844
  18.2 1.7 %collective-permute-start.3 = (bf16[640,256]{1,0:T(8,128)(2,1)S(1)}, bf16[640,256]{1,0:T(8,128)(2,1)S(1)}, u32[]{:S(2)}, u32[]{:S(2)}) collective-permute-start(bf16[640,256]{1,0:T(8,128)(2,1)S(1)} %get-tuple-element.42), channel_id=1, source_target_pairs={{0,1},{1,0},{2,3},{3,2},{4,5},{5,4},{6,7},{7,6},{8,9},{9,8},{10,11... | collective-permute-start | bytes 983048 | tf_op jit(solution)/shard_map/ppermute | solution.py:588
  18.4 8.7 %collective-permute-start.4 = (bf16[640,256]{1,0:T(8,128)(2,1)S(1)}, bf16[640,256]{1,0:T(8,128)(2,1)S(1)}, u32[]{:S(2)}, u32[]{:S(2)}) collective-permute-start(bf16[640,256]{1,0:T(8,128)(2,1)S(1)} %get-tuple-element.46), channel_id=1, source_target_pairs={{0,1},{1,0},{2,3},{3,2},{4,5},{5,4},{6,7},{7,6},{8,9},{9,8},{10,11... | collective-permute-start | bytes 983048 | tf_op jit(solution)/shard_map/ppermute | solution.py:588
  20.0 9.8 %collective-permute-start.5 = (bf16[640,256]{1,0:T(8,128)(2,1)S(1)}, bf16[640,256]{1,0:T(8,128)(2,1)S(1)}, u32[]{:S(2)}, u32[]{:S(2)}) collective-permute-start(bf16[640,256]{1,0:T(8,128)(2,1)S(1)} %add_convert_fusion.1), channel_id=1, source_target_pairs={{0,2},{1,3},{2,0},{3,1},{4,6},{5,7},{6,4},{7,5},{8,10},{9,11},{10,... | collective-permute-start | bytes 983048 | tf_op jit(solution)/shard_map/ppermute | solution.py:588
  21.8 8.0 %copy-start = (bf16[320,2048]{1,0:T(8,128)(2,1)S(1)}, bf16[320,2048]{1,0:T(8,128)(2,1)}, u32[]{:S(2)}) copy-start(bf16[320,2048]{1,0:T(8,128)(2,1)} %refs_0_.5) | copy-start | bytes 3932164
  31.1 1.9 %collective-permute-start.6 = (bf16[512,256]{1,0:T(8,128)(2,1)S(1)}, bf16[512,256]{1,0:T(8,128)(2,1)S(1)}, u32[]{:S(2)}, u32[]{:S(2)}) collective-permute-start(bf16[512,256]{1,0:T(8,128)(2,1)S(1)} %get-tuple-element.48), channel_id=1, source_target_pairs={{0,1},{1,0},{2,3},{3,2},{4,5},{5,4},{6,7},{7,6},{8,9},{9,8},{10,11... | collective-permute-start | bytes 786440 | tf_op jit(solution)/shard_map/ppermute | solution.py:588
  32.5 2.9 %collective-permute-start.8 = (bf16[512,256]{1,0:T(8,128)(2,1)S(1)}, bf16[512,256]{1,0:T(8,128)(2,1)S(1)}, u32[]{:S(2)}, u32[]{:S(2)}) collective-permute-start(bf16[512,256]{1,0:T(8,128)(2,1)S(1)} %get-tuple-element.56), channel_id=1, source_target_pairs={{0,1},{1,0},{2,3},{3,2},{4,5},{5,4},{6,7},{7,6},{8,9},{9,8},{10,11... | collective-permute-start | bytes 786440 | tf_op jit(solution)/shard_map/ppermute | solution.py:588
  33.0 10.2 %copy-start.7 = (f32[128]{0:T(128)S(1)}, f32[128]{0:T(128)}, u32[]{:S(2)}) copy-start(f32[128]{0:T(128)} %param.26) | copy-start | bytes 1540
  33.1 8.3 %collective-permute-start.9 = (bf16[512,256]{1,0:T(8,128)(2,1)S(1)}, bf16[512,256]{1,0:T(8,128)(2,1)S(1)}, u32[]{:S(2)}, u32[]{:S(2)}) collective-permute-start(bf16[512,256]{1,0:T(8,128)(2,1)S(1)} %add_convert_fusion.5), channel_id=1, source_target_pairs={{0,2},{1,3},{2,0},{3,1},{4,6},{5,7},{6,4},{7,5},{8,10},{9,11},{10,... | collective-permute-start | bytes 786440 | tf_op jit(solution)/shard_map/ppermute | solution.py:588
  34.9 8.3 %collective-permute-start.14 = (bf16[512,256]{1,0:T(8,128)(2,1)S(1)}, bf16[512,256]{1,0:T(8,128)(2,1)S(1)}, u32[]{:S(2)}, u32[]{:S(2)}) collective-permute-start(bf16[512,256]{1,0:T(8,128)(2,1)S(1)} %get-tuple-element.63), channel_id=1, source_target_pairs={{0,1},{1,0},{2,3},{3,2},{4,5},{5,4},{6,7},{7,6},{8,9},{9,8},{10,11... | collective-permute-start | bytes 786440 | tf_op jit(solution)/shard_map/ppermute | solution.py:588
  34.9 11.8 %collective-permute-start.7 = (bf16[512,256]{1,0:T(8,128)(2,1)S(1)}, bf16[512,256]{1,0:T(8,128)(2,1)S(1)}, u32[]{:S(2)}, u32[]{:S(2)}) collective-permute-start(bf16[512,256]{1,0:T(8,128)(2,1)S(1)} %get-tuple-element.54), channel_id=1, source_target_pairs={{0,1},{1,0},{2,3},{3,2},{4,5},{5,4},{6,7},{7,6},{8,9},{9,8},{10,11... | collective-permute-start | bytes 786440 | tf_op jit(solution)/shard_map/ppermute | solution.py:588
  41.4 7.4 %collective-permute-start.10 = (bf16[512,256]{1,0:T(8,128)(2,1)S(1)}, bf16[512,256]{1,0:T(8,128)(2,1)S(1)}, u32[]{:S(2)}, u32[]{:S(2)}) collective-permute-start(bf16[512,256]{1,0:T(8,128)(2,1)S(1)} %add_convert_fusion.3), channel_id=1, source_target_pairs={{0,2},{1,3},{2,0},{3,1},{4,6},{5,7},{6,4},{7,5},{8,10},{9,11},{10,... | collective-permute-start | bytes 786440 | tf_op jit(solution)/shard_map/ppermute | solution.py:588
  44.1 11.4 %collective-permute-start.15 = (bf16[2,128,256]{2,1,0:T(8,128)(2,1)S(1)}, bf16[2,128,256]{2,1,0:T(8,128)(2,1)S(1)}, u32[]{:S(2)}, u32[]{:S(2)}) collective-permute-start(bf16[2,128,256]{2,1,0:T(8,128)(2,1)S(1)} %get-tuple-element.65), channel_id=1, source_target_pairs={{0,8},{4,12},{8,0},{12,4},{1,9},{5,13},{9,1},{13,5},{2,10},{6,14},... | collective-permute-start | bytes 393224 | tf_op jit(solution)/shard_map/ppermute | solution.py:707
  46.8 9.1 %collective-permute-start.16 = (bf16[1,128,256]{2,1,0:T(8,128)(2,1)S(1)}, bf16[1,128,256]{2,1,0:T(8,128)(2,1)S(1)}, u32[]{:S(2)}, u32[]{:S(2)}) collective-permute-start(bf16[1,128,256]{2,1,0:T(8,128)(2,1)S(1)} %get-tuple-element.66), channel_id=1, source_target_pairs={{0,12},{4,8},{8,4},{12,0},{1,13},{5,9},{9,5},{13,1},{2,14},{6,10},... | collective-permute-start | bytes 196616 | tf_op jit(solution)/shard_map/ppermute | solution.py:707
  48.2 13.7 %collective-permute-start.17 = (bf16[2,128,256]{2,1,0:T(8,128)(2,1)S(1)}, bf16[2,128,256]{2,1,0:T(8,128)(2,1)S(1)}, u32[]{:S(2)}, u32[]{:S(2)}) collective-permute-start(bf16[2,128,256]{2,1,0:T(8,128)(2,1)S(1)} %get-tuple-element.67), channel_id=1, source_target_pairs={{0,4},{4,0},{8,12},{12,8},{1,5},{5,1},{9,13},{13,9},{2,6},{6,2},{1... | collective-permute-start | bytes 393224 | tf_op jit(solution)/shard_map/ppermute | solution.py:707
  49.6 19.7 %collective-permute-start.11 = (bf16[2,128,256]{2,1,0:T(8,128)(2,1)S(1)}, bf16[2,128,256]{2,1,0:T(8,128)(2,1)S(1)}, u32[]{:S(2)}, u32[]{:S(2)}) collective-permute-start(bf16[2,128,256]{2,1,0:T(8,128)(2,1)S(1)} %get-tuple-element.59), channel_id=1, source_target_pairs={{0,8},{4,12},{8,0},{12,4},{1,9},{5,13},{9,1},{13,5},{2,10},{6,14},... | collective-permute-start | bytes 393224 | tf_op jit(solution)/shard_map/ppermute | solution.py:707
  52.5 16.8 %collective-permute-start.12 = (bf16[2,128,256]{2,1,0:T(8,128)(2,1)S(1)}, bf16[2,128,256]{2,1,0:T(8,128)(2,1)S(1)}, u32[]{:S(2)}, u32[]{:S(2)}) collective-permute-start(bf16[2,128,256]{2,1,0:T(8,128)(2,1)S(1)} %get-tuple-element.60), channel_id=1, source_target_pairs={{0,12},{4,8},{8,4},{12,0},{1,13},{5,9},{9,5},{13,1},{2,14},{6,10},... | collective-permute-start | bytes 393224 | tf_op jit(solution)/shard_map/ppermute | solution.py:707
  55.4 13.9 %collective-permute-start.13 = (bf16[2,128,256]{2,1,0:T(8,128)(2,1)S(1)}, bf16[2,128,256]{2,1,0:T(8,128)(2,1)S(1)}, u32[]{:S(2)}, u32[]{:S(2)}) collective-permute-start(bf16[2,128,256]{2,1,0:T(8,128)(2,1)S(1)} %get-tuple-element.61), channel_id=1, source_target_pairs={{0,4},{4,0},{8,12},{12,8},{1,5},{5,1},{9,13},{13,9},{2,6},{6,2},{1... | collective-permute-start | bytes 393224 | tf_op jit(solution)/shard_map/ppermute | solution.py:707
  55.9 9.7 %collective-permute-start.18 = (bf16[1,128,256]{2,1,0:T(8,128)(2,1)S(1)}, bf16[1,128,256]{2,1,0:T(8,128)(2,1)S(1)}, u32[]{:S(2)}, u32[]{:S(2)}) collective-permute-start(bf16[1,128,256]{2,1,0:T(8,128)(2,1)S(1)} %slice.4), channel_id=1, source_target_pairs={{0,4},{4,0},{8,12},{12,8},{1,5},{5,1},{9,13},{13,9},{2,6},{6,2},{1... | collective-permute-start | bytes 196616 | tf_op jit(solution)/shard_map/ppermute | solution.py:707
  (5 other events, 24.7 us)

commit v8 on v6

--- a/solution.py
+++ b/solution.py
@@ -664,7 +664,7 @@
     inputs = (x_tiles, lane_rows(b_down), *(term for half in mlp_terms for term in half))
     for head in range(head_count):
         made = kv_projection(
-            where,
+            after(where, last_taps),
             kv_w_out,
             (first_taps, last_taps),
             taps_at[head * dest_count : (head + 1) * dest_count],

time: 77.5 us -> 72.2 us (0.932)
  the two profiles are of different devices: /device:TPU:17 before, /device:TPU:0 now
where the time goes in v8:
time: 72.2 us; the launch traced here: 72 us
  Pallas kernels  32.8 us (45%)
  waiting for transfers between devices  18.4 us (25%)
  starting transfers between devices  17.8 us (25%)
  local copies, waits for them, and re-layouts  2.24 us (3%)
    pallas_call x2, Pallas kernels, tap_projection(): pl.pallas_call(functools.partial(tap_kernel, blocks, head_count, dup, len...  10.1 us
    ppermute x12, waiting for transfers between devices, scatter_sum(): got[k ^ 1 << b] = lax.ppermute(sent, 'tp', pairs)  9.62 us
    ppermute x6, starting transfers between devices, move(): return lax.ppermute(value, 'grp', xor_pairs(group_count, mask))  9.23 us
    pallas_call x2, Pallas kernels, attend_head(): pl.pallas_call(functools.partial(attend_kernel, group_count, sources, hea...  9.08 us
    ppermute x6, waiting for transfers between devices, move(): return lax.ppermute(value, 'grp', xor_pairs(group_count, mask))  7.35 us
    pallas_call x2, Pallas kernels, encoder_mlp(): pl.pallas_call(functools.partial(mlp_kernel, count, base, tiles), out_sha...  6.86 us
    ppermute x12, starting transfers between devices, scatter_sum(): got[k ^ 1 << b] = lax.ppermute(sent, 'tp', pairs)  5.13 us
    ppermute x1, starting transfers between devices, gather_pieces(): pieces[k | 1 << b] = lax.ppermute(pieces[k], 'tp', pairs)  2.97 us
  transfers between devices with their start and end apart: 21, of which 10 were waited for; matrix products, arithmetic and copies ran while one was open for 2% of the time, Pallas kernels for 33%

profile of v8, /device:TPU:0, one launch (start us, length us, event | category | flops | bytes accessed | tf_op | source)
XLA Modules:
  0.0 72.0 jit_solution(17090097753924399763)
XLA Ops:
  0.0 3.0 %collective-permute-start.1 = (bf16[4,320,128]{2,1,0:T(8,128)(2,1)}, bf16[4,320,128]{2,1,0:T(8,128)(2,1)S(1)}, u32[]{:S(2)}, u32[]{:S(2)}) collective-permute-start(bf16[4,320,128]{2,1,0:T(8,128)(2,1)} %bitcast.19), channel_id=1, source_target_pairs={{0,2},{1,3},{2,0},{3,1},{4,6},{5,7},{6,4},{7,5},{8,10},{9,11},{10,... | collective-permute-start | bytes 983048 | tf_op jit(solution)/shard_map/ppermute | solution.py:601
  3.7 1.4 %copy-done.3 = bf16[4,1,128,1600]{2,3,1,0:T(8,128)(2,1)S(1)} copy-done((bf16[4,1,128,1600]{2,3,1,0:T(8,128)(2,1)S(1)}, bf16[4,1,128,1600]{2,3,1,0:T(8,128)(2,1)}, u32[]{:S(2)}) %copy-start.3) | copy-done | bytes 1638424
  5.2 5.6 %tap_projection.2 = (bf16[4,512,256]{2,1,0:T(8,128)(2,1)S(1)}, bf16[1280,1280]{1,0:T(8,128)(2,1)S(1)}, bf16[1280,1280]{1,0:T(8,128)(2,1)S(1)}, bf16[4,1600,128]{2,1,0:T(8,128)(2,1)S(1)}) custom-call(s32[26]{0:T(128)S(1)} %concatenate.3.where_ref, bf16[4,1600,128]{2,1,0:T(8,128)(2,1)S(1)} %bitcast.24, bf16[1600,2048]{1,0:T(8,128)(2,1)} %weight_hbm.3, ...), custom_call_target="tpu_custom_call" | custom-call | flops 1024 | bytes 1024 | tf_op jit(solution)/shard_map/tap_projection/pallas_call | solution.py:335
  11.3 1.3 %collective-permute-done.2.refs_3_ = bf16[4,320,128]{2,1,0:T(8,128)(2,1)S(1)} collective-permute-done((bf16[4,320,128]{2,1,0:T(8,128)(2,1)S(1)}, bf16[4,320,128]{2,1,0:T(8,128)(2,1)S(1)}, u32[]{:S(2)}, u32[]{:S(2)}) %collective-permute-start.2) | collective-permute-done | bytes 327712 | tf_op jit(solution)/shard_map/ppermute | solution.py:605
  12.6 3.4 %encoder_mlp.2 = (bf16[320,256]{1,0:T(8,128)(2,1)S(1)}, bf16[320,256]{1,0:T(8,128)(2,1)S(1)}, bf16[320,256]{1,0:T(8,128)(2,1)S(1)}, bf16[320,256]{1,0:T(8,128)(2,1)S(1)}) custom-call(s32[26]{0:T(128)S(1)} %concatenate.3.where_ref, bf16[4,320,128]{2,1,0:T(8,128)(2,1)S(1)} %bitcast.21, bf16[4,320,128]{2,1,0:T(8,128)(2,1)S(1)} %collective-permute-done.refs_1_, ...), custom_call_target="tpu_custom_call" | custom-call | flops 1024 | bytes 1024 | tf_op jit(solution)/shard_map/encoder_mlp/pallas_call | solution.py:221
  16.6 0.9 %collective-permute-done.3 = bf16[320,256]{1,0:T(8,128)(2,1)S(1)} collective-permute-done((bf16[320,256]{1,0:T(8,128)(2,1)S(1)}, bf16[320,256]{1,0:T(8,128)(2,1)S(1)}, u32[]{:S(2)}, u32[]{:S(2)}) %collective-permute-start.3) | collective-permute-done | bytes 163872 | tf_op jit(solution)/shard_map/ppermute | solution.py:588
  17.5 1.8 %collective-permute-start.6 = (bf16[320,256]{1,0:T(8,128)(2,1)S(1)}, bf16[320,256]{1,0:T(8,128)(2,1)S(1)}, u32[]{:S(2)}, u32[]{:S(2)}) collective-permute-start(bf16[320,256]{1,0:T(8,128)(2,1)S(1)} %add_convert_fusion.7), channel_id=1, source_target_pairs={{0,2},{1,3},{2,0},{3,1},{4,6},{5,7},{6,4},{7,5},{8,10},{9,11},{10,... | collective-permute-start | bytes 491528 | tf_op jit(solution)/shard_map/ppermute | solution.py:588
  19.3 3.4 %encoder_mlp.3 = (bf16[320,256]{1,0:T(8,128)(2,1)S(1)}, bf16[320,256]{1,0:T(8,128)(2,1)S(1)}, bf16[320,256]{1,0:T(8,128)(2,1)S(1)}, bf16[320,256]{1,0:T(8,128)(2,1)S(1)}) custom-call(s32[26]{0:T(128)S(1)} %concatenate.3.where_ref, bf16[4,320,128]{2,1,0:T(8,128)(2,1)S(1)} %bitcast.22, bf16[4,320,128]{2,1,0:T(8,128)(2,1)S(1)} %collective-permute-done.refs_1_, ...), custom_call_target="tpu_custom_call" | custom-call | flops 1024 | bytes 1024 | tf_op jit(solution)/shard_map/encoder_mlp/pallas_call | solution.py:221
  23.3 1.1 %collective-permute-done.4 = bf16[320,256]{1,0:T(8,128)(2,1)S(1)} collective-permute-done((bf16[320,256]{1,0:T(8,128)(2,1)S(1)}, bf16[320,256]{1,0:T(8,128)(2,1)S(1)}, u32[]{:S(2)}, u32[]{:S(2)}) %collective-permute-start.4) | collective-permute-done | bytes 163872 | tf_op jit(solution)/shard_map/ppermute | solution.py:588
  24.8 4.5 %tap_projection.3.refs_2_ = bf16[4,512,256]{2,1,0:T(8,128)(2,1)S(1)} custom-call(s32[26]{0:T(128)S(1)} %concatenate.3.where_ref, bf16[4,1600,128]{2,1,0:T(8,128)(2,1)S(1)} %get-tuple-element.52.tap_hbm, bf16[1600,2048]{1,0:T(8,128)(2,1)} %weight_hbm.3), custom_call_target="tpu_custom_call" | custom-call | flops 1024 | bytes 1024 | tf_op jit(solution)/shard_map/tap_projection/pallas_call | solution.py:335
  29.4 1.4 %collective-permute-done.8.refs_7_ = bf16[320,256]{1,0:T(8,128)(2,1)S(1)} collective-permute-done((bf16[320,256]{1,0:T(8,128)(2,1)S(1)}, bf16[320,256]{1,0:T(8,128)(2,1)S(1)}, u32[]{:S(2)}, u32[]{:S(2)}) %collective-permute-start.8) | collective-permute-done | bytes 163872 | tf_op jit(solution)/shard_map/ppermute | solution.py:588
  30.9 1.3 %kv_projection.2 = (bf16[512,256]{1,0:T(8,128)(2,1)S(1)}, bf16[512,256]{1,0:T(8,128)(2,1)S(1)}, bf16[512,256]{1,0:T(8,128)(2,1)S(1)}, bf16[512,256]{1,0:T(8,128)(2,1)S(1)}, bf16[512,320]{1,0:T(8,128)(2,1)S(1)}) custom-call(s32[26]{0:T(128)S(1)} %concatenate.3.where_ref, bf16[320,2048]{1,0:T(8,128)(2,1)S(1)} %copy-done, ...), custom_call_target="tpu_custom_call" | custom-call | flops 1024 | bytes 1024 | tf_op jit(solution)/shard_map/kv_projection/pallas_call | solution.py:407
  32.3 1.3 %kv_projection.3 = (bf16[512,256]{1,0:T(8,128)(2,1)S(1)}, bf16[512,256]{1,0:T(8,128)(2,1)S(1)}, bf16[512,256]{1,0:T(8,128)(2,1)S(1)}, bf16[512,256]{1,0:T(8,128)(2,1)S(1)}) custom-call(s32[26]{0:T(128)S(1)} %concatenate.3.where_ref, bf16[320,2048]{1,0:T(8,128)(2,1)S(1)} %copy-done, bf16[4,512,256]{2,1,0:T(8,128)(2,1)S(1)} %get-tuple-element.42.refs_1_, ...), custom_call_target="tpu_custom_call" | custom-call | flops 1024 | bytes 1024 | tf_op jit(solution)/shard_map/kv_projection/pallas_call | solution.py:407
  35.3 2.6 %prepare.1 = (bf16[512,2048]{1,0:T(8,128)(2,1)S(1)}, s32[24]{0:T(128)S(1)}) custom-call(s32[26]{0:T(128)S(1)} %concatenate.3.where_ref, f32[1,128]{1,0:T(1,128)S(1)} %bitcast.33, bf16[512,2048]{1,0:T(8,128)(2,1)S(1)} %copy-done.2), custom_call_target="tpu_custom_call" | custom-call | flops 1024 | bytes 1024 | tf_op jit(solution)/shard_map/prepare/pallas_call | solution.py:269
  38.0 4.5 %collective-permute-done.12.refs_1_ = bf16[512,256]{1,0:T(8,128)(2,1)S(1)} collective-permute-done((bf16[512,256]{1,0:T(8,128)(2,1)S(1)}, bf16[512,256]{1,0:T(8,128)(2,1)S(1)}, u32[]{:S(2)}, u32[]{:S(2)}) %collective-permute-start.12) | collective-permute-done | bytes 262176 | tf_op jit(solution)/shard_map/ppermute | solution.py:588
  43.7 2.8 %collective-permute-start.18 = (bf16[2,128,256]{2,1,0:T(8,128)(2,1)S(1)}, bf16[2,128,256]{2,1,0:T(8,128)(2,1)S(1)}, u32[]{:S(2)}, u32[]{:S(2)}) collective-permute-start(bf16[2,128,256]{2,1,0:T(8,128)(2,1)S(1)} %get-tuple-element.76), channel_id=1, source_target_pairs={{0,8},{4,12},{8,0},{12,4},{1,9},{5,13},{9,1},{13,5},{2,10},{6,14},... | collective-permute-start | bytes 393224 | tf_op jit(solution)/shard_map/ppermute | solution.py:702
  46.6 1.4 %collective-permute-start.19 = (bf16[2,128,256]{2,1,0:T(8,128)(2,1)S(1)}, bf16[2,128,256]{2,1,0:T(8,128)(2,1)S(1)}, u32[]{:S(2)}, u32[]{:S(2)}) collective-permute-start(bf16[2,128,256]{2,1,0:T(8,128)(2,1)S(1)} %get-tuple-element.77), channel_id=1, source_target_pairs={{0,12},{4,8},{8,4},{12,0},{1,13},{5,9},{9,5},{13,1},{2,14},{6,10},... | collective-permute-start | bytes 393224 | tf_op jit(solution)/shard_map/ppermute | solution.py:702
  48.3 1.6 %collective-permute-done.13.refs_1_ = bf16[512,256]{1,0:T(8,128)(2,1)S(1)} collective-permute-done((bf16[512,256]{1,0:T(8,128)(2,1)S(1)}, bf16[512,256]{1,0:T(8,128)(2,1)S(1)}, u32[]{:S(2)}, u32[]{:S(2)}) %collective-permute-start.13) | collective-permute-done | bytes 262176 | tf_op jit(solution)/shard_map/ppermute | solution.py:588
  50.7 2.7 %collective-permute-start.14 = (bf16[2,128,256]{2,1,0:T(8,128)(2,1)S(1)}, bf16[2,128,256]{2,1,0:T(8,128)(2,1)S(1)}, u32[]{:S(2)}, u32[]{:S(2)}) collective-permute-start(bf16[2,128,256]{2,1,0:T(8,128)(2,1)S(1)} %get-tuple-element.70), channel_id=1, source_target_pairs={{0,8},{4,12},{8,0},{12,4},{1,9},{5,13},{9,1},{13,5},{2,10},{6,14},... | collective-permute-start | bytes 393224 | tf_op jit(solution)/shard_map/ppermute | solution.py:702
  53.3 1.4 %collective-permute-start.15 = (bf16[2,128,256]{2,1,0:T(8,128)(2,1)S(1)}, bf16[2,128,256]{2,1,0:T(8,128)(2,1)S(1)}, u32[]{:S(2)}, u32[]{:S(2)}) collective-permute-start(bf16[2,128,256]{2,1,0:T(8,128)(2,1)S(1)} %get-tuple-element.71), channel_id=1, source_target_pairs={{0,12},{4,8},{8,4},{12,0},{1,13},{5,9},{9,5},{13,1},{2,14},{6,10},... | collective-permute-start | bytes 393224 | tf_op jit(solution)/shard_map/ppermute | solution.py:702
  54.7 1.9 %collective-permute-done.18.refs_1_ = bf16[2,128,256]{2,1,0:T(8,128)(2,1)S(1)} collective-permute-done((bf16[2,128,256]{2,1,0:T(8,128)(2,1)S(1)}, bf16[2,128,256]{2,1,0:T(8,128)(2,1)S(1)}, u32[]{:S(2)}, u32[]{:S(2)}) %collective-permute-start.18) | collective-permute-done | bytes 131104 | tf_op jit(solution)/shard_map/ppermute | solution.py:702
  57.3 4.4 %attend_head.2.refs_4_ = bf16[512,2048]{1,0:T(8,128)(2,1)} custom-call(s32[24]{0:T(128)S(1)} %get-tuple-element.61.meta_ref, bf16[512,2048]{1,0:T(8,128)(2,1)S(1)} %get-tuple-element.62.query_ref, bf16[2,128,256]{2,1,0:T(8,128)(2,1)S(1)} %get-tuple-element.75.refs_0_, bf16[2,128,256]{2,1,0:T(8,128)(2,1)S(1)} %collective-permute-done.18.refs_1_, ...), custom_call_target="tpu_custom_call" | custom-call | flops 1024 | bytes 1024 | tf_op jit(solution)/shard_map/attend_head/pallas_call | solution.py:551
  61.8 5.4 %collective-permute-done.14.refs_1_ = bf16[2,128,256]{2,1,0:T(8,128)(2,1)S(1)} collective-permute-done((bf16[2,128,256]{2,1,0:T(8,128)(2,1)S(1)}, bf16[2,128,256]{2,1,0:T(8,128)(2,1)S(1)}, u32[]{:S(2)}, u32[]{:S(2)}) %collective-permute-start.14) | collective-permute-done | bytes 131104 | tf_op jit(solution)/shard_map/ppermute | solution.py:702
  67.2 4.7 %attend_head.3 = bf16[512,2048]{1,0:T(8,128)(2,1)} custom-call(s32[24]{0:T(128)S(1)} %get-tuple-element.61.meta_ref, bf16[512,2048]{1,0:T(8,128)(2,1)S(1)} %get-tuple-element.62.query_ref, bf16[2,128,256]{2,1,0:T(8,128)(2,1)S(1)} %get-tuple-element.69.refs_0_, ...), custom_call_target="tpu_custom_call", output_to_operand_aliasing={{}: (6, {})} | custom-call | flops 1024 | bytes 1024 | tf_op jit(solution)/shard_map/attend_head/pallas_call | solution.py:551
  (59 shorter events, 8.0 us)
Async XLA Ops:
  0.0 10.9 %collective-permute-start.1 = (bf16[4,320,128]{2,1,0:T(8,128)(2,1)}, bf16[4,320,128]{2,1,0:T(8,128)(2,1)S(1)}, u32[]{:S(2)}, u32[]{:S(2)}) collective-permute-start(bf16[4,320,128]{2,1,0:T(8,128)(2,1)} %bitcast.19), channel_id=1, source_target_pairs={{0,2},{1,3},{2,0},{3,1},{4,6},{5,7},{6,4},{7,5},{8,10},{9,11},{10,... | collective-permute-start | bytes 983048 | tf_op jit(solution)/shard_map/ppermute | solution.py:601
  3.0 8.3 %collective-permute-start = (bf16[4,320,128]{2,1,0:T(8,128)(2,1)}, bf16[4,320,128]{2,1,0:T(8,128)(2,1)S(1)}, u32[]{:S(2)}, u32[]{:S(2)}) collective-permute-start(bf16[4,320,128]{2,1,0:T(8,128)(2,1)} %bitcast.20), channel_id=1, source_target_pairs={{0,1},{1,0},{2,3},{3,2},{4,5},{5,4},{6,7},{7,6},{8,9},{9,8},{10,11... | collective-permute-start | bytes 983048 | tf_op jit(solution)/shard_map/ppermute | solution.py:642
  5.2 7.4 %copy-start.5 = (f32[1280]{0:T(1024)S(1)}, f32[1280]{0:T(1024)}, u32[]{:S(2)}) copy-start(f32[1280]{0:T(1024)} %param.19) | copy-start | bytes 15364
  5.2 7.4 %copy-start.6 = (f32[1280]{0:T(1024)S(1)}, f32[1280]{0:T(1024)}, u32[]{:S(2)}) copy-start(f32[1280]{0:T(1024)} %param.21) | copy-start | bytes 15364
  10.9 1.7 %collective-permute-start.2 = (bf16[4,320,128]{2,1,0:T(8,128)(2,1)S(1)}, bf16[4,320,128]{2,1,0:T(8,128)(2,1)S(1)}, u32[]{:S(2)}, u32[]{:S(2)}) collective-permute-start(bf16[4,320,128]{2,1,0:T(8,128)(2,1)S(1)} %collective-permute-done.1.refs_2_), channel_id=1, source_target_pairs={{0,1},{1,0},{2,3},{3,2},{4,5},{5,4},{6,7},{7,6},{8,9},{9,8},{10,11... | collective-permute-start | bytes 983048 | tf_op jit(solution)/shard_map/ppermute | solution.py:605
  16.0 1.4 %collective-permute-start.3 = (bf16[320,256]{1,0:T(8,128)(2,1)S(1)}, bf16[320,256]{1,0:T(8,128)(2,1)S(1)}, u32[]{:S(2)}, u32[]{:S(2)}) collective-permute-start(bf16[320,256]{1,0:T(8,128)(2,1)S(1)} %get-tuple-element.47), channel_id=1, source_target_pairs={{0,1},{1,0},{2,3},{3,2},{4,5},{5,4},{6,7},{7,6},{8,9},{9,8},{10,11... | collective-permute-start | bytes 491528 | tf_op jit(solution)/shard_map/ppermute | solution.py:588
  16.4 6.8 %collective-permute-start.5 = (bf16[320,256]{1,0:T(8,128)(2,1)S(1)}, bf16[320,256]{1,0:T(8,128)(2,1)S(1)}, u32[]{:S(2)}, u32[]{:S(2)}) collective-permute-start(bf16[320,256]{1,0:T(8,128)(2,1)S(1)} %get-tuple-element.55), channel_id=1, source_target_pairs={{0,1},{1,0},{2,3},{3,2},{4,5},{5,4},{6,7},{7,6},{8,9},{9,8},{10,11... | collective-permute-start | bytes 491528 | tf_op jit(solution)/shard_map/ppermute | solution.py:588
  17.5 11.9 %collective-permute-start.6 = (bf16[320,256]{1,0:T(8,128)(2,1)S(1)}, bf16[320,256]{1,0:T(8,128)(2,1)S(1)}, u32[]{:S(2)}, u32[]{:S(2)}) collective-permute-start(bf16[320,256]{1,0:T(8,128)(2,1)S(1)} %add_convert_fusion.7), channel_id=1, source_target_pairs={{0,2},{1,3},{2,0},{3,1},{4,6},{5,7},{6,4},{7,5},{8,10},{9,11},{10,... | collective-permute-start | bytes 491528 | tf_op jit(solution)/shard_map/ppermute | solution.py:588
  22.7 6.7 %collective-permute-start.7 = (bf16[320,256]{1,0:T(8,128)(2,1)S(1)}, bf16[320,256]{1,0:T(8,128)(2,1)S(1)}, u32[]{:S(2)}, u32[]{:S(2)}) collective-permute-start(bf16[320,256]{1,0:T(8,128)(2,1)S(1)} %get-tuple-element.57), channel_id=1, source_target_pairs={{0,1},{1,0},{2,3},{3,2},{4,5},{5,4},{6,7},{7,6},{8,9},{9,8},{10,11... | collective-permute-start | bytes 491528 | tf_op jit(solution)/shard_map/ppermute | solution.py:588
  22.7 1.6 %collective-permute-start.4 = (bf16[320,256]{1,0:T(8,128)(2,1)S(1)}, bf16[320,256]{1,0:T(8,128)(2,1)S(1)}, u32[]{:S(2)}, u32[]{:S(2)}) collective-permute-start(bf16[320,256]{1,0:T(8,128)(2,1)S(1)} %get-tuple-element.50), channel_id=1, source_target_pairs={{0,1},{1,0},{2,3},{3,2},{4,5},{5,4},{6,7},{7,6},{8,9},{9,8},{10,11... | collective-permute-start | bytes 491528 | tf_op jit(solution)/shard_map/ppermute | solution.py:588
  24.4 6.4 %collective-permute-start.8 = (bf16[320,256]{1,0:T(8,128)(2,1)S(1)}, bf16[320,256]{1,0:T(8,128)(2,1)S(1)}, u32[]{:S(2)}, u32[]{:S(2)}) collective-permute-start(bf16[320,256]{1,0:T(8,128)(2,1)S(1)} %add_convert_fusion.6), channel_id=1, source_target_pairs={{0,2},{1,3},{2,0},{3,1},{4,6},{5,7},{6,4},{7,5},{8,10},{9,11},{10,... | collective-permute-start | bytes 491528 | tf_op jit(solution)/shard_map/ppermute | solution.py:588
  32.2 1.9 %collective-permute-start.9 = (bf16[512,256]{1,0:T(8,128)(2,1)S(1)}, bf16[512,256]{1,0:T(8,128)(2,1)S(1)}, u32[]{:S(2)}, u32[]{:S(2)}) collective-permute-start(bf16[512,256]{1,0:T(8,128)(2,1)S(1)} %get-tuple-element.59), channel_id=1, source_target_pairs={{0,1},{1,0},{2,3},{3,2},{4,5},{5,4},{6,7},{7,6},{8,9},{9,8},{10,11... | collective-permute-start | bytes 786440 | tf_op jit(solution)/shard_map/ppermute | solution.py:588
  33.6 1.7 %collective-permute-start.11 = (bf16[512,256]{1,0:T(8,128)(2,1)S(1)}, bf16[512,256]{1,0:T(8,128)(2,1)S(1)}, u32[]{:S(2)}, u32[]{:S(2)}) collective-permute-start(bf16[512,256]{1,0:T(8,128)(2,1)S(1)} %get-tuple-element.67), channel_id=1, source_target_pairs={{0,1},{1,0},{2,3},{3,2},{4,5},{5,4},{6,7},{7,6},{8,9},{9,8},{10,11... | collective-permute-start | bytes 786440 | tf_op jit(solution)/shard_map/ppermute | solution.py:588
  34.1 8.8 %copy-start.7 = (f32[128]{0:T(128)S(1)}, f32[128]{0:T(128)}, u32[]{:S(2)}) copy-start(f32[128]{0:T(128)} %param.26) | copy-start | bytes 1540
  34.2 8.3 %collective-permute-start.12 = (bf16[512,256]{1,0:T(8,128)(2,1)S(1)}, bf16[512,256]{1,0:T(8,128)(2,1)S(1)}, u32[]{:S(2)}, u32[]{:S(2)}) collective-permute-start(bf16[512,256]{1,0:T(8,128)(2,1)S(1)} %add_convert_fusion.3), channel_id=1, source_target_pairs={{0,2},{1,3},{2,0},{3,1},{4,6},{5,7},{6,4},{7,5},{8,10},{9,11},{10,... | collective-permute-start | bytes 786440 | tf_op jit(solution)/shard_map/ppermute | solution.py:588
  34.6 8.3 %collective-permute-start.17 = (bf16[512,256]{1,0:T(8,128)(2,1)S(1)}, bf16[512,256]{1,0:T(8,128)(2,1)S(1)}, u32[]{:S(2)}, u32[]{:S(2)}) collective-permute-start(bf16[512,256]{1,0:T(8,128)(2,1)S(1)} %get-tuple-element.74), channel_id=1, source_target_pairs={{0,1},{1,0},{2,3},{3,2},{4,5},{5,4},{6,7},{7,6},{8,9},{9,8},{10,11... | collective-permute-start | bytes 786440 | tf_op jit(solution)/shard_map/ppermute | solution.py:588
  34.6 11.9 %collective-permute-start.10 = (bf16[512,256]{1,0:T(8,128)(2,1)S(1)}, bf16[512,256]{1,0:T(8,128)(2,1)S(1)}, u32[]{:S(2)}, u32[]{:S(2)}) collective-permute-start(bf16[512,256]{1,0:T(8,128)(2,1)S(1)} %get-tuple-element.65), channel_id=1, source_target_pairs={{0,1},{1,0},{2,3},{3,2},{4,5},{5,4},{6,7},{7,6},{8,9},{9,8},{10,11... | collective-permute-start | bytes 786440 | tf_op jit(solution)/shard_map/ppermute | solution.py:588
  42.5 7.4 %collective-permute-start.13 = (bf16[512,256]{1,0:T(8,128)(2,1)S(1)}, bf16[512,256]{1,0:T(8,128)(2,1)S(1)}, u32[]{:S(2)}, u32[]{:S(2)}) collective-permute-start(bf16[512,256]{1,0:T(8,128)(2,1)S(1)} %add_convert_fusion.1), channel_id=1, source_target_pairs={{0,2},{1,3},{2,0},{3,1},{4,6},{5,7},{6,4},{7,5},{8,10},{9,11},{10,... | collective-permute-start | bytes 786440 | tf_op jit(solution)/shard_map/ppermute | solution.py:588
  43.7 12.9 %collective-permute-start.18 = (bf16[2,128,256]{2,1,0:T(8,128)(2,1)S(1)}, bf16[2,128,256]{2,1,0:T(8,128)(2,1)S(1)}, u32[]{:S(2)}, u32[]{:S(2)}) collective-permute-start(bf16[2,128,256]{2,1,0:T(8,128)(2,1)S(1)} %get-tuple-element.76), channel_id=1, source_target_pairs={{0,8},{4,12},{8,0},{12,4},{1,9},{5,13},{9,1},{13,5},{2,10},{6,14},... | collective-permute-start | bytes 393224 | tf_op jit(solution)/shard_map/ppermute | solution.py:702
  46.6 10.7 %collective-permute-start.19 = (bf16[2,128,256]{2,1,0:T(8,128)(2,1)S(1)}, bf16[2,128,256]{2,1,0:T(8,128)(2,1)S(1)}, u32[]{:S(2)}, u32[]{:S(2)}) collective-permute-start(bf16[2,128,256]{2,1,0:T(8,128)(2,1)S(1)} %get-tuple-element.77), channel_id=1, source_target_pairs={{0,12},{4,8},{8,4},{12,0},{1,13},{5,9},{9,5},{13,1},{2,14},{6,10},... | collective-permute-start | bytes 393224 | tf_op jit(solution)/shard_map/ppermute | solution.py:702
  48.0 9.3 %collective-permute-start.20 = (bf16[2,128,256]{2,1,0:T(8,128)(2,1)S(1)}, bf16[2,128,256]{2,1,0:T(8,128)(2,1)S(1)}, u32[]{:S(2)}, u32[]{:S(2)}) collective-permute-start(bf16[2,128,256]{2,1,0:T(8,128)(2,1)S(1)} %get-tuple-element.78), channel_id=1, source_target_pairs={{0,4},{4,0},{8,12},{12,8},{1,5},{5,1},{9,13},{13,9},{2,6},{6,2},{1... | collective-permute-start | bytes 393224 | tf_op jit(solution)/shard_map/ppermute | solution.py:702
  50.7 16.5 %collective-permute-start.14 = (bf16[2,128,256]{2,1,0:T(8,128)(2,1)S(1)}, bf16[2,128,256]{2,1,0:T(8,128)(2,1)S(1)}, u32[]{:S(2)}, u32[]{:S(2)}) collective-permute-start(bf16[2,128,256]{2,1,0:T(8,128)(2,1)S(1)} %get-tuple-element.70), channel_id=1, source_target_pairs={{0,8},{4,12},{8,0},{12,4},{1,9},{5,13},{9,1},{13,5},{2,10},{6,14},... | collective-permute-start | bytes 393224 | tf_op jit(solution)/shard_map/ppermute | solution.py:702
  53.3 13.8 %collective-permute-start.15 = (bf16[2,128,256]{2,1,0:T(8,128)(2,1)S(1)}, bf16[2,128,256]{2,1,0:T(8,128)(2,1)S(1)}, u32[]{:S(2)}, u32[]{:S(2)}) collective-permute-start(bf16[2,128,256]{2,1,0:T(8,128)(2,1)S(1)} %get-tuple-element.71), channel_id=1, source_target_pairs={{0,12},{4,8},{8,4},{12,0},{1,13},{5,9},{9,5},{13,1},{2,14},{6,10},... | collective-permute-start | bytes 393224 | tf_op jit(solution)/shard_map/ppermute | solution.py:702
  56.6 10.6 %collective-permute-start.16 = (bf16[2,128,256]{2,1,0:T(8,128)(2,1)S(1)}, bf16[2,128,256]{2,1,0:T(8,128)(2,1)S(1)}, u32[]{:S(2)}, u32[]{:S(2)}) collective-permute-start(bf16[2,128,256]{2,1,0:T(8,128)(2,1)S(1)} %get-tuple-element.72), channel_id=1, source_target_pairs={{0,4},{4,0},{8,12},{12,8},{1,5},{5,1},{9,13},{13,9},{2,6},{6,2},{1... | collective-permute-start | bytes 393224 | tf_op jit(solution)/shard_map/ppermute | solution.py:702
  (7 other events, 32.3 us)
